TPU v7x, 1024 devices: a whole 8x8x8 slice. The times are simulated.
1024 devices in a mesh: shard: 64 (over z, y), blk: 16 (over x, core).
Axes of the slice: x: 8, y: 8, z: 8, core: 2. Of those that a mesh axis runs over, the one named last changes fastest.
Arguments:
- item_feats: bfloat16 [131072, 2048], P(('shard', 'blk')), may hold values from -6 to 6
- owner: int32 [131072, 1], P(('shard', 'blk')), may hold values from 0 to 63; in each aligned block of 128 rows (0 to 127, 128 to 255, ...) at most 4 rows name the same one
- id_row: int32 [131072], P(('shard', 'blk')), may hold values from 0 to 1023
- counts: int32 [131072], P(('shard', 'blk')), may hold values from 3072 to 4096
- occurrence: int32 [262144], P(('shard', 'blk')), may hold values from 0 to 127
- users: bfloat16 [262144, 256], P(('shard', 'blk')), may hold values from -6 to 6
- w_first: bfloat16 [2048, 1024], replicated, may hold values from -0.125 to 0.125
- w_second: bfloat16 [1024, 256], replicated, may hold values from -0.1875 to 0.1875
- id_table: bfloat16 [65536, 1024], P('shard'), may hold values from -6 to 6
Outputs:
- loss: float32 [262144], P(('shard', 'blk'))
- user_grad: float32 [262144, 256], P(('shard', 'blk'))
- item_grad: float32 [131072, 256], P(('shard', 'blk'))
Inputs may be any that keep to these rules, and one draw needn't show every extreme that they name: Among the unique items of one device no owner index appears more than 4 times, and some owner appears exactly 4 times.
All inputs are finite; a program needn't handle non-finite values.
Results may differ from a plain program's by a relative error of at most 0.012.
The roundings to bfloat16 on the way count: a program that leaves them out, or rounds other values in their place, can miss the bound.
Values may be sent and summed in bfloat16 or wider, within the bound.
No kernel may reach another device: no remote copies, remote signals or barrier semaphores. Data moves between devices by JAX's collectives and lax.ppermute only.
A program may use at most 32 MiB of HBM per device.

v0:
```python
import jax
import jax.numpy as jnp
from jax import lax
from jax.sharding import PartitionSpec as P

logit_scale = 48.0


def encode_items(features, table_rows, w_first, w_second):
    pre = jnp.dot(features, w_first, preferred_element_type=jnp.float32) + table_rows.astype(
        jnp.float32
    )
    hidden = jnp.maximum(pre, 0.0).astype(jnp.bfloat16)
    emb = jnp.dot(hidden, w_second, preferred_element_type=jnp.float32)
    emb_square = jnp.sum(emb * emb, -1, keepdims=True)
    return (emb * lax.rsqrt(emb_square + 1e-06)).astype(jnp.bfloat16)


def shards(item_feats, owner, id_row, counts, occurrence, users, w_first, w_second, id_table):
    unique_rows = item_feats.shape[0]
    owners = lax.axis_size("shard")
    capacity = 2 * unique_rows // owners
    target = owner[:, 0]
    owner_hot = (target[:, None] == jnp.arange(owners, dtype=jnp.int32)[None, :]).astype(jnp.int32)
    slot_rank = jnp.sum((jnp.cumsum(owner_hot, 0) - owner_hot) * owner_hot, 1)
    position = target * capacity + slot_rank
    packed_ids = (
        jnp.zeros((owners * capacity,), jnp.int32)
        .at[position]
        .set(id_row)
        .reshape(owners, capacity)
    )
    placing = (position[None, :] == jnp.arange(owners * capacity, dtype=jnp.int32)[:, None]).astype(
        jnp.bfloat16
    )
    packed = jnp.dot(placing, item_feats, preferred_element_type=jnp.float32).astype(jnp.bfloat16)
    packed = packed.reshape(owners, capacity, item_feats.shape[1])
    feats = lax.all_to_all(packed, "shard", split_axis=0, concat_axis=0, tiled=True)
    ids = lax.all_to_all(packed_ids, "shard", split_axis=0, concat_axis=0, tiled=True)
    slots = feats.shape[1]
    table_rows = id_table[ids.reshape(-1)]
    encoded = encode_items(feats.reshape(-1, feats.shape[2]), table_rows, w_first, w_second)
    encoded = encoded.reshape(feats.shape[0], slots, encoded.shape[1])
    returned = lax.all_to_all(encoded, "shard", split_axis=0, concat_axis=0, tiled=True)
    vecs = returned.reshape(owners * capacity, returned.shape[2])[position]
    bias = jnp.log(counts.astype(jnp.float32)).astype(jnp.bfloat16)
    cand_vecs, cand_bias = (
        lax.all_gather(vecs, "blk", axis=0, tiled=True),
        lax.all_gather(bias, "blk", axis=0, tiled=True),
    )
    user_f = users.astype(jnp.float32)
    user_square = jnp.sum(user_f * user_f, -1, keepdims=True)
    inverse = lax.rsqrt(user_square + 1e-06)
    unit = user_f * inverse
    unit_b = unit.astype(jnp.bfloat16)
    logits = (
        logit_scale
        * lax.dot_general(
            unit_b, cand_vecs, (((1,), (1,)), ((), ())), preferred_element_type=jnp.float32
        )
        - cand_bias.astype(jnp.float32)[None, :]
    )
    exponent = jnp.exp(logits)
    denominator = jnp.sum(exponent, 1)
    positive = lax.axis_index("blk") * unique_rows + occurrence
    onehot = (jnp.arange(logits.shape[1], dtype=jnp.int32)[None, :] == positive[:, None]).astype(
        jnp.float32
    )
    picked = jnp.sum(logits * onehot, 1)
    loss = jnp.log(denominator) - picked
    residue = (exponent / denominator[:, None] - onehot).astype(jnp.bfloat16)
    direction = logit_scale * jnp.dot(residue, cand_vecs, preferred_element_type=jnp.float32)
    user_grad = inverse * (direction - jnp.sum(direction * unit, -1, keepdims=True) * unit)
    item_grad = lax.psum_scatter(
        (
            logit_scale
            * lax.dot_general(
                residue, unit_b, (((0,), (0,)), ((), ())), preferred_element_type=jnp.float32
            )
        ).astype(jnp.bfloat16),
        "blk",
        scatter_dimension=0,
        tiled=True,
    ).astype(jnp.float32)
    return (loss, user_grad, item_grad)


def solution(mesh):
    return jax.shard_map(
        shards,
        mesh=mesh,
        in_specs=(
            P(("shard", "blk"), None),
            P(("shard", "blk"), None),
            P(("shard", "blk")),
            P(("shard", "blk")),
            P(("shard", "blk")),
            P(("shard", "blk"), None),
            P(),
            P(),
            P("shard", None),
        ),
        out_specs=(P(("shard", "blk")), P(("shard", "blk"), None), P(("shard", "blk"), None)),
        check_vma=False,
    )
```

profile of v0, /device:TPU:1, one launch (start us, length us, event | category | flops | bytes accessed | tf_op | source)
XLA Modules:
  0.0 217.5 jit_solution(5388270226320737424)
XLA Ops:
  7.2 0.0 copy-start
  7.2 0.9 fusion.17
  8.1 0.2 reduce_window_sum.11
  8.2 0.8 select_reduce_fusion.1
  9.1 0.7 fusion.18
  9.7 1.1 scatter_custom_fusion
  10.9 0.7 all_to_all.13
  11.6 24.0 %all-to-all-start.1 = ((s32[64,1,4]{2,1,0:T(1,128)}), s32[64,1,4]{2,1,0:T(1,128)S(1)}, u32[]{:S(2)}, u32[]{:S(2)}) async-start(s32[64,1,4]{2,1,0:T(1,128)} %bitcast.3), calls=%async_computation.1 | async-start | bytes 65536 | tf_op jit(solution)/shard_map/all_to_all | solution.py:39
  35.5 0.7 multiply_add_fusion
  36.2 1.5 convolution_convert_fusion
  37.7 1.2 reshape.79
  38.9 7.4 %all-to-all-done.1 = s32[64,1,4]{2,1,0:T(1,128)S(1)} async-done(((s32[64,1,4]{2,1,0:T(1,128)}), s32[64,1,4]{2,1,0:T(1,128)S(1)}, u32[]{:S(2)}, u32[]{:S(2)}) %all-to-all-start.1) | async-done | bytes 1056 | tf_op jit(solution)/shard_map/all_to_all | solution.py:39
  46.3 4.7 %all-to-all-start = ((bf16[64,4,2048]{2,1,0:T(4,128)(2,1)}), bf16[64,4,2048]{2,1,0:T(4,128)(2,1)S(1)}, u32[]{:S(2)}, u32[]{:S(2)}) async-start(bf16[64,4,2048]{2,1,0:T(4,128)(2,1)} %reshape.79), calls=%async_computation | async-start | bytes 2097152 | tf_op jit(solution)/shard_map/all_to_all | solution.py:38
  51.1 0.5 broadcast.82
  51.6 0.7 reduce.3
  52.3 0.1 reshape.81
  52.4 0.0 copy-done
  52.4 2.0 gather_fusion
  54.4 22.5 %all-to-all-done = bf16[64,4,2048]{2,1,0:T(4,128)(2,1)S(1)} async-done(((bf16[64,4,2048]{2,1,0:T(4,128)(2,1)}), bf16[64,4,2048]{2,1,0:T(4,128)(2,1)S(1)}, u32[]{:S(2)}, u32[]{:S(2)}) %all-to-all-start) | async-done | bytes 1048608 | tf_op jit(solution)/shard_map/all_to_all | solution.py:38
  76.9 1.1 reshape.80
  78.0 0.0 copy-start.3
  78.0 4.4 %multiply_reduce_fusion = (f32[256]{0:T(256)S(1)}, f32[256,256]{1,0:T(8,128)S(1)}) fusion(bf16[1024,256]{1,0:T(8,128)(2,1)} %param.16, bf16[256,2048]{1,0:T(8,128)(2,1)} %reshape.80, bf16[2048,1024]{1,0:T(8,128)(2,1)} %param.15, bf16[256,1024]{1,0:T(8,128)(2,1)} %gather_fusion), kind=kOutput, calls=%fused_computation.29 | convolution fusion | flops 1209138944 | bytes 6554624 | tf_op jit(solution)/shard_map/dot_general | solution.py:14
  82.5 0.0 copy-start.2
  82.5 0.1 multiply_convert_fusion
  82.6 0.7 reshape.82
  83.3 8.6 %all-to-all-start.2 = ((bf16[64,4,256]{2,1,0:T(4,128)(2,1)}), bf16[64,4,256]{2,1,0:T(4,128)(2,1)S(1)}, u32[]{:S(2)}, u32[]{:S(2)}) async-start(bf16[64,4,256]{2,1,0:T(4,128)(2,1)} %reshape.82), calls=%async_computation.2 | async-start | bytes 262144 | tf_op jit(solution)/shard_map/all_to_all | solution.py:44
  91.9 0.0 all-gather.4.cloned.1.call-start
  92.0 11.5 %all-to-all-done.2 = bf16[64,4,256]{2,1,0:T(4,128)(2,1)S(1)} async-done(((bf16[64,4,256]{2,1,0:T(4,128)(2,1)}), bf16[64,4,256]{2,1,0:T(4,128)(2,1)S(1)}, u32[]{:S(2)}, u32[]{:S(2)}) %all-to-all-start.2) | async-done | bytes 131104 | tf_op jit(solution)/shard_map/all_to_all | solution.py:44
  103.5 1.5 gather_fusion.1
  105.0 0.0 all-gather.4.cloned.1.call-update
  105.0 0.0 reduce-scatter.2.cloned.1.call-start
  105.1 0.0 copy-done.3
  105.1 20.5 %all-gather.1 = bf16[16,1,128]{2,1,0:T(2,128)(2,1)S(1)} all-gather(bf16[1,1,128]{2,1,0:T(2,128)(2,1)S(1)} %convert_bitcast_fusion), channel_id=1, replica_groups=mesh['shard'=64,'blk'=16] {'blk'}, dimensions={0}, use_global_device_ids=true | all-gather | bytes 4352 | tf_op jit(solution)/shard_map/all_gather | solution.py:49
  125.6 0.0 copy-done.1
  125.6 0.1 copy.16
  125.7 0.1 fusion.13
  125.7 0.0 copy-done.2
  125.8 17.6 %all-gather.4.cloned.1.call-done = bf16[2048,256]{1,0:T(8,128)(2,1)} async-done(((bf16[128,256]{1,0:T(8,128)(2,1)}), bf16[2048,256]{1,0:T(8,128)(2,1)}) %all-gather.4.cloned.1.call-update) | async-done | bytes 1048592 | tf_op jit(solution)/shard_map/all_gather | solution.py:48
  143.4 2.2 %exponential_reduce_fusion = (f32[256]{0:T(256)S(1)}, f32[256]{0:T(256)S(1)}, f32[256,2048]{1,0:T(8,128)S(1)}) fusion(s32[256]{0:T(256)S(1)} %broadcast_add_fusion, f32[2048]{0:T(1024)S(1)} %bitcast.22, bf16[2048,256]{1,0:T(8,128)(2,1)} %all-gather.4.cloned.1.call-done, bf16[256,256]{0,1:T(8,128)(2,1)S(1)} %copy.16, f32[256]{0:T(256)S(1)} %add_rsqrt_fusion.1), kind=kOutput, calls=%fused_computation.11 | convolution fusion | flops 271777280 | bytes 3289088 | tf_op jit(solution)/shard_map/dot_general | solution.py:58
  145.5 0.6 subtract_convert_fusion
  146.1 1.5 fusion.1
  147.6 0.0 reduce-scatter.2.cloned.1.call-update
  147.7 1.8 fusion.10
  149.4 0.1 fusion.12
  149.5 0.8 copy.18
  150.3 0.6 log_subtract_fusion
  150.9 58.3 %reduce-scatter.2.cloned.1.call-done = bf16[128,256]{1,0:T(8,128)(2,1)} async-done(((bf16[2048,256]{1,0:T(8,128)(2,1)}), bf16[128,256]{1,0:T(8,128)(2,1)}) %reduce-scatter.2.cloned.1.call-update) | async-done | bytes 65552 | tf_op jit(solution)/shard_map/reduce_scatter | solution.py:74
  209.2 1.5 convert_element_type.56
  (10 shorter events, 0.1 us)
Async XLA Ops:
  7.2 45.3 %copy-start = (bf16[1024,1024]{1,0:T(8,128)(2,1)S(1)}, bf16[1024,1024]{1,0:T(8,128)(2,1)}, u32[]{:S(2)}) copy-start(bf16[1024,1024]{1,0:T(8,128)(2,1)} %param.17) | copy-start | bytes 6291460
  11.6 34.7 %all-to-all-start.1 = ((s32[64,1,4]{2,1,0:T(1,128)}), s32[64,1,4]{2,1,0:T(1,128)S(1)}, u32[]{:S(2)}, u32[]{:S(2)}) async-start(s32[64,1,4]{2,1,0:T(1,128)} %bitcast.3), calls=%async_computation.1 | async-start | bytes 65536 | tf_op jit(solution)/shard_map/all_to_all | solution.py:39
  46.3 30.6 %all-to-all-start = ((bf16[64,4,2048]{2,1,0:T(4,128)(2,1)}), bf16[64,4,2048]{2,1,0:T(4,128)(2,1)S(1)}, u32[]{:S(2)}, u32[]{:S(2)}) async-start(bf16[64,4,2048]{2,1,0:T(4,128)(2,1)} %reshape.79), calls=%async_computation | async-start | bytes 2097152 | tf_op jit(solution)/shard_map/all_to_all | solution.py:38
  78.0 27.0 %copy-start.3 = (s32[128]{0:T(128)S(1)}, s32[128]{0:T(128)}, u32[]{:S(2)}) copy-start(s32[128]{0:T(128)} %param.12) | copy-start | bytes 1540
  78.0 47.5 %copy-start.1 = (bf16[256,256]{1,0:T(8,128)(2,1)S(1)}, bf16[256,256]{1,0:T(8,128)(2,1)}, u32[]{:S(2)}) copy-start(bf16[256,256]{1,0:T(8,128)(2,1)} %param.14) | copy-start | bytes 393220
  82.5 43.3 %copy-start.2 = (s32[256]{0:T(256)S(1)}, s32[256]{0:T(256)}, u32[]{:S(2)}) copy-start(s32[256]{0:T(256)} %param.13) | copy-start | bytes 3076
  83.3 20.2 %all-to-all-start.2 = ((bf16[64,4,256]{2,1,0:T(4,128)(2,1)}), bf16[64,4,256]{2,1,0:T(4,128)(2,1)S(1)}, u32[]{:S(2)}, u32[]{:S(2)}) async-start(bf16[64,4,256]{2,1,0:T(4,128)(2,1)} %reshape.82), calls=%async_computation.2 | async-start | bytes 262144 | tf_op jit(solution)/shard_map/all_to_all | solution.py:44
  91.9 51.4 %all-gather.4.cloned.1.call-start = ((), (), s32[]{:S(2)}) async-start(), calls=%async_computation.5 | async-start | bytes 1114112 | tf_op jit(solution)/shard_map/all_gather | solution.py:48
  105.0 104.2 %reduce-scatter.2.cloned.1.call-start = ((), (), s32[]{:S(2)}) async-start(), calls=%async_computation.4 | async-start | bytes 1114112 | tf_op jit(solution)/shard_map/reduce_scatter | solution.py:74
Sparse Core Ops, SparseCore 0:
  105.1 38.1 all-gather.3
  147.8 61.3 reduce-scatter.1
where the time goes:
time: 218 us
  waiting for transfers between devices  117 us (54%)
  starting transfers between devices  37.4 us (17%)
  blocking collectives  20.5 us (9%)
  between operations  14.3 us (7%)
  matrix products  11.3 us (5%)
  local copies, waits for them, and re-layouts  9.93 us (5%)
  other arithmetic  6.83 us (3%)
    reduce_scatter x1, waiting for transfers between devices, shards(): lax.psum_scatter((logit_scale * lax.dot_general(residue, unit_b, (((0,),...  58.3 us
    all_to_all x1, starting transfers between devices, shards(): lax.all_to_all(packed_ids, 'shard', split_axis=0, concat_axis=0, tiled=True)  24 us
    all_to_all x1, waiting for transfers between devices, shards(): lax.all_to_all(packed, 'shard', split_axis=0, concat_axis=0, tiled=True)  22.5 us
    all_gather x1, blocking collectives, shards(): lax.all_gather(bias, 'blk', axis=0, tiled=True)  20.5 us
    all_gather x1, waiting for transfers between devices, shards(): lax.all_gather(vecs, 'blk', axis=0, tiled=True)  17.6 us
    all_to_all x1, waiting for transfers between devices, shards(): lax.all_to_all(encoded, 'shard', split_axis=0, concat_axis=0, tiled=True)  11.5 us
    all_to_all x1, starting transfers between devices, shards(): lax.all_to_all(encoded, 'shard', split_axis=0, concat_axis=0, tiled=True)  8.63 us
    all_to_all x1, waiting for transfers between devices, shards(): lax.all_to_all(packed_ids, 'shard', split_axis=0, concat_axis=0, tiled=True)  7.41 us
  transfers between devices with their start and end apart: 5, of which 5 were waited for; matrix products, arithmetic and copies ran while one was open for 5% of the time, Pallas kernels for 0%

commit v1 on v0

v1 whole, which is shorter than its diff:
```python
import functools

import jax
import jax.numpy as jnp
from jax import lax
from jax.experimental import pallas as pl
from jax.experimental.pallas import tpu as pltpu
from jax.sharding import PartitionSpec as P

logit_scale = 48.0
log2_e = 1.4426950408889634
exponent_scale = logit_scale * log2_e
vmem = pl.BlockSpec(memory_space=pltpu.VMEM)
f32, bf16 = jnp.float32, jnp.bfloat16


def call(kernel, out_shape, flops, moved, exps=0):
    many = isinstance(out_shape, (tuple, list))
    return pl.pallas_call(
        kernel,
        out_shape=out_shape,
        out_specs=[vmem] * len(out_shape) if many else vmem,
        compiler_params=pltpu.CompilerParams(vmem_limit_bytes=48 * 2**20),
        cost_estimate=pl.CostEstimate(flops=flops, bytes_accessed=moved, transcendentals=exps),
    )


def dot(a, b, contract=((1,), (0,))):
    return lax.dot_general(a, b, (contract, ((), ())), preferred_element_type=f32)


def iota(shape, dim):
    return lax.broadcasted_iota(jnp.int32, shape, dim)


def place_kernel(owners, capacity, owner_ref, id_ref, ids_ref, placing_ref):
    n = owner_ref.shape[1]
    eye = iota((n, n), 0) == iota((n, n), 1)
    owner = jnp.sum(jnp.where(eye, owner_ref[...], 0).astype(f32), 1, keepdims=True)
    ids = jnp.sum(jnp.where(eye, id_ref[...], 0).astype(f32), 1, keepdims=True)
    hot = jnp.where(owner == iota((n, owners), 1).astype(f32), 1.0, 0.0)
    earlier = jnp.where(iota((n, n), 0) > iota((n, n), 1), 1.0, 0.0).astype(bf16)
    before = dot(earlier, hot.astype(bf16))
    rank = jnp.sum(before * hot, 1, keepdims=True)
    high = jnp.floor(ids * (1.0 / 32.0))
    low = ids - 32.0 * high
    lane = iota((n, 128), 1).astype(f32)
    parts = jnp.where(lane == rank, high, 0.0) + jnp.where(lane == rank + capacity, low, 0.0)
    ids_ref[...] = dot(hot.astype(bf16), parts.astype(bf16), ((0,), (0,))).astype(jnp.int32)
    position = owner * capacity + rank
    placing_ref[...] = jnp.where(
        position == iota((n, owners * capacity), 1).astype(f32), 1.0, 0.0
    ).astype(bf16)


def rows_kernel(capacity, ids_ref, table_ref, out_ref):
    peers = ids_ref.shape[0]
    slots = peers * capacity
    peer_of = iota((slots, peers), 0) // capacity
    spread = jnp.where(peer_of == iota((slots, peers), 1), 1.0, 0.0).astype(bf16)
    parts = dot(spread, ids_ref[...].astype(bf16))
    lane, slot = iota((slots, 128), 1), iota((slots, 128), 0) % capacity
    weight = jnp.where(lane == slot, 32.0, 0.0) + jnp.where(lane == slot + capacity, 1.0, 0.0)
    ids = jnp.sum(parts * weight, 1, keepdims=True)
    hot = jnp.where(ids == iota((slots, table_ref.shape[0]), 1).astype(f32), 1.0, 0.0)
    out_ref[...] = dot(hot.astype(bf16), table_ref[...]).astype(bf16)


def encode_kernel(pre_ref, placing_ref, rows_ref, second_ref, out_ref):
    rows = dot(placing_ref[...], rows_ref[...])
    hidden = jnp.maximum(pre_ref[...] + rows, 0.0).astype(bf16)
    emb = dot(hidden, second_ref[...])
    square = jnp.sum(emb * emb, -1, keepdims=True)
    out_ref[...] = (emb * lax.rsqrt(square + 1e-06)).astype(bf16)


def partial_kernel(vecs_ref, bias_ref, units_ref, out_ref):
    blocks, rows = out_ref.shape
    peers, n, width = vecs_ref.shape

    def step(t, carry):
        units = units_ref[pl.ds(2 * t, 2), :rows, :].reshape(2 * rows, width)
        total = jnp.zeros((8, 2 * rows), f32)
        for i in range(peers // 2):
            vecs = vecs_ref[2 * i : 2 * i + 2].reshape(2 * n, width)
            logits = dot(vecs, units, ((1,), (1,)))
            bias = bias_ref[2 * i : 2 * i + 2].reshape(2 * n, 128)
            bias = jnp.concatenate([bias] * (2 * rows // 128), 1)
            total += jnp.sum(jnp.exp2(logits * exponent_scale - bias).reshape(-1, 8, 2 * rows), 0)
        total = jnp.sum(total, 0, keepdims=True)
        out_ref[pl.ds(2 * t, 1), :] = total[:, :rows]
        out_ref[pl.ds(2 * t + 1, 1), :] = total[:, rows:]
        return carry

    lax.fori_loop(0, blocks // 2, step, 0)


def user_kernel(
    place_ref, mine_ref, other_ref, bias_ref, unit_b_ref, users_ref, occurrence_ref, loss_ref, grad_ref, exps
):
    peers, n, width = mine_ref.shape
    rows = users_ref.shape[0]
    unit_b = unit_b_ref[...]
    total = jnp.zeros((rows, 128), f32)
    for half, ref in enumerate((mine_ref, other_ref)):
        for i in range(peers):
            logits = dot(unit_b, ref[i], ((1,), (1,))) * exponent_scale - bias_ref[half, i : i + 1, :]
            exponent = jnp.exp2(logits)
            total += exponent
            exps[:, (half * peers + i) * n : (half * peers + i + 1) * n] = exponent
    denominator = jnp.sum(total, 1, keepdims=True)
    place = place_ref[0]
    eye = iota((rows, rows), 0) == iota((rows, rows), 1)
    occurrence = jnp.sum(jnp.where(eye, occurrence_ref[...], 0).astype(f32), 1, keepdims=True)
    hot = jnp.where(occurrence == iota((rows, n), 1).astype(f32), 1.0, 0.0)
    own = pl.ds(pl.multiple_of(place * n, n), n)
    own_logits = dot(unit_b, mine_ref[place], ((1,), (1,))) * exponent_scale
    own_logits = own_logits - bias_ref[0, pl.ds(place, 1), :]
    picked = jnp.sum(own_logits * hot, 1, keepdims=True) * (1.0 / log2_e)
    loss = jnp.log(denominator) - picked
    loss_ref[...] = jnp.sum(jnp.where(eye, loss, 0.0), 0, keepdims=True)
    exps[:, own] = exps[:, own] - hot * denominator
    inverse = 1.0 / denominator
    direction = jnp.zeros((rows, width), f32)
    for half, ref in enumerate((mine_ref, other_ref)):
        for i in range(peers // 2):
            start = (half * peers + 2 * i) * n
            residue = (exps[:, start : start + 2 * n] * inverse).astype(bf16)
            direction += dot(residue, ref[2 * i : 2 * i + 2].reshape(2 * n, width))
    direction = logit_scale * direction
    user_f = users_ref[...].astype(f32)
    scale = lax.rsqrt(jnp.sum(user_f * user_f, -1, keepdims=True) + 1e-06)
    unit = user_f * scale
    grad_ref[...] = scale * (direction - jnp.sum(direction * unit, -1, keepdims=True) * unit)


def item_kernel(block_ref, vecs_ref, bias_ref, units_ref, first_ref, second_ref, occurrence_ref, out_ref):
    n, width = vecs_ref.shape
    blocks, rows = first_ref.shape
    vecs = vecs_ref[...]
    bias = jnp.concatenate([bias_ref[...]] * (rows // 128), 1)
    block = block_ref[0]
    grad = jnp.zeros((n, width), f32)
    for b in range(blocks):
        units = units_ref[b, :rows, :]
        inverse = 1.0 / (first_ref[b : b + 1, :] + second_ref[b : b + 1, :])
        exponent = jnp.exp2(dot(vecs, units, ((1,), (1,))) * exponent_scale - bias)
        occurrence = jnp.where(block == b, occurrence_ref[...], -1)
        hot = jnp.where(occurrence == iota((n, rows), 0), 1.0, 0.0)
        residue = (exponent * inverse - hot).astype(bf16)
        grad += dot(residue, units)
    out_ref[...] = logit_scale * grad


def shards(item_feats, owner, id_row, counts, occurrence, users, w_first, w_second, id_table):
    n, width = item_feats.shape[0], users.shape[1]
    rows = users.shape[0]
    owners, blocks = lax.axis_size("shard"), lax.axis_size("blk")
    capacity = 2 * n // owners
    slots = owners * capacity
    peers = blocks // 2
    block = lax.axis_index("blk")
    core, place = block % 2, block // 2
    swap = [(i, i ^ 1) for i in range(blocks)]

    ids, placing = call(
        functools.partial(place_kernel, owners, capacity),
        (
            jax.ShapeDtypeStruct((owners, 128), jnp.int32),
            jax.ShapeDtypeStruct((n, slots), bf16),
        ),
        8 * n * n * owners,
        4 * owners * 128,
    )(owner.reshape(1, n), id_row.reshape(1, n))
    ids = lax.all_to_all(ids.reshape(owners, 1, 128), "shard", 0, 0, tiled=True)

    user_f = users.astype(f32)
    unit_b = (user_f * lax.rsqrt(jnp.sum(user_f * user_f, -1, keepdims=True) + 1e-06)).astype(bf16)
    bias = jnp.log(counts.astype(f32)).astype(bf16)
    extra = jnp.pad(bias[None, :], ((0, 15), (0, width - n)))
    units = lax.all_gather(jnp.concatenate([unit_b, extra]), "blk", axis=0, tiled=False)
    biases = units[:, rows, :n].astype(f32) * log2_e
    biases = jnp.roll(biases.reshape(peers, 2, n).transpose(1, 0, 2), core, 0)
    bias_columns = jnp.broadcast_to(biases[0][:, :, None], (peers, n, 128))
    own_bias = lax.dynamic_index_in_dim(bias_columns, place, 0, False)

    table_rows = call(
        functools.partial(rows_kernel, capacity),
        jax.ShapeDtypeStruct((slots, id_table.shape[1]), bf16),
        2 * slots * id_table.size,
        2 * id_table.size,
    )(ids.reshape(owners, 128), id_table)
    received = lax.all_to_all(
        table_rows.reshape(owners, capacity, -1), "shard", 0, 0, tiled=True
    ).reshape(slots, -1)
    pre = jnp.dot(item_feats, w_first, preferred_element_type=f32)
    vecs = call(
        encode_kernel,
        jax.ShapeDtypeStruct((n, width), bf16),
        2 * n * slots * w_first.shape[1],
        2 * received.size,
    )(pre, placing, received, w_second)

    mine = lax.all_to_all(
        jnp.broadcast_to(vecs[None], (peers, n, width)),
        "blk",
        0,
        0,
        axis_index_groups=[list(range(c, blocks, 2)) for c in range(2)],
        tiled=True,
    )
    other = lax.ppermute(mine, "blk", swap)
    first = call(
        partial_kernel,
        jax.ShapeDtypeStruct((blocks, rows), f32),
        2 * blocks * rows * peers * n * width,
        units.size * 2,
        blocks * rows * peers * n,
    )(mine, bias_columns, units)
    second = lax.ppermute(first, "blk", swap)
    smem = pl.BlockSpec(memory_space=pltpu.SMEM)
    params = pltpu.CompilerParams(vmem_limit_bytes=48 * 2**20)
    loss, user_grad = pl.pallas_call(
        user_kernel,
        out_shape=(jax.ShapeDtypeStruct((1, rows), f32), jax.ShapeDtypeStruct((rows, width), f32)),
        in_specs=[smem] + [vmem] * 6,
        out_specs=[vmem] * 2,
        scratch_shapes=[pltpu.VMEM((rows, blocks * n), f32)],
        compiler_params=params,
        cost_estimate=pl.CostEstimate(
            flops=4 * rows * blocks * n * width,
            bytes_accessed=2 * units.size,
            transcendentals=rows * blocks * n,
        ),
    )(place[None], mine, other, biases, unit_b, users, occurrence.reshape(1, rows))
    item_grad = pl.pallas_call(
        item_kernel,
        out_shape=jax.ShapeDtypeStruct((n, width), f32),
        in_specs=[smem] + [vmem] * 6,
        out_specs=vmem,
        compiler_params=params,
        cost_estimate=pl.CostEstimate(
            flops=4 * rows * blocks * n * width,
            bytes_accessed=2 * units.size,
            transcendentals=rows * blocks * n,
        ),
    )(block[None], vecs, own_bias, units, first, second, occurrence.reshape(1, rows))
    return (loss.reshape(rows), user_grad, item_grad)


def solution(mesh):
    return jax.shard_map(
        shards,
        mesh=mesh,
        in_specs=(
            P(("shard", "blk"), None),
            P(("shard", "blk"), None),
            P(("shard", "blk")),
            P(("shard", "blk")),
            P(("shard", "blk")),
            P(("shard", "blk"), None),
            P(),
            P(),
            P("shard", None),
        ),
        out_specs=(P(("shard", "blk")), P(("shard", "blk"), None), P(("shard", "blk"), None)),
        check_vma=False,
    )
```

time: 218 us -> 120 us (0.55)
  waiting for transfers between devices: 117 us -> 24.9 us
  starting transfers between devices: 37.4 us -> 21.4 us
  blocking collectives: 20.5 us -> 34.6 us
  Pallas kernels: 0 us -> 10.4 us
  matrix products: 11.3 us -> 2.95 us
  local copies, waits for them, and re-layouts: 9.93 us -> 6.83 us
  other arithmetic: 6.83 us -> 4.19 us
    reduce_scatter x1 -> x0, waiting for transfers between devices: 58.3 us -> none  [shards(): lax.psum_scatter((logit_scale * lax.dot_general(residue, unit_b, (((0,),...]
    all_to_all x0 -> x1, blocking collectives: none -> 34.6 us  [shards(): ids = lax.all_to_all(ids.reshape(owners, 1, 128), 'shard', 0, 0, tiled=True)]
    all_to_all x3 -> x2, starting transfers between devices: 37.3 us -> 11.1 us  [the longest x1 6.46 us: shards(): lax.all_to_all(jnp.broadcast_to(vecs[None], (peers, n, width)), 'blk', 0,...]
    all_gather x1 -> x0, blocking collectives: 20.5 us -> none  [shards(): lax.all_gather(bias, 'blk', axis=0, tiled=True)]
    all_gather x1, waiting for transfers between devices: 17.6 us -> 0.02 us  [shards(): lax.all_gather(jnp.concatenate([unit_b, extra]), 'blk', axis=0, tiled=False)]
    all_to_all x3 -> x2, waiting for transfers between devices: 41.4 us -> 24.8 us  [the longest x1 12.6 us: shards(): lax.all_to_all(table_rows.reshape(owners, capacity, -1), 'shard', 0, 0, t...]
    pallas_call x0 -> x6, Pallas kernels: none -> 10.4 us  [the longest x1 3.93 us: shards(): call(partial_kernel, jax.ShapeDtypeStruct((blocks, rows), f32), 2 * block...]
    ppermute x0 -> x2, starting transfers between devices: none -> 10.3 us  [the longest x1 8.34 us: shards(): other = lax.ppermute(mine, 'blk', swap)]
  transfers between devices with their start and end apart: 5 -> 5, of which waited for: 5 -> 2; matrix products, arithmetic and copies ran while one was open for 5% -> 5% of each run, Pallas kernels for 0% -> 7%
where the time goes in v1:
time: 120 us; the launch traced here: 119 us
  blocking collectives  34.6 us (29%)
  waiting for transfers between devices  24.9 us (21%)
  starting transfers between devices  21.4 us (18%)
  between operations  14.2 us (12%)
  Pallas kernels  10.4 us (9%)
  local copies, waits for them, and re-layouts  6.83 us (6%)
  other arithmetic  4.19 us (3%)
  matrix products  2.95 us (2%)
    all_to_all x1, blocking collectives, shards(): ids = lax.all_to_all(ids.reshape(owners, 1, 128), 'shard', 0, 0, tiled=True)  34.6 us
    all_to_all x1, waiting for transfers between devices, shards(): lax.all_to_all(table_rows.reshape(owners, capacity, -1), 'shard', 0, 0, t...  12.6 us
    all_to_all x1, waiting for transfers between devices, shards(): lax.all_to_all(jnp.broadcast_to(vecs[None], (peers, n, width)), 'blk', 0,...  12.2 us
    ppermute x1, starting transfers between devices, shards(): other = lax.ppermute(mine, 'blk', swap)  8.34 us
    all_to_all x1, starting transfers between devices, shards(): lax.all_to_all(jnp.broadcast_to(vecs[None], (peers, n, width)), 'blk', 0,...  6.46 us
    all_to_all x1, starting transfers between devices, shards(): lax.all_to_all(table_rows.reshape(owners, capacity, -1), 'shard', 0, 0, t...  4.63 us
    unnamed x18, local copies, waits for them, and re-layouts  4.59 us
    pallas_call x1, Pallas kernels, shards(): call(partial_kernel, jax.ShapeDtypeStruct((blocks, rows), f32), 2 * block...  3.93 us
  transfers between devices with their start and end apart: 5, of which 2 were waited for; matrix products, arithmetic and copies ran while one was open for 5% of the time, Pallas kernels for 7%

profile of v1, /device:TPU:1, one launch (start us, length us, event | category | flops | bytes accessed | tf_op | source)
XLA Modules:
  0.0 119.4 jit_solution(7142588519176723133)
XLA Ops:
  7.2 0.0 copy-start
  7.2 0.0 all-gather.3.cloned.1.call-start
  7.2 0.7 convert_bitcast_fusion
  7.9 1.0 fusion.1
  9.0 1.0 fusion.2.unit_b_ref
  10.0 0.7 fusion.3
  10.7 0.0 all-gather.3.cloned.1.call-update
  10.7 0.0 copy-start.7
  10.7 0.6 copy-done.7
  11.3 0.0 copy-start.8
  11.3 0.7 copy-done.8
  12.0 0.4 shard_map.112
  12.4 34.6 %all_to_all.15 = s32[64,1,128]{2,1,0:T(1,128)S(1)} all-to-all(s32[64,1,128]{2,1,0:T(1,128)S(1)} %bitcast.27), channel_id=1, replica_groups=mesh['shard'=64,'blk'=16] {'shard'}, dimensions={0} | all-to-all | bytes 65536 | tf_op jit(solution)/shard_map/all_to_all | solution.py:175
  47.0 0.0 copy-start.3
  47.0 1.6 %copy-done.3 = bf16[1024,1024]{1,0:T(8,128)(2,1)S(1)} copy-done((bf16[1024,1024]{1,0:T(8,128)(2,1)S(1)}, bf16[1024,1024]{1,0:T(8,128)(2,1)}, u32[]{:S(2)}) %copy-start.3) | copy-done | bytes 2097176
  48.7 0.9 shard_map.113
  49.6 0.0 copy-start.4
  49.6 1.0 reshape.51
  50.6 4.6 %all-to-all-start.1 = ((bf16[64,4,1024]{2,1,0:T(4,128)(2,1)}), bf16[64,4,1024]{2,1,0:T(4,128)(2,1)S(1)}, u32[]{:S(2)}, u32[]{:S(2)}) async-start(bf16[64,4,1024]{2,1,0:T(4,128)(2,1)} %reshape.51), calls=%async_computation.1 | async-start | bytes 1048576 | tf_op jit(solution)/shard_map/all_to_all | solution.py:193
  55.2 0.0 copy-done
  55.2 2.9 %fusion.7.pre_ref = f32[128,1024]{1,0:T(8,128)S(1)} fusion(bf16[128,2048]{1,0:T(8,128)(2,1)S(1)} %copy-done, bf16[2048,1024]{1,0:T(8,128)(2,1)} %param.15), kind=kOutput, calls=%fused_computation.18 | convolution fusion | flops 536870912 | bytes 5242880 | tf_op jit(solution)/shard_map/dot_general | solution.py:196
  58.2 12.6 %all-to-all-done.1 = bf16[64,4,1024]{2,1,0:T(4,128)(2,1)S(1)} async-done(((bf16[64,4,1024]{2,1,0:T(4,128)(2,1)}), bf16[64,4,1024]{2,1,0:T(4,128)(2,1)S(1)}, u32[]{:S(2)}, u32[]{:S(2)}) %all-to-all-start.1) | async-done | bytes 524320 | tf_op jit(solution)/shard_map/all_to_all | solution.py:193
  70.8 0.1 reshape.52.rows_ref
  70.9 0.0 copy-done.4
  70.9 0.5 shard_map.114.vecs_ref
  71.4 0.8 broadcast_in_dim.28
  72.3 6.5 %all-to-all-start.2 = ((bf16[8,128,256]{2,1,0:T(8,128)(2,1)}), bf16[8,128,256]{2,1,0:T(8,128)(2,1)S(1)}, u32[]{:S(2)}, u32[]{:S(2)}) async-start(bf16[8,128,256]{2,1,0:T(8,128)(2,1)} %broadcast_in_dim.28), calls=%async_computation.2 | async-start | bytes 1048576 | tf_op jit(solution)/shard_map/all_to_all | solution.py:204
  78.7 12.2 %all-to-all-done.2.mine_ref.vecs_ref = bf16[8,128,256]{2,1,0:T(8,128)(2,1)S(1)} async-done(((bf16[8,128,256]{2,1,0:T(8,128)(2,1)}), bf16[8,128,256]{2,1,0:T(8,128)(2,1)S(1)}, u32[]{:S(2)}, u32[]{:S(2)}) %all-to-all-start.2) | async-done | bytes 524320 | tf_op jit(solution)/shard_map/all_to_all | solution.py:204
  90.9 8.3 %collective-permute-start = (bf16[8,128,256]{2,1,0:T(8,128)(2,1)S(1)}, bf16[8,128,256]{2,1,0:T(8,128)(2,1)S(1)}, u32[]{:S(2)}, u32[]{:S(2)}) collective-permute-start(bf16[8,128,256]{2,1,0:T(8,128)(2,1)S(1)} %all-to-all-done.2.mine_ref.vecs_ref), channel_id=1, source_target_pairs={{0,1},{1,0},{2,3},{3,2},{4,5},{5,4},{6,7},{7,6},{8,9},{9,8},{10,11... | collective-permute-start | bytes 1572872 | tf_op jit(solution)/shard_map/ppermute | solution.py:212
  99.3 0.0 all-gather.3.cloned.1.call-done
  99.3 0.8 fusion.5
  100.1 0.0 copy-start.5
  100.1 0.0 copy-start.6
  100.1 0.2 broadcast_in_dim.34.bias_ref
  100.3 0.0 copy-start.1
  100.4 1.6 %copy-done.1 = bf16[4352,256]{1,0:T(8,128)(2,1)S(1)} copy-done((bf16[4352,256]{1,0:T(8,128)(2,1)S(1)}, bf16[4352,256]{1,0:T(8,128)(2,1)}, u32[]{:S(2)}) %copy-start.1) | copy-done | bytes 2228248
  102.0 0.0 copy-start.2
  102.0 3.9 %shard_map.116.first_ref = f32[16,256]{1,0:T(8,128)S(1)} custom-call(bf16[8,128,256]{2,1,0:T(8,128)(2,1)S(1)} %all-to-all-done.2.mine_ref.vecs_ref, f32[8,128,128]{2,1,0:T(8,128)S(1)} %broadcast_in_dim.34.bias_ref, bf16[16,272,256]{2,1,0:T(8,128)(2,1)S(1)} %bitcast.24), custom_call_target="tpu_custom_call" | custom-call | flops 2147483648 | bytes 2228224 | tf_op jit(solution)/shard_map/pallas_call | solution.py:213
  105.9 1.9 %collective-permute-start.1 = (f32[16,256]{1,0:T(8,128)S(1)}, f32[16,256]{1,0:T(8,128)S(1)}, u32[]{:S(2)}, u32[]{:S(2)}) collective-permute-start(f32[16,256]{1,0:T(8,128)S(1)} %shard_map.116.first_ref), channel_id=1, source_target_pairs={{0,1},{1,0},{2,3},{3,2},{4,5},{5,4},{6,7},{7,6},{8,9},{9,8},{10,11... | collective-permute-start | bytes 49160 | tf_op jit(solution)/shard_map/ppermute | solution.py:220
  107.9 0.0 collective-permute-done.other_ref
  107.9 0.0 copy-done.5
  107.9 0.0 copy-done.6
  107.9 2.5 %shard_map.115 = (f32[1,256]{1,0:T(1,128)}, f32[256,256]{1,0:T(8,128)}) custom-call(s32[1]{0:T(128)} %bitcast.place_ref, bf16[8,128,256]{2,1,0:T(8,128)(2,1)S(1)} %all-to-all-done.2.mine_ref.vecs_ref, bf16[8,128,256]{2,1,0:T(8,128)(2,1)S(1)} %collective-permute-done.other_ref, f32[2,8,128]{2,1,0:T(8,128)S(1)} %fusion.4.bias_ref, ...), custom_call_target="tpu_custom_call" | custom-call | flops 536870912 | bytes 2228224 | tf_op jit(solution)/shard_map/pallas_call | solution.py:223
  110.4 0.0 collective-permute-done.1.second_ref
  110.4 0.1 broadcast_in_dim.32.bias_ref
  110.4 0.0 copy-done.2
  110.5 2.1 %shard_map.117 = f32[128,256]{1,0:T(8,128)} custom-call(s32[1]{0:T(128)} %bitcast.12.block_ref, bf16[128,256]{1,0:T(8,128)(2,1)S(1)} %shard_map.114.vecs_ref, f32[128,128]{1,0:T(8,128)S(1)} %broadcast_in_dim.32.bias_ref, bf16[16,272,256]{2,1,0:T(8,128)(2,1)S(1)} %bitcast.25, f32[16,256]{1,0:T(8,128)S(1)} %shard_map.116.first_ref, ...), custom_call_target="tpu_custom_call" | custom-call | flops 536870912 | bytes 2228224 | tf_op jit(solution)/shard_map/pallas_call | solution.py:236
  (5 shorter events, 0.0 us)
Async XLA Ops:
  7.2 48.0 %copy-start = (bf16[128,2048]{1,0:T(8,128)(2,1)S(1)}, bf16[128,2048]{1,0:T(8,128)(2,1)}, u32[]{:S(2)}) copy-start(bf16[128,2048]{1,0:T(8,128)(2,1)} %param.9) | copy-start | bytes 1572868
  7.2 92.1 %all-gather.3.cloned.1.call-start = ((), (), s32[]{:S(2)}) async-start(), calls=%async_computation.3 | async-start | bytes 2367488 | tf_op jit(solution)/shard_map/all_gather | solution.py:181
  10.7 0.7 copy-start.7
  11.3 0.7 copy-start.8
  47.0 1.6 %copy-start.3 = (bf16[1024,1024]{1,0:T(8,128)(2,1)S(1)}, bf16[1024,1024]{1,0:T(8,128)(2,1)}, u32[]{:S(2)}) copy-start(bf16[1024,1024]{1,0:T(8,128)(2,1)} %table_ref.1) | copy-start | bytes 6291460
  49.6 21.4 %copy-start.4 = (bf16[1024,256]{1,0:T(8,128)(2,1)S(1)}, bf16[1024,256]{1,0:T(8,128)(2,1)}, u32[]{:S(2)}) copy-start(bf16[1024,256]{1,0:T(8,128)(2,1)} %second_ref.1) | copy-start | bytes 1572868
  50.6 20.2 %all-to-all-start.1 = ((bf16[64,4,1024]{2,1,0:T(4,128)(2,1)}), bf16[64,4,1024]{2,1,0:T(4,128)(2,1)S(1)}, u32[]{:S(2)}, u32[]{:S(2)}) async-start(bf16[64,4,1024]{2,1,0:T(4,128)(2,1)} %reshape.51), calls=%async_computation.1 | async-start | bytes 1048576 | tf_op jit(solution)/shard_map/all_to_all | solution.py:193
  72.3 18.7 %all-to-all-start.2 = ((bf16[8,128,256]{2,1,0:T(8,128)(2,1)}), bf16[8,128,256]{2,1,0:T(8,128)(2,1)S(1)}, u32[]{:S(2)}, u32[]{:S(2)}) async-start(bf16[8,128,256]{2,1,0:T(8,128)(2,1)} %broadcast_in_dim.28), calls=%async_computation.2 | async-start | bytes 1048576 | tf_op jit(solution)/shard_map/all_to_all | solution.py:204
  90.9 16.9 %collective-permute-start = (bf16[8,128,256]{2,1,0:T(8,128)(2,1)S(1)}, bf16[8,128,256]{2,1,0:T(8,128)(2,1)S(1)}, u32[]{:S(2)}, u32[]{:S(2)}) collective-permute-start(bf16[8,128,256]{2,1,0:T(8,128)(2,1)S(1)} %all-to-all-done.2.mine_ref.vecs_ref), channel_id=1, source_target_pairs={{0,1},{1,0},{2,3},{3,2},{4,5},{5,4},{6,7},{7,6},{8,9},{9,8},{10,11... | collective-permute-start | bytes 1572872 | tf_op jit(solution)/shard_map/ppermute | solution.py:212
  100.1 7.8 %copy-start.5 = (bf16[256,256]{1,0:T(8,128)(2,1)S(1)}, bf16[256,256]{1,0:T(8,128)(2,1)}, u32[]{:S(2)}) copy-start(bf16[256,256]{1,0:T(8,128)(2,1)} %users_ref.1) | copy-start | bytes 393220
  100.1 7.7 %copy-start.6 = (s32[256]{0:T(256)S(1)}, s32[256]{0:T(256)}, u32[]{:S(2)}) copy-start(s32[256]{0:T(256)} %param.13) | copy-start | bytes 3076
  100.3 1.6 %copy-start.1 = (bf16[4352,256]{1,0:T(8,128)(2,1)S(1)}, bf16[4352,256]{1,0:T(8,128)(2,1)}, u32[]{:S(2)}) copy-start(bf16[4352,256]{1,0:T(8,128)(2,1)} %all-gather.3.cloned.1.call-done) | copy-start | bytes 6684676
  102.0 8.5 %copy-start.2 = (bf16[4352,256]{1,0:T(8,128)(2,1)S(1)}, bf16[4352,256]{1,0:T(8,128)(2,1)}, u32[]{:S(2)}) copy-start(bf16[4352,256]{1,0:T(8,128)(2,1)} %all-gather.3.cloned.1.call-done) | copy-start | bytes 6684676
  105.9 4.5 %collective-permute-start.1 = (f32[16,256]{1,0:T(8,128)S(1)}, f32[16,256]{1,0:T(8,128)S(1)}, u32[]{:S(2)}, u32[]{:S(2)}) collective-permute-start(f32[16,256]{1,0:T(8,128)S(1)} %shard_map.116.first_ref), channel_id=1, source_target_pairs={{0,1},{1,0},{2,3},{3,2},{4,5},{5,4},{6,7},{7,6},{8,9},{9,8},{10,11... | collective-permute-start | bytes 49160 | tf_op jit(solution)/shard_map/ppermute | solution.py:220
Sparse Core Ops, SparseCore 0:
  11.3 57.0 all-gather.2

commit v2 on v1

v2 whole, which is shorter than its diff:
```python
import functools

import jax
import jax.numpy as jnp
from jax import lax
from jax.experimental import pallas as pl
from jax.experimental.pallas import tpu as pltpu
from jax.sharding import PartitionSpec as P

logit_scale = 48.0
log2_e = 1.4426950408889634
exponent_scale = logit_scale * log2_e
vmem = pl.BlockSpec(memory_space=pltpu.VMEM)
far_memory = pl.BlockSpec(memory_space=pltpu.HBM)
f32, bf16 = jnp.float32, jnp.bfloat16


def call(kernel, out_shape, flops, moved, exps=0, in_specs=None, scratch=(), room=16):
    options = {} if in_specs is None else {"in_specs": in_specs}
    return pl.pallas_call(
        kernel,
        out_shape=out_shape,
        out_specs=[vmem] * len(out_shape) if isinstance(out_shape, tuple) else vmem,
        scratch_shapes=scratch,
        compiler_params=pltpu.CompilerParams(vmem_limit_bytes=room * 2**20),
        cost_estimate=pl.CostEstimate(flops=flops, bytes_accessed=moved, transcendentals=exps),
        **options,
    )


def dot(a, b, contract=((1,), (0,))):
    return lax.dot_general(a, b, (contract, ((), ())), preferred_element_type=f32)


def iota(shape, dim):
    return lax.broadcasted_iota(jnp.int32, shape, dim)


def place_kernel(
    owners,
    capacity,
    owner_in,
    id_in,
    users_in,
    counts_in,
    ids_ref,
    placing_ref,
    payload_ref,
    owner_ref,
    id_ref,
    users_ref,
    counts_ref,
    sems,
):
    pairs = (owner_in, owner_ref), (id_in, id_ref), (users_in, users_ref), (counts_in, counts_ref)
    copies = [pltpu.make_async_copy(*pair, sems.at[i]) for i, pair in enumerate(pairs)]
    for copy in copies:
        copy.start()
    for copy in copies:
        copy.wait()
    n = owner_ref.shape[1]
    eye = iota((n, n), 0) == iota((n, n), 1)
    owner = jnp.sum(jnp.where(eye, owner_ref[...], 0).astype(f32), 1, keepdims=True)
    ids = jnp.sum(jnp.where(eye, id_ref[...], 0).astype(f32), 1, keepdims=True)
    hot = jnp.where(owner == iota((n, owners), 1).astype(f32), 1.0, 0.0)
    earlier = jnp.where(iota((n, n), 0) > iota((n, n), 1), 1.0, 0.0).astype(bf16)
    before = dot(earlier, hot.astype(bf16))
    rank = jnp.sum(before * hot, 1, keepdims=True)
    high = jnp.floor(ids * (1.0 / 32.0))
    low = ids - 32.0 * high
    lane = iota((n, 128), 1).astype(f32)
    parts = jnp.where(lane == rank, high, 0.0) + jnp.where(lane == rank + capacity, low, 0.0)
    ids_ref[...] = dot(hot.astype(bf16), parts.astype(bf16), ((0,), (0,))).astype(jnp.int32)
    position = owner * capacity + rank
    placing_ref[...] = jnp.where(
        position == iota((n, owners * capacity), 1).astype(f32), 1.0, 0.0
    ).astype(bf16)
    rows = users_ref.shape[0]
    user_f = users_ref[...].astype(f32)
    inverse = lax.rsqrt(jnp.sum(user_f * user_f, -1, keepdims=True) + 1e-06)
    payload_ref[:rows, :] = (user_f * inverse).astype(bf16)
    bias = jnp.broadcast_to(jnp.log(counts_ref[...].astype(f32)), (16, n))
    payload_ref[rows:, :] = jnp.concatenate([bias] * (payload_ref.shape[1] // n), 1).astype(bf16)


def table_kernel(table_in, after_ref, table_ref, sem):
    copy = pltpu.make_async_copy(table_in, table_ref, sem)
    copy.start()
    copy.wait()


def rows_kernel(capacity, ids_ref, table_ref, out_ref):
    peers = ids_ref.shape[0]
    slots = peers * capacity
    peer_of = iota((slots, peers), 0) // capacity
    spread = jnp.where(peer_of == iota((slots, peers), 1), 1.0, 0.0).astype(bf16)
    parts = dot(spread, ids_ref[...].astype(bf16))
    lane, slot = iota((slots, 128), 1), iota((slots, 128), 0) % capacity
    weight = jnp.where(lane == slot, 32.0, 0.0) + jnp.where(lane == slot + capacity, 1.0, 0.0)
    ids = jnp.sum(parts * weight, 1, keepdims=True)
    hot = jnp.where(ids == iota((slots, table_ref.shape[0]), 1).astype(f32), 1.0, 0.0).astype(bf16)
    out_ref[...] = dot(hot, table_ref[...]).astype(bf16).reshape(out_ref.shape)


def encode_kernel(pre_ref, placing_ref, rows_ref, second_ref, out_ref):
    rows = dot(placing_ref[...], rows_ref[...].reshape(placing_ref.shape[1], -1))
    hidden = jnp.maximum(pre_ref[...] + rows, 0.0).astype(bf16)
    emb = dot(hidden, second_ref[...])
    square = jnp.sum(emb * emb, -1, keepdims=True)
    vecs = (emb * lax.rsqrt(square + 1e-06)).astype(bf16)
    for i in range(out_ref.shape[0]):
        out_ref[i] = vecs


def column(row):
    n = row.shape[1]
    return jnp.sum(jnp.where(iota((n, n), 0) == iota((n, n), 1), row, 0.0), 1, keepdims=True)


def sums(place, vecs_ref, bias_ref, unit_refs, store):
    peers, n, width = vecs_ref.shape
    rows = unit_refs[0].shape[1] - 16
    biases = [bias_ref[pl.ds(lax.rem(place - i + peers, peers), 1), :] for i in range(peers)]
    biases = [jnp.broadcast_to(column(bias), (n, 128)) for bias in biases]
    for t in range(0, 2 * len(unit_refs), 2):
        units = unit_refs[t // 2][:, :rows, :].reshape(2 * rows, width)

        def step(i, total):
            vecs = vecs_ref[pl.ds(2 * i, 2)].reshape(2 * n, width)
            logits = dot(vecs, units, ((1,), (1,)))
            bias = jnp.concatenate(biases[2 * i : 2 * i + 2])
            bias = jnp.concatenate([bias] * (2 * rows // 128), 1)
            exponent = jnp.exp2(logits * exponent_scale - bias)
            return total + jnp.sum(exponent.reshape(-1, 8, 2 * rows), 0)

        total = jnp.zeros((8, 2 * rows), f32)
        for i in range(peers // 2):
            total = step(i, total)
        total = jnp.sum(total, 0, keepdims=True)
        store(t, total[:, :rows])
        store(t + 1, total[:, rows:])


def first_kernel(place_ref, vecs_ref, bias_ref, *refs):
    out_ref = refs[-1]

    def store(t, value):
        out_ref[t : t + 1, :] = value

    sums(place_ref[0], vecs_ref, bias_ref, refs[:-1], store)


def item_sum(vecs, bias, units, sums_ref, hot):
    n, width = vecs.shape
    bias = jnp.broadcast_to(column(bias), (n, 128))
    grad = jnp.zeros((n, width), f32)
    rows = units[0].shape[1] - 16
    for t in range(2 * len(units)):
        unit = units[t // 2][t % 2, :rows, :]
        exponent = jnp.exp2(
            dot(vecs, unit, ((1,), (1,))) * exponent_scale
            - jnp.concatenate([bias] * (rows // 128), 1)
        )
        residue = exponent * (1.0 / sums_ref[t : t + 1, :])
        if t == 0 and hot is not None:
            residue = residue - hot
        grad += dot(residue.astype(bf16), unit)
    return logit_scale * grad


def second_kernel(place_ref, vecs_ref, bias_ref, first_ref, *refs):
    units, sums_ref, grad_ref = refs[:-2], refs[-2], refs[-1]
    place = place_ref[0]

    def store(t, value):
        sums_ref[t : t + 1, :] = first_ref[t : t + 1, :] + value

    sums(place, vecs_ref, bias_ref, units, store)
    grad_ref[...] = item_sum(vecs_ref[place], bias_ref[0:1, :], units, sums_ref, None)


def user_kernel(
    place_ref,
    mine_ref,
    other_ref,
    bias_ref,
    other_bias_ref,
    sums_ref,
    users_ref,
    occurrence_ref,
    units_ref,
    loss_ref,
    grad_ref,
    exps,
):
    peers, n, width = mine_ref.shape
    rows = users_ref.shape[0]
    place = place_ref[0]
    unit_b = units_ref[0, :rows, :]
    denominator = column(sums_ref[0:1, :])
    inverse = 1.0 / denominator
    occurrence = column(occurrence_ref[...].astype(f32))
    hot = jnp.where(occurrence == iota((rows, n), 1).astype(f32), 1.0, 0.0)
    direction = jnp.zeros((rows, width), f32)
    for half, (ref, bias_half) in enumerate(((mine_ref, bias_ref), (other_ref, other_bias_ref))):
        for i in range(peers):
            bias = bias_half[pl.ds(lax.rem(place - i + peers, peers), 1), :]
            logits = dot(unit_b, ref[i], ((1,), (1,))) * exponent_scale - bias
            exps[:, i * n : (i + 1) * n] = jnp.exp2(logits) * inverse
        if half == 0:
            own = pl.ds(pl.multiple_of(place * n, n), n)
            exps[:, own] = exps[:, own] - hot
        direction += dot(exps[...].astype(bf16), ref[...].reshape(peers * n, width))
    own_logits = dot(unit_b, mine_ref[place], ((1,), (1,))) * exponent_scale - bias_ref[0:1, :]
    picked = jnp.sum(own_logits * hot, 1, keepdims=True) * (1.0 / log2_e)
    loss = jnp.log(denominator) - picked
    eye = iota((rows, rows), 0) == iota((rows, rows), 1)
    loss_ref[...] = jnp.sum(jnp.where(eye, loss, 0.0), 0, keepdims=True)
    direction = logit_scale * direction
    user_f = users_ref[...].astype(f32)
    scale = lax.rsqrt(jnp.sum(user_f * user_f, -1, keepdims=True) + 1e-06)
    unit = user_f * scale
    grad_ref[...] = scale * (direction - jnp.sum(direction * unit, -1, keepdims=True) * unit)


def item_kernel(place_ref, mine_ref, bias_ref, sums_ref, occurrence_ref, taken_ref, *refs):
    units, out_ref = refs[:-1], refs[-1]
    n, rows = mine_ref.shape[1], occurrence_ref.shape[1]
    hot = jnp.where(occurrence_ref[...] == iota((n, rows), 0), 1.0, 0.0)
    grad = item_sum(mine_ref[place_ref[0]], bias_ref[0:1, :], units, sums_ref, hot)
    out_ref[...] = grad + taken_ref[...]


def shards(item_feats, owner, id_row, counts, occurrence, users, w_first, w_second, id_table):
    n, width = item_feats.shape[0], users.shape[1]
    rows = users.shape[0]
    owners, blocks = lax.axis_size("shard"), lax.axis_size("blk")
    capacity = 2 * n // owners
    slots = owners * capacity
    peers = blocks // 2
    block = lax.axis_index("blk")
    core, place = block % 2, block // 2
    swap = [(i, i ^ 1) for i in range(blocks)]

    shape = jax.ShapeDtypeStruct
    place_sizes = (
        shape((owners, 128), jnp.int32),
        shape((n, slots), bf16),
        shape((rows + 16, width), bf16),
    )
    ids_sent, placing, payload = call(
        functools.partial(place_kernel, owners, capacity),
        place_sizes,
        8 * n * n * owners,
        4 * owners * 128,
        in_specs=[far_memory] * 4,
        scratch=[
            pltpu.VMEM((1, n), jnp.int32),
            pltpu.VMEM((1, n), jnp.int32),
            pltpu.VMEM((rows, width), bf16),
            pltpu.VMEM((1, n), jnp.int32),
            pltpu.SemaphoreType.DMA((4,)),
        ],
        room=60,
    )(owner.reshape(1, n), id_row.reshape(1, n), users, counts.reshape(1, n))
    ids = lax.all_to_all(ids_sent.reshape(owners, 1, 128), "shard", 0, 0, tiled=True)
    table = call(
        table_kernel,
        shape(id_table.shape, bf16),
        0,
        4 * id_table.size,
        in_specs=[far_memory] * 2,
        scratch=[pltpu.SemaphoreType.DMA],
    )(id_table, ids_sent)

    def turn(array, step, other_step=None):
        steps = (step, step if other_step is None else other_step)
        pairs = [(i, (i + 2 * steps[i % 2]) % blocks) for i in range(blocks)]
        return lax.ppermute(array, "blk", pairs)

    table_rows = call(
        functools.partial(rows_kernel, capacity),
        shape((owners, capacity, id_table.shape[1]), bf16),
        2 * slots * id_table.size,
        2 * id_table.size,
    )(ids.reshape(owners, 128), table)
    far = turn(payload, peers // 2)
    table_rows, payload, far = lax.optimization_barrier((table_rows, payload, far))
    received = lax.all_to_all(table_rows, "shard", 0, 0, tiled=True)
    pair = jnp.stack([payload, far])
    units = [pair, turn(pair, 1), turn(pair, -1), turn(pair, 2, -2)]
    bias = [u[i, rows : rows + 1, :n] for u in units for i in range(2)]
    first_core = core == 0
    bias_2, bias_6 = jnp.where(first_core, bias[6], bias[7]), jnp.where(first_core, bias[7], bias[6])
    ordered = [bias[0], bias[2], bias_2, bias[5], bias[1], bias[3], bias_6, bias[4]]
    biases = jnp.concatenate(ordered).astype(f32) * log2_e
    other_biases = lax.ppermute(biases, "blk", swap)

    pre = jnp.dot(item_feats, w_first, preferred_element_type=f32)
    vecs = call(
        encode_kernel,
        shape((peers, n, width), bf16),
        2 * n * slots * w_first.shape[1],
        2 * received.size,
    )(pre, placing, received, w_second)

    mine = lax.all_to_all(
        vecs,
        "blk",
        0,
        0,
        axis_index_groups=[list(range(c, blocks, 2)) for c in range(2)],
        tiled=True,
    )
    mine, biases, other_biases = lax.optimization_barrier((mine, biases, other_biases))
    other = lax.ppermute(mine, "blk", swap)
    smem = pl.BlockSpec(memory_space=pltpu.SMEM)

    def step(kernel, out_shape, pairs, inputs, scratch=()):
        specs = [smem] + [vmem] * (len(inputs) - 1)
        moved = peers * rows * width * 4
        return call(kernel, out_shape, 2 * pairs * width, moved, pairs, specs, scratch, 48)(*inputs)

    at, occurrence = place[None], occurrence.reshape(1, rows)
    pairs = peers * rows * peers * n
    first = step(first_kernel, shape((peers, rows), f32), pairs, (at, mine, biases, *units))
    total, given = step(
        second_kernel,
        (shape((peers, rows), f32), shape((n, width), f32)),
        pairs,
        (at, other, other_biases, first, *units),
    )
    taken = lax.ppermute(given, "blk", swap)
    loss, user_grad = step(
        user_kernel,
        (shape((1, rows), f32), shape((rows, width), f32)),
        pairs,
        (at, mine, other, biases, other_biases, total, users, occurrence, pair),
        [pltpu.VMEM((rows, peers * n), f32)],
    )
    item_grad = step(
        item_kernel,
        shape((n, width), f32),
        peers * rows * n,
        (at, mine, biases, total, occurrence, taken, *units),
    )
    return (loss.reshape(rows), user_grad, item_grad)


def solution(mesh):
    return jax.shard_map(
        shards,
        mesh=mesh,
        in_specs=(
            P(("shard", "blk"), None),
            P(("shard", "blk"), None),
            P(("shard", "blk")),
            P(("shard", "blk")),
            P(("shard", "blk")),
            P(("shard", "blk"), None),
            P(),
            P(),
            P("shard", None),
        ),
        out_specs=(P(("shard", "blk")), P(("shard", "blk"), None), P(("shard", "blk"), None)),
        check_vma=False,
    )
```

time: 120 us -> 105 us (0.88)
  starting transfers between devices: 21.4 us -> 72 us
  blocking collectives: 34.6 us -> 0 us
  between operations: 14.2 us -> 0.85 us
  waiting for transfers between devices: 24.9 us -> 12.6 us
  local copies, waits for them, and re-layouts: 6.83 us -> 3.14 us
  other arithmetic: 4.19 us -> 0.95 us
  Pallas kernels: 10.4 us -> 12.3 us
    all_to_all x1 -> x0, blocking collectives: 34.6 us -> none  [shards(): ids = lax.all_to_all(ids.reshape(owners, 1, 128), 'shard', 0, 0, tiled=True)]
    ppermute x1 -> x6, starting transfers between devices: 1.92 us -> 34.2 us  [the longest x4 16.6 us: turn(): return lax.ppermute(array, 'blk', pairs)]
    all_to_all x2 -> x3, starting transfers between devices: 11.1 us -> 34.2 us  [the longest x1 25.3 us: shards(): lax.all_to_all(ids_sent.reshape(owners, 1, 128), 'shard', 0, 0, tiled=True)]
    all_to_all x2 -> x3, waiting for transfers between devices: 24.8 us -> 11.5 us  [the longest x1 8.34 us: shards(): lax.all_to_all(ids_sent.reshape(owners, 1, 128), 'shard', 0, 0, tiled=True)]
    ppermute x1, starting transfers between devices: 8.34 us -> 3.57 us  [shards(): other = lax.ppermute(mine, 'blk', swap)]
    unnamed x18 -> x16, local copies, waits for them, and re-layouts: 4.59 us -> 2.37 us
    pallas_call x6 -> x8, Pallas kernels: 10.4 us -> 12.3 us  [the longest x4 7.05 us: step(): call(kernel, out_shape, 2 * pairs * width, moved, pairs, specs, scratch, 48)]
  transfers between devices with their start and end apart: 5 -> 10, of which waited for: 2 -> 5; matrix products, arithmetic and copies ran while one was open for 5% -> 4% of each run, Pallas kernels for 7% -> 6%
where the time goes in v2:
time: 105 us
  starting transfers between devices  72 us (69%)
  waiting for transfers between devices  12.6 us (12%)
  Pallas kernels  12.3 us (12%)
  local copies, waits for them, and re-layouts  3.14 us (3%)
  matrix products  2.9 us (3%)
    all_to_all x1, starting transfers between devices, shards(): lax.all_to_all(ids_sent.reshape(owners, 1, 128), 'shard', 0, 0, tiled=True)  25.3 us
    ppermute x4, starting transfers between devices, turn(): return lax.ppermute(array, 'blk', pairs)  16.6 us
    ppermute x1, starting transfers between devices, shards(): other_biases = lax.ppermute(biases, 'blk', swap)  15.3 us
    all_to_all x1, waiting for transfers between devices, shards(): lax.all_to_all(ids_sent.reshape(owners, 1, 128), 'shard', 0, 0, tiled=True)  8.34 us
    pallas_call x4, Pallas kernels, step(): call(kernel, out_shape, 2 * pairs * width, moved, pairs, specs, scratch, 48)  7.05 us
    all_to_all x1, starting transfers between devices, shards(): received = lax.all_to_all(table_rows, 'shard', 0, 0, tiled=True)  4.63 us
    all_to_all x1, starting transfers between devices, shards(): lax.all_to_all(vecs, 'blk', 0, 0, axis_index_groups=[list(range(c, blocks...  4.23 us
    ppermute x1, starting transfers between devices, shards(): other = lax.ppermute(mine, 'blk', swap)  3.57 us
  transfers between devices with their start and end apart: 10, of which 5 were waited for; matrix products, arithmetic and copies ran while one was open for 4% of the time, Pallas kernels for 6%

profile of v2, /device:TPU:1, one launch (start us, length us, event | category | flops | bytes accessed | tf_op | source)
XLA Modules:
  0.0 104.6 jit_solution(17042169099934698173)
XLA Ops:
  0.6 0.0 copy-start
  0.6 2.1 %shard_map.112 = (s32[64,128]{1,0:T(8,128)}, bf16[128,256]{1,0:T(8,128)(2,1)}, bf16[272,256]{1,0:T(8,128)(2,1)}) custom-call(s32[1,128]{1,0:T(1,128)} %bitcast.36, s32[1,128]{1,0:T(1,128)} %bitcast.37, bf16[256,256]{1,0:T(8,128)(2,1)} %users_ref.1, s32[1,128]{1,0:T(1,128)} %bitcast.38), custom_call_target="tpu_custom_call" | custom-call | flops 8388608 | bytes 32768 | tf_op jit(solution)/shard_map/pallas_call | solution.py:251
  2.7 7.9 %collective-permute-start = (bf16[272,256]{1,0:T(8,128)(2,1)}, bf16[272,256]{1,0:T(8,128)(2,1)}, u32[]{:S(2)}, u32[]{:S(2)}) collective-permute-start(bf16[272,256]{1,0:T(8,128)(2,1)} %get-tuple-element.20), channel_id=1, source_target_pairs={{0,8},{1,9},{2,10},{3,11},{4,12},{5,13},{6,14},{7,15},{8,0},{9,1},... | collective-permute-start | bytes 417800 | tf_op jit(solution)/shard_map/ppermute | solution.py:279
  10.7 25.3 %all-to-all-start = ((s32[64,1,128]{2,1,0:T(1,128)}), s32[64,1,128]{2,1,0:T(1,128)S(1)}, u32[]{:S(2)}, u32[]{:S(2)}) async-start(s32[64,1,128]{2,1,0:T(1,128)} %bitcast.30), calls=%async_computation | async-start | bytes 65536 | tf_op jit(solution)/shard_map/all_to_all | solution.py:266
  36.0 0.0 copy-start.1
  36.0 1.6 %copy-done.1 = bf16[1024,1024]{1,0:T(8,128)(2,1)S(1)} copy-done((bf16[1024,1024]{1,0:T(8,128)(2,1)S(1)}, bf16[1024,1024]{1,0:T(8,128)(2,1)}, u32[]{:S(2)}) %copy-start.1) | copy-done | bytes 2097176
  37.6 0.0 copy-start.3
  37.6 0.8 copy-done.3
  38.4 0.0 copy-start.7
  38.4 0.1 shard_map.113.table_ref
  38.5 8.3 %all-to-all-done = s32[64,1,128]{2,1,0:T(1,128)S(1)} async-done(((s32[64,1,128]{2,1,0:T(1,128)}), s32[64,1,128]{2,1,0:T(1,128)S(1)}, u32[]{:S(2)}, u32[]{:S(2)}) %all-to-all-start) | async-done | bytes 32800 | tf_op jit(solution)/shard_map/all_to_all | solution.py:266
  46.9 0.0 copy-start.2
  46.9 0.0 copy-start.5
  46.9 1.7 %shard_map.114 = bf16[64,4,1024]{2,1,0:T(4,128)(2,1)} custom-call(s32[64,128]{1,0:T(8,128)S(1)} %bitcast.31, bf16[1024,1024]{1,0:T(8,128)(2,1)S(1)} %shard_map.113.table_ref), custom_call_target="tpu_custom_call" | custom-call | flops 536870912 | bytes 2097152 | tf_op jit(solution)/shard_map/pallas_call | solution.py:281
  48.6 0.0 collective-permute-done
  48.6 4.6 %all-to-all-start.1 = ((bf16[64,4,1024]{2,1,0:T(4,128)(2,1)}), bf16[64,4,1024]{2,1,0:T(4,128)(2,1)S(1)}, u32[]{:S(2)}, u32[]{:S(2)}) async-start(bf16[64,4,1024]{2,1,0:T(4,128)(2,1)} %shard_map.114), calls=%async_computation.1 | async-start | bytes 1048576 | tf_op jit(solution)/shard_map/all_to_all | solution.py:289
  53.2 0.0 copy-done.7
  53.2 0.9 pad_maximum_fusion.refs_0_.units_ref
  54.2 2.2 %collective-permute-start.3 = (bf16[2,272,256]{2,1,0:T(8,128)(2,1)S(1)}, bf16[2,272,256]{2,1,0:T(8,128)(2,1)S(1)}, u32[]{:S(2)}, u32[]{:S(2)}) collective-permute-start(bf16[2,272,256]{2,1,0:T(8,128)(2,1)S(1)} %pad_maximum_fusion.refs_0_.units_ref), channel_id=1, source_target_pairs={{0,14},{1,15},{2,0},{3,1},{4,2},{5,3},{6,4},{7,5},{8,6},{9,7},{10,... | collective-permute-start | bytes 835592 | tf_op jit(solution)/shard_map/ppermute | solution.py:279
  56.4 0.0 copy-done
  56.4 2.9 %fusion.2.pre_ref = f32[128,1024]{1,0:T(8,128)S(1)} fusion(bf16[128,2048]{1,0:T(8,128)(2,1)S(1)} %copy-done, bf16[2048,1024]{1,0:T(8,128)(2,1)} %param.15), kind=kOutput, calls=%fused_computation.12 | convolution fusion | flops 536870912 | bytes 5242880 | tf_op jit(solution)/shard_map/dot_general | solution.py:299
  59.3 3.7 %collective-permute-start.2 = (bf16[2,272,256]{2,1,0:T(8,128)(2,1)S(1)}, bf16[2,272,256]{2,1,0:T(8,128)(2,1)S(1)}, u32[]{:S(2)}, u32[]{:S(2)}) collective-permute-start(bf16[2,272,256]{2,1,0:T(8,128)(2,1)S(1)} %pad_maximum_fusion.refs_0_.units_ref), channel_id=1, source_target_pairs={{0,4},{1,13},{2,6},{3,15},{4,8},{5,1},{6,10},{7,3},{8,12},{9,5},{1... | collective-permute-start | bytes 835592 | tf_op jit(solution)/shard_map/ppermute | solution.py:279
  63.0 2.8 %collective-permute-start.1 = (bf16[2,272,256]{2,1,0:T(8,128)(2,1)S(1)}, bf16[2,272,256]{2,1,0:T(8,128)(2,1)S(1)}, u32[]{:S(2)}, u32[]{:S(2)}) collective-permute-start(bf16[2,272,256]{2,1,0:T(8,128)(2,1)S(1)} %pad_maximum_fusion.refs_0_.units_ref), channel_id=1, source_target_pairs={{0,2},{1,3},{2,4},{3,5},{4,6},{5,7},{6,8},{7,9},{8,10},{9,11},{10,... | collective-permute-start | bytes 835592 | tf_op jit(solution)/shard_map/ppermute | solution.py:279
  65.8 3.2 %all-to-all-done.1.rows_ref = bf16[64,4,1024]{2,1,0:T(4,128)(2,1)S(1)} async-done(((bf16[64,4,1024]{2,1,0:T(4,128)(2,1)}), bf16[64,4,1024]{2,1,0:T(4,128)(2,1)S(1)}, u32[]{:S(2)}, u32[]{:S(2)}) %all-to-all-start.1) | async-done | bytes 524320 | tf_op jit(solution)/shard_map/all_to_all | solution.py:289
  69.0 0.0 copy-done.2
  69.0 0.0 copy-done.5
  69.0 1.3 %shard_map.115 = bf16[8,128,256]{2,1,0:T(8,128)(2,1)} custom-call(f32[128,1024]{1,0:T(8,128)S(1)} %fusion.2.pre_ref, bf16[128,256]{1,0:T(8,128)(2,1)S(1)} %copy-done.5, bf16[64,4,1024]{2,1,0:T(4,128)(2,1)S(1)} %all-to-all-done.1.rows_ref, bf16[1024,256]{1,0:T(8,128)(2,1)S(1)} %copy-done.2), custom_call_target="tpu_custom_call" | custom-call | flops 67108864 | bytes 524288 | tf_op jit(solution)/shard_map/pallas_call | solution.py:300
  70.3 4.2 %all-to-all-start.2 = ((bf16[8,128,256]{2,1,0:T(8,128)(2,1)}), bf16[8,128,256]{2,1,0:T(8,128)(2,1)S(1)}, u32[]{:S(2)}, u32[]{:S(2)}) async-start(bf16[8,128,256]{2,1,0:T(8,128)(2,1)} %shard_map.115), calls=%async_computation.2 | async-start | bytes 1048576 | tf_op jit(solution)/shard_map/all_to_all | solution.py:307
  74.5 0.0 copy-start.4
  74.5 0.0 copy-start.6
  74.6 0.7 slice_bitcast_fusion.2
  75.3 0.0 collective-permute-done.3.refs_2_
  75.3 0.1 collective-permute-done.1.refs_1_
  75.4 0.0 collective-permute-done.2.refs_3_
  75.4 15.3 %collective-permute-start.4 = (f32[8,128]{1,0:T(8,128)S(1)}, f32[8,128]{1,0:T(8,128)S(1)}, u32[]{:S(2)}, u32[]{:S(2)}) collective-permute-start(f32[8,128]{1,0:T(8,128)S(1)} %convert_multiply_fusion.bias_ref), channel_id=1, source_target_pairs={{0,1},{1,0},{2,3},{3,2},{4,5},{5,4},{6,7},{7,6},{8,9},{9,8},{10,11... | collective-permute-start | bytes 12296 | tf_op jit(solution)/shard_map/ppermute | solution.py:297
  90.7 0.8 collective-permute-done.4.bias_ref.other_bias_ref
  91.5 0.0 all-to-all-done.2.vecs_ref.mine_ref
  91.5 3.6 %collective-permute-start.5 = (bf16[8,128,256]{2,1,0:T(8,128)(2,1)S(1)}, bf16[8,128,256]{2,1,0:T(8,128)(2,1)S(1)}, u32[]{:S(2)}, u32[]{:S(2)}) collective-permute-start(bf16[8,128,256]{2,1,0:T(8,128)(2,1)S(1)} %all-to-all-done.2.vecs_ref.mine_ref), channel_id=1, source_target_pairs={{0,1},{1,0},{2,3},{3,2},{4,5},{5,4},{6,7},{7,6},{8,9},{9,8},{10,11... | collective-permute-start | bytes 1572872 | tf_op jit(solution)/shard_map/ppermute | solution.py:316
  95.1 1.4 %shard_map.116.first_ref = f32[8,256]{1,0:T(8,128)S(1)} custom-call(s32[1]{0:T(128)} %bitcast.place_ref, bf16[8,128,256]{2,1,0:T(8,128)(2,1)S(1)} %all-to-all-done.2.vecs_ref.mine_ref, f32[8,128]{1,0:T(8,128)S(1)} %convert_multiply_fusion.bias_ref, bf16[2,272,256]{2,1,0:T(8,128)(2,1)S(1)} %pad_maximum_fusion.refs_0_.units_ref, ...), custom_call_target="tpu_custom_call" | custom-call | flops 1073741824 | bytes 2097152 | tf_op jit(solution)/shard_map/pallas_call | solution.py:322
  96.5 0.1 collective-permute-done.5.vecs_ref.other_ref
  96.6 2.0 %shard_map.117 = (f32[8,256]{1,0:T(8,128)S(1)}, f32[128,256]{1,0:T(8,128)S(1)}) custom-call(s32[1]{0:T(128)} %bitcast.place_ref, bf16[8,128,256]{2,1,0:T(8,128)(2,1)S(1)} %collective-permute-done.5.vecs_ref.other_ref, f32[8,128]{1,0:T(8,128)S(1)} %collective-permute-done.4.bias_ref.other_bias_ref, f32[8,256]{1,0:T(8,128)S(1)} %shard_map.116.first_ref, ...), custom_call_target="tpu_custom_call" | custom-call | flops 1073741824 | bytes 2097152 | tf_op jit(solution)/shard_map/pallas_call | solution.py:322
  98.6 2.3 %collective-permute-start.6 = (f32[128,256]{1,0:T(8,128)S(1)}, f32[128,256]{1,0:T(8,128)S(1)}, u32[]{:S(2)}, u32[]{:S(2)}) collective-permute-start(f32[128,256]{1,0:T(8,128)S(1)} %get-tuple-element.28), channel_id=1, source_target_pairs={{0,1},{1,0},{2,3},{3,2},{4,5},{5,4},{6,7},{7,6},{8,9},{9,8},{10,11... | collective-permute-start | bytes 393224 | tf_op jit(solution)/shard_map/ppermute | solution.py:333
  100.9 0.0 copy-done.4
  100.9 0.0 copy-done.6
  100.9 2.2 %shard_map.118 = (f32[1,256]{1,0:T(1,128)}, f32[256,256]{1,0:T(8,128)}) custom-call(s32[1]{0:T(128)} %bitcast.place_ref, bf16[8,128,256]{2,1,0:T(8,128)(2,1)S(1)} %all-to-all-done.2.vecs_ref.mine_ref, bf16[8,128,256]{2,1,0:T(8,128)(2,1)S(1)} %collective-permute-done.5.vecs_ref.other_ref, f32[8,128]{1,0:T(8,128)S(1)} %convert_multiply_fusion.bias_ref, ...), custom_call_target="tpu_custom_call" | custom-call | flops 1073741824 | bytes 2097152 | tf_op jit(solution)/shard_map/pallas_call | solution.py:322
  103.2 0.0 collective-permute-done.6.taken_ref
  103.2 1.5 %shard_map.119 = f32[128,256]{1,0:T(8,128)} custom-call(s32[1]{0:T(128)} %bitcast.place_ref, bf16[8,128,256]{2,1,0:T(8,128)(2,1)S(1)} %all-to-all-done.2.vecs_ref.mine_ref, f32[8,128]{1,0:T(8,128)S(1)} %convert_multiply_fusion.bias_ref, f32[8,256]{1,0:T(8,128)S(1)} %get-tuple-element.25.sums_ref, s32[1,256]{1,0:T(1,128)S(1)} %bitcast.33, ...), custom_call_target="tpu_custom_call" | custom-call | flops 134217728 | bytes 2097152 | tf_op jit(solution)/shard_map/pallas_call | solution.py:322
  (5 shorter events, 0.1 us)
Async XLA Ops:
  0.6 55.7 %copy-start = (bf16[128,2048]{1,0:T(8,128)(2,1)S(1)}, bf16[128,2048]{1,0:T(8,128)(2,1)}, u32[]{:S(2)}) copy-start(bf16[128,2048]{1,0:T(8,128)(2,1)} %param.9) | copy-start | bytes 1572868
  2.7 45.9 %collective-permute-start = (bf16[272,256]{1,0:T(8,128)(2,1)}, bf16[272,256]{1,0:T(8,128)(2,1)}, u32[]{:S(2)}, u32[]{:S(2)}) collective-permute-start(bf16[272,256]{1,0:T(8,128)(2,1)} %get-tuple-element.20), channel_id=1, source_target_pairs={{0,8},{1,9},{2,10},{3,11},{4,12},{5,13},{6,14},{7,15},{8,0},{9,1},... | collective-permute-start | bytes 417800 | tf_op jit(solution)/shard_map/ppermute | solution.py:279
  10.7 36.2 %all-to-all-start = ((s32[64,1,128]{2,1,0:T(1,128)}), s32[64,1,128]{2,1,0:T(1,128)S(1)}, u32[]{:S(2)}, u32[]{:S(2)}) async-start(s32[64,1,128]{2,1,0:T(1,128)} %bitcast.30), calls=%async_computation | async-start | bytes 65536 | tf_op jit(solution)/shard_map/all_to_all | solution.py:266
  36.0 1.6 %copy-start.1 = (bf16[1024,1024]{1,0:T(8,128)(2,1)S(1)}, bf16[1024,1024]{1,0:T(8,128)(2,1)}, u32[]{:S(2)}) copy-start(bf16[1024,1024]{1,0:T(8,128)(2,1)} %table_in.1) | copy-start | bytes 6291460
  37.6 0.8 copy-start.3
  38.4 14.9 %copy-start.7 = (bf16[272,256]{1,0:T(8,128)(2,1)S(1)}, bf16[272,256]{1,0:T(8,128)(2,1)}, u32[]{:S(2)}) copy-start(bf16[272,256]{1,0:T(8,128)(2,1)} %get-tuple-element.20) | copy-start | bytes 417796
  46.9 22.1 %copy-start.2 = (bf16[1024,256]{1,0:T(8,128)(2,1)S(1)}, bf16[1024,256]{1,0:T(8,128)(2,1)}, u32[]{:S(2)}) copy-start(bf16[1024,256]{1,0:T(8,128)(2,1)} %second_ref.1) | copy-start | bytes 1572868
  46.9 22.1 %copy-start.5 = (bf16[128,256]{1,0:T(8,128)(2,1)S(1)}, bf16[128,256]{1,0:T(8,128)(2,1)}, u32[]{:S(2)}) copy-start(bf16[128,256]{1,0:T(8,128)(2,1)} %get-tuple-element.16.placing_ref) | copy-start | bytes 196612
  48.6 20.4 %all-to-all-start.1 = ((bf16[64,4,1024]{2,1,0:T(4,128)(2,1)}), bf16[64,4,1024]{2,1,0:T(4,128)(2,1)S(1)}, u32[]{:S(2)}, u32[]{:S(2)}) async-start(bf16[64,4,1024]{2,1,0:T(4,128)(2,1)} %shard_map.114), calls=%async_computation.1 | async-start | bytes 1048576 | tf_op jit(solution)/shard_map/all_to_all | solution.py:289
  54.2 21.1 %collective-permute-start.3 = (bf16[2,272,256]{2,1,0:T(8,128)(2,1)S(1)}, bf16[2,272,256]{2,1,0:T(8,128)(2,1)S(1)}, u32[]{:S(2)}, u32[]{:S(2)}) collective-permute-start(bf16[2,272,256]{2,1,0:T(8,128)(2,1)S(1)} %pad_maximum_fusion.refs_0_.units_ref), channel_id=1, source_target_pairs={{0,14},{1,15},{2,0},{3,1},{4,2},{5,3},{6,4},{7,5},{8,6},{9,7},{10,... | collective-permute-start | bytes 835592 | tf_op jit(solution)/shard_map/ppermute | solution.py:279
  59.3 16.1 %collective-permute-start.2 = (bf16[2,272,256]{2,1,0:T(8,128)(2,1)S(1)}, bf16[2,272,256]{2,1,0:T(8,128)(2,1)S(1)}, u32[]{:S(2)}, u32[]{:S(2)}) collective-permute-start(bf16[2,272,256]{2,1,0:T(8,128)(2,1)S(1)} %pad_maximum_fusion.refs_0_.units_ref), channel_id=1, source_target_pairs={{0,4},{1,13},{2,6},{3,15},{4,8},{5,1},{6,10},{7,3},{8,12},{9,5},{1... | collective-permute-start | bytes 835592 | tf_op jit(solution)/shard_map/ppermute | solution.py:279
  63.0 12.4 %collective-permute-start.1 = (bf16[2,272,256]{2,1,0:T(8,128)(2,1)S(1)}, bf16[2,272,256]{2,1,0:T(8,128)(2,1)S(1)}, u32[]{:S(2)}, u32[]{:S(2)}) collective-permute-start(bf16[2,272,256]{2,1,0:T(8,128)(2,1)S(1)} %pad_maximum_fusion.refs_0_.units_ref), channel_id=1, source_target_pairs={{0,2},{1,3},{2,4},{3,5},{4,6},{5,7},{6,8},{7,9},{8,10},{9,11},{10,... | collective-permute-start | bytes 835592 | tf_op jit(solution)/shard_map/ppermute | solution.py:279
  70.3 21.2 %all-to-all-start.2 = ((bf16[8,128,256]{2,1,0:T(8,128)(2,1)}), bf16[8,128,256]{2,1,0:T(8,128)(2,1)S(1)}, u32[]{:S(2)}, u32[]{:S(2)}) async-start(bf16[8,128,256]{2,1,0:T(8,128)(2,1)} %shard_map.115), calls=%async_computation.2 | async-start | bytes 1048576 | tf_op jit(solution)/shard_map/all_to_all | solution.py:307
  74.5 26.4 %copy-start.4 = (bf16[256,256]{1,0:T(8,128)(2,1)S(1)}, bf16[256,256]{1,0:T(8,128)(2,1)}, u32[]{:S(2)}) copy-start(bf16[256,256]{1,0:T(8,128)(2,1)} %users_ref.1) | copy-start | bytes 393220
  74.5 26.4 %copy-start.6 = (s32[256]{0:T(256)S(1)}, s32[256]{0:T(256)}, u32[]{:S(2)}) copy-start(s32[256]{0:T(256)} %param.13) | copy-start | bytes 3076
  75.4 16.1 %collective-permute-start.4 = (f32[8,128]{1,0:T(8,128)S(1)}, f32[8,128]{1,0:T(8,128)S(1)}, u32[]{:S(2)}, u32[]{:S(2)}) collective-permute-start(f32[8,128]{1,0:T(8,128)S(1)} %convert_multiply_fusion.bias_ref), channel_id=1, source_target_pairs={{0,1},{1,0},{2,3},{3,2},{4,5},{5,4},{6,7},{7,6},{8,9},{9,8},{10,11... | collective-permute-start | bytes 12296 | tf_op jit(solution)/shard_map/ppermute | solution.py:297
  91.5 5.1 %collective-permute-start.5 = (bf16[8,128,256]{2,1,0:T(8,128)(2,1)S(1)}, bf16[8,128,256]{2,1,0:T(8,128)(2,1)S(1)}, u32[]{:S(2)}, u32[]{:S(2)}) collective-permute-start(bf16[8,128,256]{2,1,0:T(8,128)(2,1)S(1)} %all-to-all-done.2.vecs_ref.mine_ref), channel_id=1, source_target_pairs={{0,1},{1,0},{2,3},{3,2},{4,5},{5,4},{6,7},{7,6},{8,9},{9,8},{10,11... | collective-permute-start | bytes 1572872 | tf_op jit(solution)/shard_map/ppermute | solution.py:316
  98.6 4.6 %collective-permute-start.6 = (f32[128,256]{1,0:T(8,128)S(1)}, f32[128,256]{1,0:T(8,128)S(1)}, u32[]{:S(2)}, u32[]{:S(2)}) collective-permute-start(f32[128,256]{1,0:T(8,128)S(1)} %get-tuple-element.28), channel_id=1, source_target_pairs={{0,1},{1,0},{2,3},{3,2},{4,5},{5,4},{6,7},{7,6},{8,9},{9,8},{10,11... | collective-permute-start | bytes 393224 | tf_op jit(solution)/shard_map/ppermute | solution.py:333

commit v3 on v2

v3 whole, which is shorter than its diff:
```python
import functools

import jax
import jax.numpy as jnp
from jax import lax
from jax.experimental import pallas as pl
from jax.experimental.pallas import tpu as pltpu
from jax.sharding import PartitionSpec as P

logit_scale = 48.0
log2_e = 1.4426950408889634
exponent_scale = logit_scale * log2_e
vmem = pl.BlockSpec(memory_space=pltpu.VMEM)
far_memory = pl.BlockSpec(memory_space=pltpu.HBM)
f32, bf16 = jnp.float32, jnp.bfloat16


def call(kernel, out_shape, flops, moved, exps=0, in_specs=None, scratch=(), room=16):
    options = {} if in_specs is None else {"in_specs": in_specs}
    return pl.pallas_call(
        kernel,
        out_shape=out_shape,
        out_specs=[vmem] * len(out_shape) if isinstance(out_shape, tuple) else vmem,
        scratch_shapes=scratch,
        compiler_params=pltpu.CompilerParams(vmem_limit_bytes=room * 2**20),
        cost_estimate=pl.CostEstimate(flops=flops, bytes_accessed=moved, transcendentals=exps),
        **options,
    )


def dot(a, b, contract=((1,), (0,))):
    return lax.dot_general(a, b, (contract, ((), ())), preferred_element_type=f32)


def iota(shape, dim):
    return lax.broadcasted_iota(jnp.int32, shape, dim)


def place_kernel(
    owners,
    capacity,
    owner_in,
    id_in,
    users_in,
    ids_ref,
    placing_ref,
    payload_ref,
    owner_ref,
    id_ref,
    users_ref,
    sems,
):
    pairs = (owner_in, owner_ref), (id_in, id_ref), (users_in, users_ref)
    copies = [pltpu.make_async_copy(*pair, sems.at[i]) for i, pair in enumerate(pairs)]
    for copy in copies:
        copy.start()
    for copy in copies:
        copy.wait()
    n = owner_ref.shape[1]
    eye = iota((n, n), 0) == iota((n, n), 1)
    owner = jnp.sum(jnp.where(eye, owner_ref[...], 0).astype(f32), 1, keepdims=True)
    ids = jnp.sum(jnp.where(eye, id_ref[...], 0).astype(f32), 1, keepdims=True)
    hot = jnp.where(owner == iota((n, owners), 1).astype(f32), 1.0, 0.0)
    earlier = jnp.where(iota((n, n), 0) > iota((n, n), 1), 1.0, 0.0).astype(bf16)
    before = dot(earlier, hot.astype(bf16))
    rank = jnp.sum(before * hot, 1, keepdims=True)
    high = jnp.floor(ids * (1.0 / 32.0))
    low = ids - 32.0 * high
    lane = iota((n, 128), 1).astype(f32)
    parts = jnp.where(lane == rank, high, 0.0) + jnp.where(lane == rank + capacity, low, 0.0)
    ids_ref[...] = dot(hot.astype(bf16), parts.astype(bf16), ((0,), (0,))).astype(jnp.int32)
    position = owner * capacity + rank
    placing_ref[...] = jnp.where(
        position == iota((n, owners * capacity), 1).astype(f32), 1.0, 0.0
    ).astype(bf16)
    user_f = users_ref[...].astype(f32)
    inverse = lax.rsqrt(jnp.sum(user_f * user_f, -1, keepdims=True) + 1e-06)
    payload_ref[...] = (user_f * inverse).astype(bf16)


def table_kernel(table_in, table_ref, sem):
    copy = pltpu.make_async_copy(table_in, table_ref, sem)
    copy.start()
    copy.wait()


def pair_kernel(near_ref, far_ref, out_ref):
    out_ref[0] = near_ref[...]
    out_ref[1] = far_ref[...]


def ready_kernel(one_ref, two_ref, three_ref, out_ref):
    out_ref[...] = jnp.zeros_like(out_ref)


def rows_kernel(capacity, ids_ref, table_ref, out_ref):
    peers = ids_ref.shape[0]
    slots = peers * capacity
    peer_of = iota((slots, peers), 0) // capacity
    spread = jnp.where(peer_of == iota((slots, peers), 1), 1.0, 0.0).astype(bf16)
    parts = dot(spread, ids_ref[...].astype(bf16))
    lane, slot = iota((slots, 128), 1), iota((slots, 128), 0) % capacity
    weight = jnp.where(lane == slot, 32.0, 0.0) + jnp.where(lane == slot + capacity, 1.0, 0.0)
    ids = jnp.sum(parts * weight, 1, keepdims=True)
    hot = jnp.where(ids == iota((slots, table_ref.shape[0]), 1).astype(f32), 1.0, 0.0).astype(bf16)
    out_ref[...] = dot(hot, table_ref[...]).astype(bf16).reshape(out_ref.shape)


def encode_kernel(pre_ref, placing_ref, rows_ref, second_ref, counts_ref, out_ref):
    rows = dot(placing_ref[...], rows_ref[...].reshape(placing_ref.shape[1], -1))
    hidden = jnp.maximum(pre_ref[...] + rows, 0.0).astype(bf16)
    emb = dot(hidden, second_ref[...])
    square = jnp.sum(emb * emb, -1, keepdims=True)
    vecs = (emb * lax.rsqrt(square + 1e-06)).astype(bf16)
    n, width = vecs.shape
    bias = jnp.broadcast_to(jnp.log(counts_ref[...].astype(f32)), (16, n))
    bias = jnp.concatenate([bias] * (width // n), 1).astype(bf16)
    for i in range(out_ref.shape[0]):
        out_ref[i, :n, :] = vecs
        out_ref[i, n:, :] = bias


def bias_row(ref, i, n):
    return ref[i, n : n + 16, :n].astype(f32)[0:1, :] * log2_e


def column(row):
    n = row.shape[1]
    return jnp.sum(jnp.where(iota((n, n), 0) == iota((n, n), 1), row, 0.0), 1, keepdims=True)


def sums(vecs_ref, unit_refs, store):
    peers, width = vecs_ref.shape[0], vecs_ref.shape[2]
    n, rows = vecs_ref.shape[1] - 16, unit_refs[0].shape[1]
    biases = [jnp.broadcast_to(column(bias_row(vecs_ref, i, n)), (n, 128)) for i in range(peers)]
    for t in range(0, 2 * len(unit_refs), 2):
        units = unit_refs[t // 2][...].reshape(2 * rows, width)
        total = jnp.zeros((8, 2 * rows), f32)
        for i in range(0, peers, 2):
            vecs = vecs_ref[i : i + 2, :n, :].reshape(2 * n, width)
            logits = dot(vecs, units, ((1,), (1,)))
            bias = jnp.concatenate([jnp.concatenate(biases[i : i + 2])] * (2 * rows // 128), 1)
            exponent = jnp.exp2(logits * exponent_scale - bias)
            total = total + jnp.sum(exponent.reshape(-1, 8, 2 * rows), 0)
        total = jnp.sum(total, 0, keepdims=True)
        store(t, total[:, :rows])
        store(t + 1, total[:, rows:])


def first_kernel(vecs_ref, ready_ref, *refs):
    out_ref = refs[-1]

    def store(t, value):
        out_ref[t : t + 1, :] = value

    sums(vecs_ref, refs[:-1], store)


def item_sum(place, vecs_ref, units, sums_ref, hot):
    n, width = vecs_ref.shape[1] - 16, vecs_ref.shape[2]
    vecs = vecs_ref[place, :n, :]
    bias = jnp.broadcast_to(column(bias_row(vecs_ref, place, n)), (n, 128))
    grad = jnp.zeros((n, width), f32)
    rows = units[0].shape[1]
    for t in range(2 * len(units)):
        unit = units[t // 2][t % 2]
        exponent = jnp.exp2(
            dot(vecs, unit, ((1,), (1,))) * exponent_scale
            - jnp.concatenate([bias] * (rows // 128), 1)
        )
        residue = exponent * (1.0 / sums_ref[t : t + 1, :])
        if t == 0 and hot is not None:
            residue = residue - hot
        grad += dot(residue.astype(bf16), unit)
    return logit_scale * grad


def second_kernel(place_ref, vecs_ref, first_ref, *refs):
    units, sums_ref, grad_ref = refs[:-2], refs[-2], refs[-1]

    def store(t, value):
        sums_ref[t : t + 1, :] = first_ref[t : t + 1, :] + value

    sums(vecs_ref, units, store)
    grad_ref[...] = item_sum(place_ref[0], vecs_ref, units, sums_ref, None)


def user_kernel(
    place_ref,
    mine_ref,
    other_ref,
    sums_ref,
    users_ref,
    occurrence_ref,
    units_ref,
    loss_ref,
    grad_ref,
    exps,
):
    peers, width = mine_ref.shape[0], mine_ref.shape[2]
    n, rows = mine_ref.shape[1] - 16, users_ref.shape[0]
    place = place_ref[0]
    unit_b = units_ref[0]
    denominator = column(sums_ref[0:1, :])
    inverse = 1.0 / denominator
    occurrence = column(occurrence_ref[...].astype(f32))
    hot = jnp.where(occurrence == iota((rows, n), 1).astype(f32), 1.0, 0.0)
    direction = jnp.zeros((rows, width), f32)
    for half, ref in enumerate((mine_ref, other_ref)):
        for i in range(peers):
            logits = dot(unit_b, ref[i, :n, :], ((1,), (1,))) * exponent_scale
            logits = logits - bias_row(ref, i, n)
            exps[:, i * n : (i + 1) * n] = jnp.exp2(logits) * inverse
        if half == 0:
            own = pl.ds(pl.multiple_of(place * n, n), n)
            exps[:, own] = exps[:, own] - hot
        direction += dot(exps[...].astype(bf16), ref[:, :n, :].reshape(peers * n, width))
    own_logits = dot(unit_b, mine_ref[place, :n, :], ((1,), (1,))) * exponent_scale
    own_logits = own_logits - bias_row(mine_ref, place, n)
    picked = jnp.sum(own_logits * hot, 1, keepdims=True) * (1.0 / log2_e)
    loss = jnp.log(denominator) - picked
    eye = iota((rows, rows), 0) == iota((rows, rows), 1)
    loss_ref[...] = jnp.sum(jnp.where(eye, loss, 0.0), 0, keepdims=True)
    direction = logit_scale * direction
    user_f = users_ref[...].astype(f32)
    scale = lax.rsqrt(jnp.sum(user_f * user_f, -1, keepdims=True) + 1e-06)
    unit = user_f * scale
    grad_ref[...] = scale * (direction - jnp.sum(direction * unit, -1, keepdims=True) * unit)


def item_kernel(place_ref, mine_ref, sums_ref, occurrence_ref, taken_ref, *refs):
    units, out_ref = refs[:-1], refs[-1]
    n, rows = mine_ref.shape[1] - 16, occurrence_ref.shape[1]
    hot = jnp.where(occurrence_ref[...] == iota((n, rows), 0), 1.0, 0.0)
    grad = item_sum(place_ref[0], mine_ref, units, sums_ref, hot)
    out_ref[...] = grad + taken_ref[...]


def shards(item_feats, owner, id_row, counts, occurrence, users, w_first, w_second, id_table):
    n, width = item_feats.shape[0], users.shape[1]
    rows = users.shape[0]
    owners, blocks = lax.axis_size("shard"), lax.axis_size("blk")
    capacity = 2 * n // owners
    slots = owners * capacity
    peers = blocks // 2
    block = lax.axis_index("blk")
    place = block // 2
    swap = [(i, i ^ 1) for i in range(blocks)]

    shape = jax.ShapeDtypeStruct
    long = 10**11
    place_sizes = (
        shape((owners, 128), jnp.int32),
        shape((n, slots), bf16),
        shape((rows, width), bf16),
    )
    ids_sent, placing, payload = call(
        functools.partial(place_kernel, owners, capacity),
        place_sizes,
        8 * n * n * owners,
        4 * owners * 128,
        in_specs=[far_memory] * 3,
        scratch=[
            pltpu.VMEM((1, n), jnp.int32),
            pltpu.VMEM((1, n), jnp.int32),
            pltpu.VMEM((rows, width), bf16),
            pltpu.SemaphoreType.DMA((3,)),
        ],
        room=60,
    )(owner.reshape(1, n), id_row.reshape(1, n), users)
    ids = lax.all_to_all(ids_sent.reshape(owners, 1, 128), "shard", 0, 0, tiled=True)
    table = call(
        table_kernel,
        shape(id_table.shape, bf16),
        long // 20,
        4 * id_table.size,
        in_specs=[far_memory],
        scratch=[pltpu.SemaphoreType.DMA],
    )(id_table)

    def turn(array, step, other_step=None):
        steps = (step, step if other_step is None else other_step)
        pairs = [(i, (i + 2 * steps[i % 2]) % blocks) for i in range(blocks)]
        return lax.ppermute(array, "blk", pairs)

    table_rows = call(
        functools.partial(rows_kernel, capacity),
        shape((owners, capacity, id_table.shape[1]), bf16),
        2 * slots * id_table.size,
        2 * id_table.size,
    )(ids.reshape(owners, 128), table)
    far = turn(payload, peers // 2)
    table_rows, feats = lax.optimization_barrier((table_rows, item_feats))
    pre = jnp.dot(feats, w_first, preferred_element_type=f32)
    received = lax.all_to_all(table_rows, "shard", 0, 0, tiled=True)
    pair = call(pair_kernel, shape((2, rows, width), bf16), long, 4 * rows * width)(payload, far)
    units = [pair, turn(pair, 1), turn(pair, -1), turn(pair, 2, -2)]
    vecs = call(
        encode_kernel,
        shape((peers, n + 16, width), bf16),
        2 * n * slots * w_first.shape[1],
        2 * received.size,
    )(pre, placing, received, w_second, counts.reshape(1, n))

    mine = lax.all_to_all(
        vecs,
        "blk",
        0,
        0,
        axis_index_groups=[list(range(c, blocks, 2)) for c in range(2)],
        tiled=True,
    )
    ready = call(
        ready_kernel, shape((8, 128), f32), long, 1024, in_specs=[pl.BlockSpec(memory_space=pl.ANY)] * 3
    )(*units[1:])
    mine, ready = lax.optimization_barrier((mine, ready))
    other = lax.ppermute(mine, "blk", swap)
    smem = pl.BlockSpec(memory_space=pltpu.SMEM)

    def step(kernel, out_shape, pairs, inputs, scratch=()):
        specs = [smem if i is at else vmem for i in inputs]
        moved = peers * rows * width * 4
        return call(kernel, out_shape, 2 * pairs * width, moved, pairs, specs, scratch, 48)(*inputs)

    at, occurrence = place[None], occurrence.reshape(1, rows)
    pairs = peers * rows * peers * n
    first = step(first_kernel, shape((peers, rows), f32), pairs, (mine, ready, *units))
    total, given = step(
        second_kernel,
        (shape((peers, rows), f32), shape((n, width), f32)),
        pairs,
        (at, other, first, *units),
    )
    taken = lax.ppermute(given, "blk", swap)
    loss, user_grad = step(
        user_kernel,
        (shape((1, rows), f32), shape((rows, width), f32)),
        pairs,
        (at, mine, other, total, users, occurrence, pair),
        [pltpu.VMEM((rows, peers * n), f32)],
    )
    item_grad = step(
        item_kernel,
        shape((n, width), f32),
        peers * rows * n,
        (at, mine, total, occurrence, taken, *units),
    )
    return (loss.reshape(rows), user_grad, item_grad)


def solution(mesh):
    return jax.shard_map(
        shards,
        mesh=mesh,
        in_specs=(
            P(("shard", "blk"), None),
            P(("shard", "blk"), None),
            P(("shard", "blk")),
            P(("shard", "blk")),
            P(("shard", "blk")),
            P(("shard", "blk"), None),
            P(),
            P(),
            P("shard", None),
        ),
        out_specs=(P(("shard", "blk")), P(("shard", "blk"), None), P(("shard", "blk"), None)),
        check_vma=False,
    )
```

time: 105 us -> 102 us (0.971)
  waiting for transfers between devices: 12.6 us -> 20.7 us
  starting transfers between devices: 72 us -> 65.1 us
  matrix products: 2.9 us -> 0.74 us
  local copies, waits for them, and re-layouts: 3.14 us -> 1.64 us
    ppermute x1 -> x0, starting transfers between devices: 15.3 us -> none  [shards(): other_biases = lax.ppermute(biases, 'blk', swap)]
    all_to_all x1, waiting for transfers between devices: 0.01 us -> 12.2 us  [shards(): lax.all_to_all(vecs, 'blk', 0, 0, axis_index_groups=[list(range(c, blocks...]
    all_to_all x1, waiting for transfers between devices: 8.34 us -> 1.95 us  [shards(): lax.all_to_all(ids_sent.reshape(owners, 1, 128), 'shard', 0, 0, tiled=True)]
    ppermute x1, starting transfers between devices: 3.57 us -> 9.35 us  [shards(): other = lax.ppermute(mine, 'blk', swap)]
    all_to_all x1, starting transfers between devices: 4.63 us -> 10.2 us  [shards(): received = lax.all_to_all(table_rows, 'shard', 0, 0, tiled=True)]
    all_to_all x1, waiting for transfers between devices: 3.18 us -> 6.24 us  [shards(): received = lax.all_to_all(table_rows, 'shard', 0, 0, tiled=True)]
    dot_general x1, matrix products: 2.9 us -> 0.74 us  [shards(): pre = jnp.dot(feats, w_first, preferred_element_type=f32)]
    all_to_all x1, starting transfers between devices: 25.3 us -> 24 us  [shards(): lax.all_to_all(ids_sent.reshape(owners, 1, 128), 'shard', 0, 0, tiled=True)]
  transfers between devices with their start and end apart: 10 -> 9, of which waited for: 5 -> 4; matrix products, arithmetic and copies ran while one was open for 4% -> 1% of each run, Pallas kernels for 6% -> 7%
where the time goes in v3:
time: 102 us; the launch traced here: 101 us
  starting transfers between devices  65.1 us (64%)
  waiting for transfers between devices  20.7 us (20%)
  Pallas kernels  12.4 us (12%)
  local copies, waits for them, and re-layouts  1.64 us (2%)
    all_to_all x1, starting transfers between devices, shards(): lax.all_to_all(ids_sent.reshape(owners, 1, 128), 'shard', 0, 0, tiled=True)  24 us
    ppermute x4, starting transfers between devices, turn(): return lax.ppermute(array, 'blk', pairs)  15.8 us
    all_to_all x1, waiting for transfers between devices, shards(): lax.all_to_all(vecs, 'blk', 0, 0, axis_index_groups=[list(range(c, blocks...  12.2 us
    all_to_all x1, starting transfers between devices, shards(): received = lax.all_to_all(table_rows, 'shard', 0, 0, tiled=True)  10.2 us
    ppermute x1, starting transfers between devices, shards(): other = lax.ppermute(mine, 'blk', swap)  9.35 us
    pallas_call x4, Pallas kernels, step(): call(kernel, out_shape, 2 * pairs * width, moved, pairs, specs, scratch, 48)  7.09 us
    all_to_all x1, waiting for transfers between devices, shards(): received = lax.all_to_all(table_rows, 'shard', 0, 0, tiled=True)  6.24 us
    all_to_all x1, starting transfers between devices, shards(): lax.all_to_all(vecs, 'blk', 0, 0, axis_index_groups=[list(range(c, blocks...  3.54 us
  transfers between devices with their start and end apart: 9, of which 4 were waited for; matrix products, arithmetic and copies ran while one was open for 1% of the time, Pallas kernels for 7%

profile of v3, /device:TPU:1, one launch (start us, length us, event | category | flops | bytes accessed | tf_op | source)
XLA Modules:
  0.0 101.5 jit_solution(659686193988433769)
XLA Ops:
  0.6 0.0 copy-start
  0.6 2.1 %shard_map.112 = (s32[64,128]{1,0:T(8,128)}, bf16[128,256]{1,0:T(8,128)(2,1)}, bf16[256,256]{1,0:T(8,128)(2,1)}) custom-call(s32[1,128]{1,0:T(1,128)} %bitcast.17, s32[1,128]{1,0:T(1,128)} %bitcast.18, bf16[256,256]{1,0:T(8,128)(2,1)} %users_ref.1), custom_call_target="tpu_custom_call" | custom-call | flops 8388608 | bytes 32768 | tf_op jit(solution)/shard_map/pallas_call | solution.py:257
  2.7 24.0 %all-to-all-start = ((s32[64,1,128]{2,1,0:T(1,128)}), s32[64,1,128]{2,1,0:T(1,128)S(1)}, u32[]{:S(2)}, u32[]{:S(2)}) async-start(s32[64,1,128]{2,1,0:T(1,128)} %bitcast.16), calls=%async_computation | async-start | bytes 65536 | tf_op jit(solution)/shard_map/all_to_all | solution.py:271
  26.7 7.1 %collective-permute-start = (bf16[256,256]{1,0:T(8,128)(2,1)}, bf16[256,256]{1,0:T(8,128)(2,1)S(1)}, u32[]{:S(2)}, u32[]{:S(2)}) collective-permute-start(bf16[256,256]{1,0:T(8,128)(2,1)} %get-tuple-element.18.near_ref), channel_id=1, source_target_pairs={{0,8},{1,9},{2,10},{3,11},{4,12},{5,13},{6,14},{7,15},{8,0},{9,1},... | collective-permute-start | bytes 393224 | tf_op jit(solution)/shard_map/ppermute | solution.py:284
  33.8 0.0 copy-start.6
  33.8 1.6 %copy-done.6 = bf16[1024,1024]{1,0:T(8,128)(2,1)S(1)} copy-done((bf16[1024,1024]{1,0:T(8,128)(2,1)S(1)}, bf16[1024,1024]{1,0:T(8,128)(2,1)}, u32[]{:S(2)}) %copy-start.6) | copy-done | bytes 2097176
  35.4 0.0 copy-start.7
  35.4 0.1 shard_map.113.table_ref
  35.6 1.9 %all-to-all-done = s32[64,1,128]{2,1,0:T(1,128)S(1)} async-done(((s32[64,1,128]{2,1,0:T(1,128)}), s32[64,1,128]{2,1,0:T(1,128)S(1)}, u32[]{:S(2)}, u32[]{:S(2)}) %all-to-all-start) | async-done | bytes 32800 | tf_op jit(solution)/shard_map/all_to_all | solution.py:271
  37.5 1.7 %shard_map.114 = bf16[64,4,1024]{2,1,0:T(4,128)(2,1)} custom-call(s32[64,128]{1,0:T(8,128)S(1)} %bitcast.12, bf16[1024,1024]{1,0:T(8,128)(2,1)S(1)} %shard_map.113.table_ref), custom_call_target="tpu_custom_call" | custom-call | flops 536870912 | bytes 2097152 | tf_op jit(solution)/shard_map/pallas_call | solution.py:286
  39.2 10.2 %all-to-all-start.1 = ((bf16[64,4,1024]{2,1,0:T(4,128)(2,1)}), bf16[64,4,1024]{2,1,0:T(4,128)(2,1)S(1)}, u32[]{:S(2)}, u32[]{:S(2)}) async-start(bf16[64,4,1024]{2,1,0:T(4,128)(2,1)} %shard_map.114), calls=%async_computation.1 | async-start | bytes 1048576 | tf_op jit(solution)/shard_map/all_to_all | solution.py:295
  49.4 0.0 copy-start.8
  49.4 0.0 collective-permute-done.far_ref
  49.5 0.0 copy-done.7
  49.5 0.0 copy-start.1
  49.5 0.0 copy-start.3
  49.5 0.0 copy-start.5
  49.5 2.5 %collective-permute-start.1 = (bf16[2,256,256]{2,1,0:T(8,128)(2,1)S(1)}, bf16[2,256,256]{2,1,0:T(8,128)(2,1)S(1)}, u32[]{:S(2)}, u32[]{:S(2)}) collective-permute-start(bf16[2,256,256]{2,1,0:T(8,128)(2,1)S(1)} %shard_map.116.refs_0_.units_ref), channel_id=1, source_target_pairs={{0,2},{1,3},{2,4},{3,5},{4,6},{5,7},{6,8},{7,9},{8,10},{9,11},{10,... | collective-permute-start | bytes 786440 | tf_op jit(solution)/shard_map/ppermute | solution.py:284
  52.0 4.3 %collective-permute-start.2 = (bf16[2,256,256]{2,1,0:T(8,128)(2,1)S(1)}, bf16[2,256,256]{2,1,0:T(8,128)(2,1)S(1)}, u32[]{:S(2)}, u32[]{:S(2)}) collective-permute-start(bf16[2,256,256]{2,1,0:T(8,128)(2,1)S(1)} %shard_map.116.refs_0_.units_ref), channel_id=1, source_target_pairs={{0,14},{1,15},{2,0},{3,1},{4,2},{5,3},{6,4},{7,5},{8,6},{9,7},{10,... | collective-permute-start | bytes 786440 | tf_op jit(solution)/shard_map/ppermute | solution.py:284
  56.3 1.9 %collective-permute-start.3 = (bf16[2,256,256]{2,1,0:T(8,128)(2,1)S(1)}, bf16[2,256,256]{2,1,0:T(8,128)(2,1)S(1)}, u32[]{:S(2)}, u32[]{:S(2)}) collective-permute-start(bf16[2,256,256]{2,1,0:T(8,128)(2,1)S(1)} %shard_map.116.refs_0_.units_ref), channel_id=1, source_target_pairs={{0,4},{1,13},{2,6},{3,15},{4,8},{5,1},{6,10},{7,3},{8,12},{9,5},{1... | collective-permute-start | bytes 786440 | tf_op jit(solution)/shard_map/ppermute | solution.py:284
  58.2 0.0 copy-done
  58.2 0.0 copy-done.8
  58.2 0.7 fusion.pre_ref
  59.0 6.2 %all-to-all-done.1.rows_ref = bf16[64,4,1024]{2,1,0:T(4,128)(2,1)S(1)} async-done(((bf16[64,4,1024]{2,1,0:T(4,128)(2,1)}), bf16[64,4,1024]{2,1,0:T(4,128)(2,1)S(1)}, u32[]{:S(2)}, u32[]{:S(2)}) %all-to-all-start.1) | async-done | bytes 524320 | tf_op jit(solution)/shard_map/all_to_all | solution.py:295
  65.2 0.0 copy-done.1
  65.2 0.0 copy-done.3
  65.2 0.0 copy-done.5
  65.2 1.3 %shard_map.115 = bf16[8,144,256]{2,1,0:T(8,128)(2,1)} custom-call(f32[128,1024]{1,0:T(8,128)S(1)} %fusion.pre_ref, bf16[128,256]{1,0:T(8,128)(2,1)S(1)} %copy-done.3, bf16[64,4,1024]{2,1,0:T(4,128)(2,1)S(1)} %all-to-all-done.1.rows_ref, bf16[1024,256]{1,0:T(8,128)(2,1)S(1)} %copy-done.1, s32[1,128]{1,0:T(1,128)S(1)} %bitcast.15), custom_call_target="tpu_custom_call" | custom-call | flops 67108864 | bytes 524288 | tf_op jit(solution)/shard_map/pallas_call | solution.py:298
  66.6 3.5 %all-to-all-start.2 = ((bf16[8,144,256]{2,1,0:T(8,128)(2,1)}), bf16[8,144,256]{2,1,0:T(8,128)(2,1)S(1)}, u32[]{:S(2)}, u32[]{:S(2)}) async-start(bf16[8,144,256]{2,1,0:T(8,128)(2,1)} %shard_map.115), calls=%async_computation.2 | async-start | bytes 1179648 | tf_op jit(solution)/shard_map/all_to_all | solution.py:305
  70.1 0.0 collective-permute-done.1.one_ref.refs_1_
  70.1 0.0 collective-permute-done.2.two_ref.refs_2_
  70.1 0.0 collective-permute-done.3.three_ref.refs_3_
  70.2 0.0 copy-start.2
  70.2 0.0 copy-start.4
  70.2 12.2 %all-to-all-done.2.vecs_ref.mine_ref = bf16[8,144,256]{2,1,0:T(8,128)(2,1)S(1)} async-done(((bf16[8,144,256]{2,1,0:T(8,128)(2,1)}), bf16[8,144,256]{2,1,0:T(8,128)(2,1)S(1)}, u32[]{:S(2)}, u32[]{:S(2)}) %all-to-all-start.2) | async-done | bytes 589856 | tf_op jit(solution)/shard_map/all_to_all | solution.py:305
  82.4 9.3 %collective-permute-start.4 = (bf16[8,144,256]{2,1,0:T(8,128)(2,1)S(1)}, bf16[8,144,256]{2,1,0:T(8,128)(2,1)S(1)}, u32[]{:S(2)}, u32[]{:S(2)}) collective-permute-start(bf16[8,144,256]{2,1,0:T(8,128)(2,1)S(1)} %all-to-all-done.2.vecs_ref.mine_ref), channel_id=1, source_target_pairs={{0,1},{1,0},{2,3},{3,2},{4,5},{5,4},{6,7},{7,6},{8,9},{9,8},{10,11... | collective-permute-start | bytes 1769480 | tf_op jit(solution)/shard_map/ppermute | solution.py:317
  91.8 1.4 %shard_map.118.first_ref = f32[8,256]{1,0:T(8,128)S(1)} custom-call(bf16[8,144,256]{2,1,0:T(8,128)(2,1)S(1)} %all-to-all-done.2.vecs_ref.mine_ref, f32[8,128]{1,0:T(8,128)S(1)} %shard_map.117.ready_ref, bf16[2,256,256]{2,1,0:T(8,128)(2,1)S(1)} %shard_map.116.refs_0_.units_ref, bf16[2,256,256]{2,1,0:T(8,128)(2,1)S(1)} %collective-permute-done.1.one_ref.refs_1_, ...), custom_call_target="tpu_custom_call" | custom-call | flops 1073741824 | bytes 2097152 | tf_op jit(solution)/shard_map/pallas_call | solution.py:323
  93.2 0.2 collective-permute-done.4.vecs_ref.other_ref
  93.4 2.0 %shard_map.119 = (f32[8,256]{1,0:T(8,128)S(1)}, f32[128,256]{1,0:T(8,128)S(1)}) custom-call(s32[1]{0:T(128)} %bitcast.place_ref, bf16[8,144,256]{2,1,0:T(8,128)(2,1)S(1)} %collective-permute-done.4.vecs_ref.other_ref, f32[8,256]{1,0:T(8,128)S(1)} %shard_map.118.first_ref, bf16[2,256,256]{2,1,0:T(8,128)(2,1)S(1)} %shard_map.116.refs_0_.units_ref, ...), custom_call_target="tpu_custom_call" | custom-call | flops 1073741824 | bytes 2097152 | tf_op jit(solution)/shard_map/pallas_call | solution.py:323
  95.4 2.3 %collective-permute-start.5 = (f32[128,256]{1,0:T(8,128)S(1)}, f32[128,256]{1,0:T(8,128)S(1)}, u32[]{:S(2)}, u32[]{:S(2)}) collective-permute-start(f32[128,256]{1,0:T(8,128)S(1)} %get-tuple-element.24), channel_id=1, source_target_pairs={{0,1},{1,0},{2,3},{3,2},{4,5},{5,4},{6,7},{7,6},{8,9},{9,8},{10,11... | collective-permute-start | bytes 393224 | tf_op jit(solution)/shard_map/ppermute | solution.py:334
  97.7 0.0 copy-done.2
  97.7 0.0 copy-done.4
  97.7 2.3 %shard_map.120 = (f32[1,256]{1,0:T(1,128)}, f32[256,256]{1,0:T(8,128)}) custom-call(s32[1]{0:T(128)} %bitcast.place_ref, bf16[8,144,256]{2,1,0:T(8,128)(2,1)S(1)} %all-to-all-done.2.vecs_ref.mine_ref, bf16[8,144,256]{2,1,0:T(8,128)(2,1)S(1)} %collective-permute-done.4.vecs_ref.other_ref, f32[8,256]{1,0:T(8,128)S(1)} %get-tuple-element.21.sums_ref, ...), custom_call_target="tpu_custom_call" | custom-call | flops 1073741824 | bytes 2097152 | tf_op jit(solution)/shard_map/pallas_call | solution.py:323
  100.0 0.0 collective-permute-done.5.taken_ref
  100.0 1.5 %shard_map.121 = f32[128,256]{1,0:T(8,128)} custom-call(s32[1]{0:T(128)} %bitcast.place_ref, bf16[8,144,256]{2,1,0:T(8,128)(2,1)S(1)} %all-to-all-done.2.vecs_ref.mine_ref, f32[8,256]{1,0:T(8,128)S(1)} %get-tuple-element.21.sums_ref, s32[1,256]{1,0:T(1,128)S(1)} %bitcast.14, f32[128,256]{1,0:T(8,128)S(1)} %collective-permute-done.5.taken_ref, ...), custom_call_target="tpu_custom_call" | custom-call | flops 134217728 | bytes 2097152 | tf_op jit(solution)/shard_map/pallas_call | solution.py:323
  (2 shorter events, 0.0 us)
Async XLA Ops:
  0.6 57.6 %copy-start = (bf16[128,2048]{1,0:T(8,128)(2,1)S(1)}, bf16[128,2048]{1,0:T(8,128)(2,1)}, u32[]{:S(2)}) copy-start(bf16[128,2048]{1,0:T(8,128)(2,1)} %param.9) | copy-start | bytes 1572868
  2.7 34.8 %all-to-all-start = ((s32[64,1,128]{2,1,0:T(1,128)}), s32[64,1,128]{2,1,0:T(1,128)S(1)}, u32[]{:S(2)}, u32[]{:S(2)}) async-start(s32[64,1,128]{2,1,0:T(1,128)} %bitcast.16), calls=%async_computation | async-start | bytes 65536 | tf_op jit(solution)/shard_map/all_to_all | solution.py:271
  26.7 22.8 %collective-permute-start = (bf16[256,256]{1,0:T(8,128)(2,1)}, bf16[256,256]{1,0:T(8,128)(2,1)S(1)}, u32[]{:S(2)}, u32[]{:S(2)}) collective-permute-start(bf16[256,256]{1,0:T(8,128)(2,1)} %get-tuple-element.18.near_ref), channel_id=1, source_target_pairs={{0,8},{1,9},{2,10},{3,11},{4,12},{5,13},{6,14},{7,15},{8,0},{9,1},... | collective-permute-start | bytes 393224 | tf_op jit(solution)/shard_map/ppermute | solution.py:284
  33.8 1.6 %copy-start.6 = (bf16[1024,1024]{1,0:T(8,128)(2,1)S(1)}, bf16[1024,1024]{1,0:T(8,128)(2,1)}, u32[]{:S(2)}) copy-start(bf16[1024,1024]{1,0:T(8,128)(2,1)} %table_in.1) | copy-start | bytes 6291460
  35.4 14.0 %copy-start.7 = (bf16[256,256]{1,0:T(8,128)(2,1)S(1)}, bf16[256,256]{1,0:T(8,128)(2,1)}, u32[]{:S(2)}) copy-start(bf16[256,256]{1,0:T(8,128)(2,1)} %get-tuple-element.18.near_ref) | copy-start | bytes 393220
  39.2 26.0 %all-to-all-start.1 = ((bf16[64,4,1024]{2,1,0:T(4,128)(2,1)}), bf16[64,4,1024]{2,1,0:T(4,128)(2,1)S(1)}, u32[]{:S(2)}, u32[]{:S(2)}) async-start(bf16[64,4,1024]{2,1,0:T(4,128)(2,1)} %shard_map.114), calls=%async_computation.1 | async-start | bytes 1048576 | tf_op jit(solution)/shard_map/all_to_all | solution.py:295
  49.4 8.8 %copy-start.8 = (bf16[2048,1024]{1,0:T(8,128)(2,1)S(1)}, bf16[2048,1024]{1,0:T(8,128)(2,1)}, u32[]{:S(2)}) copy-start(bf16[2048,1024]{1,0:T(8,128)(2,1)} %param.15) | copy-start | bytes 12582916
  49.5 15.7 %copy-start.1 = (bf16[1024,256]{1,0:T(8,128)(2,1)S(1)}, bf16[1024,256]{1,0:T(8,128)(2,1)}, u32[]{:S(2)}) copy-start(bf16[1024,256]{1,0:T(8,128)(2,1)} %second_ref.1) | copy-start | bytes 1572868
  49.5 15.7 %copy-start.3 = (bf16[128,256]{1,0:T(8,128)(2,1)S(1)}, bf16[128,256]{1,0:T(8,128)(2,1)}, u32[]{:S(2)}) copy-start(bf16[128,256]{1,0:T(8,128)(2,1)} %get-tuple-element.16.placing_ref) | copy-start | bytes 196612
  49.5 15.7 %copy-start.5 = (s32[128]{0:T(128)S(1)}, s32[128]{0:T(128)}, u32[]{:S(2)}) copy-start(s32[128]{0:T(128)} %param.12) | copy-start | bytes 1540
  49.5 20.6 %collective-permute-start.1 = (bf16[2,256,256]{2,1,0:T(8,128)(2,1)S(1)}, bf16[2,256,256]{2,1,0:T(8,128)(2,1)S(1)}, u32[]{:S(2)}, u32[]{:S(2)}) collective-permute-start(bf16[2,256,256]{2,1,0:T(8,128)(2,1)S(1)} %shard_map.116.refs_0_.units_ref), channel_id=1, source_target_pairs={{0,2},{1,3},{2,4},{3,5},{4,6},{5,7},{6,8},{7,9},{8,10},{9,11},{10,... | collective-permute-start | bytes 786440 | tf_op jit(solution)/shard_map/ppermute | solution.py:284
  52.0 18.1 %collective-permute-start.2 = (bf16[2,256,256]{2,1,0:T(8,128)(2,1)S(1)}, bf16[2,256,256]{2,1,0:T(8,128)(2,1)S(1)}, u32[]{:S(2)}, u32[]{:S(2)}) collective-permute-start(bf16[2,256,256]{2,1,0:T(8,128)(2,1)S(1)} %shard_map.116.refs_0_.units_ref), channel_id=1, source_target_pairs={{0,14},{1,15},{2,0},{3,1},{4,2},{5,3},{6,4},{7,5},{8,6},{9,7},{10,... | collective-permute-start | bytes 786440 | tf_op jit(solution)/shard_map/ppermute | solution.py:284
  56.3 13.8 %collective-permute-start.3 = (bf16[2,256,256]{2,1,0:T(8,128)(2,1)S(1)}, bf16[2,256,256]{2,1,0:T(8,128)(2,1)S(1)}, u32[]{:S(2)}, u32[]{:S(2)}) collective-permute-start(bf16[2,256,256]{2,1,0:T(8,128)(2,1)S(1)} %shard_map.116.refs_0_.units_ref), channel_id=1, source_target_pairs={{0,4},{1,13},{2,6},{3,15},{4,8},{5,1},{6,10},{7,3},{8,12},{9,5},{1... | collective-permute-start | bytes 786440 | tf_op jit(solution)/shard_map/ppermute | solution.py:284
  66.6 15.9 %all-to-all-start.2 = ((bf16[8,144,256]{2,1,0:T(8,128)(2,1)}), bf16[8,144,256]{2,1,0:T(8,128)(2,1)S(1)}, u32[]{:S(2)}, u32[]{:S(2)}) async-start(bf16[8,144,256]{2,1,0:T(8,128)(2,1)} %shard_map.115), calls=%async_computation.2 | async-start | bytes 1179648 | tf_op jit(solution)/shard_map/all_to_all | solution.py:305
  70.2 27.5 %copy-start.2 = (bf16[256,256]{1,0:T(8,128)(2,1)S(1)}, bf16[256,256]{1,0:T(8,128)(2,1)}, u32[]{:S(2)}) copy-start(bf16[256,256]{1,0:T(8,128)(2,1)} %users_ref.1) | copy-start | bytes 393220
  70.2 27.5 %copy-start.4 = (s32[256]{0:T(256)S(1)}, s32[256]{0:T(256)}, u32[]{:S(2)}) copy-start(s32[256]{0:T(256)} %param.13) | copy-start | bytes 3076
  82.4 11.0 %collective-permute-start.4 = (bf16[8,144,256]{2,1,0:T(8,128)(2,1)S(1)}, bf16[8,144,256]{2,1,0:T(8,128)(2,1)S(1)}, u32[]{:S(2)}, u32[]{:S(2)}) collective-permute-start(bf16[8,144,256]{2,1,0:T(8,128)(2,1)S(1)} %all-to-all-done.2.vecs_ref.mine_ref), channel_id=1, source_target_pairs={{0,1},{1,0},{2,3},{3,2},{4,5},{5,4},{6,7},{7,6},{8,9},{9,8},{10,11... | collective-permute-start | bytes 1769480 | tf_op jit(solution)/shard_map/ppermute | solution.py:317
  95.4 4.6 %collective-permute-start.5 = (f32[128,256]{1,0:T(8,128)S(1)}, f32[128,256]{1,0:T(8,128)S(1)}, u32[]{:S(2)}, u32[]{:S(2)}) collective-permute-start(f32[128,256]{1,0:T(8,128)S(1)} %get-tuple-element.24), channel_id=1, source_target_pairs={{0,1},{1,0},{2,3},{3,2},{4,5},{5,4},{6,7},{7,6},{8,9},{9,8},{10,11... | collective-permute-start | bytes 393224 | tf_op jit(solution)/shard_map/ppermute | solution.py:334

commit v4 on v3

--- a/solution.py
+++ b/solution.py
@@ -13,14 +13,17 @@
 vmem = pl.BlockSpec(memory_space=pltpu.VMEM)
 far_memory = pl.BlockSpec(memory_space=pltpu.HBM)
 f32, bf16 = jnp.float32, jnp.bfloat16
-
-
-def call(kernel, out_shape, flops, moved, exps=0, in_specs=None, scratch=(), room=16):
+extra = 8
+
+
+def call(kernel, out_shape, flops, moved, exps=0, in_specs=None, scratch=(), room=16, out_specs=None):
+    if out_specs is None:
+        out_specs = [vmem] * len(out_shape) if isinstance(out_shape, tuple) else vmem
     options = {} if in_specs is None else {"in_specs": in_specs}
     return pl.pallas_call(
         kernel,
         out_shape=out_shape,
-        out_specs=[vmem] * len(out_shape) if isinstance(out_shape, tuple) else vmem,
+        out_specs=out_specs,
         scratch_shapes=scratch,
         compiler_params=pltpu.CompilerParams(vmem_limit_bytes=room * 2**20),
         cost_estimate=pl.CostEstimate(flops=flops, bytes_accessed=moved, transcendentals=exps),
@@ -93,7 +96,7 @@
     out_ref[...] = jnp.zeros_like(out_ref)
 
 
-def rows_kernel(capacity, ids_ref, table_ref, out_ref):
+def rows_kernel(capacity, ids_ref, table_ref, out_ref, rows_ref, sems):
     peers = ids_ref.shape[0]
     slots = peers * capacity
     peer_of = iota((slots, peers), 0) // capacity
@@ -103,25 +106,38 @@
     weight = jnp.where(lane == slot, 32.0, 0.0) + jnp.where(lane == slot + capacity, 1.0, 0.0)
     ids = jnp.sum(parts * weight, 1, keepdims=True)
     hot = jnp.where(ids == iota((slots, table_ref.shape[0]), 1).astype(f32), 1.0, 0.0).astype(bf16)
-    out_ref[...] = dot(hot, table_ref[...]).astype(bf16).reshape(out_ref.shape)
-
-
-def encode_kernel(pre_ref, placing_ref, rows_ref, second_ref, counts_ref, out_ref):
+    copies = []
+    for half in range(2):
+        part = pl.ds(half * (peers // 2), peers // 2)
+        rows = dot(hot[half * (slots // 2) : (half + 1) * (slots // 2)], table_ref[...]).astype(bf16)
+        rows_ref[part] = rows.reshape(peers // 2, capacity, -1)
+        copies.append(pltpu.make_async_copy(rows_ref.at[part], out_ref.at[part], sems.at[half]))
+        copies[-1].start()
+    for copy in copies:
+        copy.wait()
+
+
+def encode_kernel(pre_ref, placing_ref, rows_ref, second_ref, counts_ref, out_ref, vecs_ref, sems):
     rows = dot(placing_ref[...], rows_ref[...].reshape(placing_ref.shape[1], -1))
     hidden = jnp.maximum(pre_ref[...] + rows, 0.0).astype(bf16)
     emb = dot(hidden, second_ref[...])
     square = jnp.sum(emb * emb, -1, keepdims=True)
     vecs = (emb * lax.rsqrt(square + 1e-06)).astype(bf16)
     n, width = vecs.shape
-    bias = jnp.broadcast_to(jnp.log(counts_ref[...].astype(f32)), (16, n))
+    bias = jnp.broadcast_to(jnp.log(counts_ref[...].astype(f32)), (extra, n))
     bias = jnp.concatenate([bias] * (width // n), 1).astype(bf16)
-    for i in range(out_ref.shape[0]):
-        out_ref[i, :n, :] = vecs
-        out_ref[i, n:, :] = bias
+    vecs_ref[:n, :] = vecs
+    vecs_ref[n:, :] = bias
+    peers = out_ref.shape[0]
+    copies = [pltpu.make_async_copy(vecs_ref, out_ref.at[i], sems.at[i]) for i in range(peers)]
+    for copy in copies:
+        copy.start()
+    for copy in copies:
+        copy.wait()
 
 
 def bias_row(ref, i, n):
-    return ref[i, n : n + 16, :n].astype(f32)[0:1, :] * log2_e
+    return ref[i, n : n + extra, :n].astype(f32)[0:1, :] * log2_e
 
 
 def column(row):
@@ -131,7 +147,7 @@
 
 def sums(vecs_ref, unit_refs, store):
     peers, width = vecs_ref.shape[0], vecs_ref.shape[2]
-    n, rows = vecs_ref.shape[1] - 16, unit_refs[0].shape[1]
+    n, rows = vecs_ref.shape[1] - extra, unit_refs[0].shape[1]
     biases = [jnp.broadcast_to(column(bias_row(vecs_ref, i, n)), (n, 128)) for i in range(peers)]
     for t in range(0, 2 * len(unit_refs), 2):
         units = unit_refs[t // 2][...].reshape(2 * rows, width)
@@ -157,7 +173,7 @@
 
 
 def item_sum(place, vecs_ref, units, sums_ref, hot):
-    n, width = vecs_ref.shape[1] - 16, vecs_ref.shape[2]
+    n, width = vecs_ref.shape[1] - extra, vecs_ref.shape[2]
     vecs = vecs_ref[place, :n, :]
     bias = jnp.broadcast_to(column(bias_row(vecs_ref, place, n)), (n, 128))
     grad = jnp.zeros((n, width), f32)
@@ -198,7 +214,7 @@
     exps,
 ):
     peers, width = mine_ref.shape[0], mine_ref.shape[2]
-    n, rows = mine_ref.shape[1] - 16, users_ref.shape[0]
+    n, rows = mine_ref.shape[1] - extra, users_ref.shape[0]
     place = place_ref[0]
     unit_b = units_ref[0]
     denominator = column(sums_ref[0:1, :])
@@ -230,7 +246,7 @@
 
 def item_kernel(place_ref, mine_ref, sums_ref, occurrence_ref, taken_ref, *refs):
     units, out_ref = refs[:-1], refs[-1]
-    n, rows = mine_ref.shape[1] - 16, occurrence_ref.shape[1]
+    n, rows = mine_ref.shape[1] - extra, occurrence_ref.shape[1]
     hot = jnp.where(occurrence_ref[...] == iota((n, rows), 0), 1.0, 0.0)
     grad = item_sum(place_ref[0], mine_ref, units, sums_ref, hot)
     out_ref[...] = grad + taken_ref[...]
@@ -288,6 +304,11 @@
         shape((owners, capacity, id_table.shape[1]), bf16),
         2 * slots * id_table.size,
         2 * id_table.size,
+        scratch=[
+            pltpu.VMEM((owners, capacity, id_table.shape[1]), bf16),
+            pltpu.SemaphoreType.DMA((2,)),
+        ],
+        out_specs=far_memory,
     )(ids.reshape(owners, 128), table)
     far = turn(payload, peers // 2)
     table_rows, feats = lax.optimization_barrier((table_rows, item_feats))
@@ -297,9 +318,11 @@
     units = [pair, turn(pair, 1), turn(pair, -1), turn(pair, 2, -2)]
     vecs = call(
         encode_kernel,
-        shape((peers, n + 16, width), bf16),
+        shape((peers, n + extra, width), bf16),
         2 * n * slots * w_first.shape[1],
         2 * received.size,
+        scratch=[pltpu.VMEM((n + extra, width), bf16), pltpu.SemaphoreType.DMA((peers,))],
+        out_specs=far_memory,
     )(pre, placing, received, w_second, counts.reshape(1, n))
 
     mine = lax.all_to_all(

time: 102 us -> 101 us (level)
  no operation moved by 1% of the time
where the time goes in v4:
time: 101 us
  starting transfers between devices  64.9 us (64%)
  waiting for transfers between devices  20.2 us (20%)
  Pallas kernels  12.3 us (12%)
  local copies, waits for them, and re-layouts  1.64 us (2%)
    all_to_all x1, starting transfers between devices, shards(): lax.all_to_all(ids_sent.reshape(owners, 1, 128), 'shard', 0, 0, tiled=True)  24 us
    ppermute x4, starting transfers between devices, turn(): return lax.ppermute(array, 'blk', pairs)  15.8 us
    all_to_all x1, waiting for transfers between devices, shards(): lax.all_to_all(vecs, 'blk', 0, 0, axis_index_groups=[list(range(c, blocks...  11.8 us
    all_to_all x1, starting transfers between devices, shards(): received = lax.all_to_all(table_rows, 'shard', 0, 0, tiled=True)  10.2 us
    ppermute x1, starting transfers between devices, shards(): other = lax.ppermute(mine, 'blk', swap)  9.12 us
    pallas_call x4, Pallas kernels, step(): call(kernel, out_shape, 2 * pairs * width, moved, pairs, specs, scratch, 48)  7.07 us
    all_to_all x1, waiting for transfers between devices, shards(): received = lax.all_to_all(table_rows, 'shard', 0, 0, tiled=True)  6.24 us
    all_to_all x1, starting transfers between devices, shards(): lax.all_to_all(vecs, 'blk', 0, 0, axis_index_groups=[list(range(c, blocks...  3.55 us
  transfers between devices with their start and end apart: 9, of which 4 were waited for; matrix products, arithmetic and copies ran while one was open for 1% of the time, Pallas kernels for 7%

profile of v4, /device:TPU:1, one launch (start us, length us, event | category | flops | bytes accessed | tf_op | source)
XLA Modules:
  0.0 100.8 jit_solution(7458132558228187683)
XLA Ops:
  0.6 0.0 copy-start
  0.6 2.1 %shard_map.112 = (s32[64,128]{1,0:T(8,128)}, bf16[128,256]{1,0:T(8,128)(2,1)}, bf16[256,256]{1,0:T(8,128)(2,1)}) custom-call(s32[1,128]{1,0:T(1,128)} %bitcast.17, s32[1,128]{1,0:T(1,128)} %bitcast.18, bf16[256,256]{1,0:T(8,128)(2,1)} %users_ref.1), custom_call_target="tpu_custom_call" | custom-call | flops 8388608 | bytes 32768 | tf_op jit(solution)/shard_map/pallas_call | solution.py:273
  2.7 24.0 %all-to-all-start = ((s32[64,1,128]{2,1,0:T(1,128)}), s32[64,1,128]{2,1,0:T(1,128)S(1)}, u32[]{:S(2)}, u32[]{:S(2)}) async-start(s32[64,1,128]{2,1,0:T(1,128)} %bitcast.16), calls=%async_computation | async-start | bytes 65536 | tf_op jit(solution)/shard_map/all_to_all | solution.py:287
  26.7 7.1 %collective-permute-start = (bf16[256,256]{1,0:T(8,128)(2,1)}, bf16[256,256]{1,0:T(8,128)(2,1)S(1)}, u32[]{:S(2)}, u32[]{:S(2)}) collective-permute-start(bf16[256,256]{1,0:T(8,128)(2,1)} %get-tuple-element.18.near_ref), channel_id=1, source_target_pairs={{0,8},{1,9},{2,10},{3,11},{4,12},{5,13},{6,14},{7,15},{8,0},{9,1},... | collective-permute-start | bytes 393224 | tf_op jit(solution)/shard_map/ppermute | solution.py:300
  33.8 0.0 copy-start.6
  33.8 1.6 %copy-done.6 = bf16[1024,1024]{1,0:T(8,128)(2,1)S(1)} copy-done((bf16[1024,1024]{1,0:T(8,128)(2,1)S(1)}, bf16[1024,1024]{1,0:T(8,128)(2,1)}, u32[]{:S(2)}) %copy-start.6) | copy-done | bytes 2097176
  35.4 0.0 copy-start.7
  35.4 0.1 shard_map.113.table_ref
  35.6 1.9 %all-to-all-done = s32[64,1,128]{2,1,0:T(1,128)S(1)} async-done(((s32[64,1,128]{2,1,0:T(1,128)}), s32[64,1,128]{2,1,0:T(1,128)S(1)}, u32[]{:S(2)}, u32[]{:S(2)}) %all-to-all-start) | async-done | bytes 32800 | tf_op jit(solution)/shard_map/all_to_all | solution.py:287
  37.5 1.6 %shard_map.114 = bf16[64,4,1024]{2,1,0:T(4,128)(2,1)} custom-call(s32[64,128]{1,0:T(8,128)S(1)} %bitcast.12, bf16[1024,1024]{1,0:T(8,128)(2,1)S(1)} %shard_map.113.table_ref), custom_call_target="tpu_custom_call" | custom-call | flops 536870912 | bytes 2097152 | tf_op jit(solution)/shard_map/pallas_call | solution.py:302
  39.1 10.2 %all-to-all-start.1 = ((bf16[64,4,1024]{2,1,0:T(4,128)(2,1)}), bf16[64,4,1024]{2,1,0:T(4,128)(2,1)S(1)}, u32[]{:S(2)}, u32[]{:S(2)}) async-start(bf16[64,4,1024]{2,1,0:T(4,128)(2,1)} %shard_map.114), calls=%async_computation.1 | async-start | bytes 1048576 | tf_op jit(solution)/shard_map/all_to_all | solution.py:316
  49.4 0.0 copy-start.8
  49.4 0.0 collective-permute-done.far_ref
  49.4 0.0 copy-done.7
  49.4 0.0 copy-start.1
  49.4 0.0 copy-start.3
  49.4 0.0 copy-start.5
  49.5 2.5 %collective-permute-start.1 = (bf16[2,256,256]{2,1,0:T(8,128)(2,1)S(1)}, bf16[2,256,256]{2,1,0:T(8,128)(2,1)S(1)}, u32[]{:S(2)}, u32[]{:S(2)}) collective-permute-start(bf16[2,256,256]{2,1,0:T(8,128)(2,1)S(1)} %shard_map.116.refs_0_.units_ref), channel_id=1, source_target_pairs={{0,2},{1,3},{2,4},{3,5},{4,6},{5,7},{6,8},{7,9},{8,10},{9,11},{10,... | collective-permute-start | bytes 786440 | tf_op jit(solution)/shard_map/ppermute | solution.py:300
  51.9 4.3 %collective-permute-start.2 = (bf16[2,256,256]{2,1,0:T(8,128)(2,1)S(1)}, bf16[2,256,256]{2,1,0:T(8,128)(2,1)S(1)}, u32[]{:S(2)}, u32[]{:S(2)}) collective-permute-start(bf16[2,256,256]{2,1,0:T(8,128)(2,1)S(1)} %shard_map.116.refs_0_.units_ref), channel_id=1, source_target_pairs={{0,14},{1,15},{2,0},{3,1},{4,2},{5,3},{6,4},{7,5},{8,6},{9,7},{10,... | collective-permute-start | bytes 786440 | tf_op jit(solution)/shard_map/ppermute | solution.py:300
  56.2 1.9 %collective-permute-start.3 = (bf16[2,256,256]{2,1,0:T(8,128)(2,1)S(1)}, bf16[2,256,256]{2,1,0:T(8,128)(2,1)S(1)}, u32[]{:S(2)}, u32[]{:S(2)}) collective-permute-start(bf16[2,256,256]{2,1,0:T(8,128)(2,1)S(1)} %shard_map.116.refs_0_.units_ref), channel_id=1, source_target_pairs={{0,4},{1,13},{2,6},{3,15},{4,8},{5,1},{6,10},{7,3},{8,12},{9,5},{1... | collective-permute-start | bytes 786440 | tf_op jit(solution)/shard_map/ppermute | solution.py:300
  58.2 0.0 copy-done
  58.2 0.0 copy-done.8
  58.2 0.7 fusion.pre_ref
  58.9 6.2 %all-to-all-done.1.rows_ref = bf16[64,4,1024]{2,1,0:T(4,128)(2,1)S(1)} async-done(((bf16[64,4,1024]{2,1,0:T(4,128)(2,1)}), bf16[64,4,1024]{2,1,0:T(4,128)(2,1)S(1)}, u32[]{:S(2)}, u32[]{:S(2)}) %all-to-all-start.1) | async-done | bytes 524320 | tf_op jit(solution)/shard_map/all_to_all | solution.py:316
  65.2 0.0 copy-done.1
  65.2 0.0 copy-done.3
  65.2 0.0 copy-done.5
  65.2 1.4 %shard_map.115 = bf16[8,136,256]{2,1,0:T(8,128)(2,1)} custom-call(f32[128,1024]{1,0:T(8,128)S(1)} %fusion.pre_ref, bf16[128,256]{1,0:T(8,128)(2,1)S(1)} %copy-done.3, bf16[64,4,1024]{2,1,0:T(4,128)(2,1)S(1)} %all-to-all-done.1.rows_ref, bf16[1024,256]{1,0:T(8,128)(2,1)S(1)} %copy-done.1, s32[1,128]{1,0:T(1,128)S(1)} %bitcast.15), custom_call_target="tpu_custom_call" | custom-call | flops 67108864 | bytes 524288 | tf_op jit(solution)/shard_map/pallas_call | solution.py:319
  66.6 3.5 %all-to-all-start.2 = ((bf16[8,136,256]{2,1,0:T(8,128)(2,1)}), bf16[8,136,256]{2,1,0:T(8,128)(2,1)S(1)}, u32[]{:S(2)}, u32[]{:S(2)}) async-start(bf16[8,136,256]{2,1,0:T(8,128)(2,1)} %shard_map.115), calls=%async_computation.2 | async-start | bytes 1114112 | tf_op jit(solution)/shard_map/all_to_all | solution.py:328
  70.1 0.0 collective-permute-done.1.one_ref.refs_1_
  70.1 0.0 collective-permute-done.2.two_ref.refs_2_
  70.1 0.0 collective-permute-done.3.three_ref.refs_3_
  70.2 0.0 copy-start.2
  70.2 0.0 copy-start.4
  70.2 11.8 %all-to-all-done.2.vecs_ref.mine_ref = bf16[8,136,256]{2,1,0:T(8,128)(2,1)S(1)} async-done(((bf16[8,136,256]{2,1,0:T(8,128)(2,1)}), bf16[8,136,256]{2,1,0:T(8,128)(2,1)S(1)}, u32[]{:S(2)}, u32[]{:S(2)}) %all-to-all-start.2) | async-done | bytes 557088 | tf_op jit(solution)/shard_map/all_to_all | solution.py:328
  82.0 9.1 %collective-permute-start.4 = (bf16[8,136,256]{2,1,0:T(8,128)(2,1)S(1)}, bf16[8,136,256]{2,1,0:T(8,128)(2,1)S(1)}, u32[]{:S(2)}, u32[]{:S(2)}) collective-permute-start(bf16[8,136,256]{2,1,0:T(8,128)(2,1)S(1)} %all-to-all-done.2.vecs_ref.mine_ref), channel_id=1, source_target_pairs={{0,1},{1,0},{2,3},{3,2},{4,5},{5,4},{6,7},{7,6},{8,9},{9,8},{10,11... | collective-permute-start | bytes 1671176 | tf_op jit(solution)/shard_map/ppermute | solution.py:340
  91.2 1.4 %shard_map.118.first_ref = f32[8,256]{1,0:T(8,128)S(1)} custom-call(bf16[8,136,256]{2,1,0:T(8,128)(2,1)S(1)} %all-to-all-done.2.vecs_ref.mine_ref, f32[8,128]{1,0:T(8,128)S(1)} %shard_map.117.ready_ref, bf16[2,256,256]{2,1,0:T(8,128)(2,1)S(1)} %shard_map.116.refs_0_.units_ref, bf16[2,256,256]{2,1,0:T(8,128)(2,1)S(1)} %collective-permute-done.1.one_ref.refs_1_, ...), custom_call_target="tpu_custom_call" | custom-call | flops 1073741824 | bytes 2097152 | tf_op jit(solution)/shard_map/pallas_call | solution.py:346
  92.5 0.2 collective-permute-done.4.vecs_ref.other_ref
  92.7 2.0 %shard_map.119 = (f32[8,256]{1,0:T(8,128)S(1)}, f32[128,256]{1,0:T(8,128)S(1)}) custom-call(s32[1]{0:T(128)} %bitcast.place_ref, bf16[8,136,256]{2,1,0:T(8,128)(2,1)S(1)} %collective-permute-done.4.vecs_ref.other_ref, f32[8,256]{1,0:T(8,128)S(1)} %shard_map.118.first_ref, bf16[2,256,256]{2,1,0:T(8,128)(2,1)S(1)} %shard_map.116.refs_0_.units_ref, ...), custom_call_target="tpu_custom_call" | custom-call | flops 1073741824 | bytes 2097152 | tf_op jit(solution)/shard_map/pallas_call | solution.py:346
  94.7 2.3 %collective-permute-start.5 = (f32[128,256]{1,0:T(8,128)S(1)}, f32[128,256]{1,0:T(8,128)S(1)}, u32[]{:S(2)}, u32[]{:S(2)}) collective-permute-start(f32[128,256]{1,0:T(8,128)S(1)} %get-tuple-element.24), channel_id=1, source_target_pairs={{0,1},{1,0},{2,3},{3,2},{4,5},{5,4},{6,7},{7,6},{8,9},{9,8},{10,11... | collective-permute-start | bytes 393224 | tf_op jit(solution)/shard_map/ppermute | solution.py:357
  97.0 0.0 copy-done.2
  97.0 0.0 copy-done.4
  97.0 2.3 %shard_map.120 = (f32[1,256]{1,0:T(1,128)}, f32[256,256]{1,0:T(8,128)}) custom-call(s32[1]{0:T(128)} %bitcast.place_ref, bf16[8,136,256]{2,1,0:T(8,128)(2,1)S(1)} %all-to-all-done.2.vecs_ref.mine_ref, bf16[8,136,256]{2,1,0:T(8,128)(2,1)S(1)} %collective-permute-done.4.vecs_ref.other_ref, f32[8,256]{1,0:T(8,128)S(1)} %get-tuple-element.21.sums_ref, ...), custom_call_target="tpu_custom_call" | custom-call | flops 1073741824 | bytes 2097152 | tf_op jit(solution)/shard_map/pallas_call | solution.py:346
  99.3 0.0 collective-permute-done.5.taken_ref
  99.3 1.5 %shard_map.121 = f32[128,256]{1,0:T(8,128)} custom-call(s32[1]{0:T(128)} %bitcast.place_ref, bf16[8,136,256]{2,1,0:T(8,128)(2,1)S(1)} %all-to-all-done.2.vecs_ref.mine_ref, f32[8,256]{1,0:T(8,128)S(1)} %get-tuple-element.21.sums_ref, s32[1,256]{1,0:T(1,128)S(1)} %bitcast.14, f32[128,256]{1,0:T(8,128)S(1)} %collective-permute-done.5.taken_ref, ...), custom_call_target="tpu_custom_call" | custom-call | flops 134217728 | bytes 2097152 | tf_op jit(solution)/shard_map/pallas_call | solution.py:346
  (2 shorter events, 0.0 us)
Async XLA Ops:
  0.6 57.5 %copy-start = (bf16[128,2048]{1,0:T(8,128)(2,1)S(1)}, bf16[128,2048]{1,0:T(8,128)(2,1)}, u32[]{:S(2)}) copy-start(bf16[128,2048]{1,0:T(8,128)(2,1)} %param.9) | copy-start | bytes 1572868
  2.7 34.8 %all-to-all-start = ((s32[64,1,128]{2,1,0:T(1,128)}), s32[64,1,128]{2,1,0:T(1,128)S(1)}, u32[]{:S(2)}, u32[]{:S(2)}) async-start(s32[64,1,128]{2,1,0:T(1,128)} %bitcast.16), calls=%async_computation | async-start | bytes 65536 | tf_op jit(solution)/shard_map/all_to_all | solution.py:287
  26.7 22.7 %collective-permute-start = (bf16[256,256]{1,0:T(8,128)(2,1)}, bf16[256,256]{1,0:T(8,128)(2,1)S(1)}, u32[]{:S(2)}, u32[]{:S(2)}) collective-permute-start(bf16[256,256]{1,0:T(8,128)(2,1)} %get-tuple-element.18.near_ref), channel_id=1, source_target_pairs={{0,8},{1,9},{2,10},{3,11},{4,12},{5,13},{6,14},{7,15},{8,0},{9,1},... | collective-permute-start | bytes 393224 | tf_op jit(solution)/shard_map/ppermute | solution.py:300
  33.8 1.6 %copy-start.6 = (bf16[1024,1024]{1,0:T(8,128)(2,1)S(1)}, bf16[1024,1024]{1,0:T(8,128)(2,1)}, u32[]{:S(2)}) copy-start(bf16[1024,1024]{1,0:T(8,128)(2,1)} %table_in.1) | copy-start | bytes 6291460
  35.4 14.0 %copy-start.7 = (bf16[256,256]{1,0:T(8,128)(2,1)S(1)}, bf16[256,256]{1,0:T(8,128)(2,1)}, u32[]{:S(2)}) copy-start(bf16[256,256]{1,0:T(8,128)(2,1)} %get-tuple-element.18.near_ref) | copy-start | bytes 393220
  39.1 26.0 %all-to-all-start.1 = ((bf16[64,4,1024]{2,1,0:T(4,128)(2,1)}), bf16[64,4,1024]{2,1,0:T(4,128)(2,1)S(1)}, u32[]{:S(2)}, u32[]{:S(2)}) async-start(bf16[64,4,1024]{2,1,0:T(4,128)(2,1)} %shard_map.114), calls=%async_computation.1 | async-start | bytes 1048576 | tf_op jit(solution)/shard_map/all_to_all | solution.py:316
  49.4 8.8 %copy-start.8 = (bf16[2048,1024]{1,0:T(8,128)(2,1)S(1)}, bf16[2048,1024]{1,0:T(8,128)(2,1)}, u32[]{:S(2)}) copy-start(bf16[2048,1024]{1,0:T(8,128)(2,1)} %param.15) | copy-start | bytes 12582916
  49.4 15.8 %copy-start.1 = (bf16[1024,256]{1,0:T(8,128)(2,1)S(1)}, bf16[1024,256]{1,0:T(8,128)(2,1)}, u32[]{:S(2)}) copy-start(bf16[1024,256]{1,0:T(8,128)(2,1)} %second_ref.1) | copy-start | bytes 1572868
  49.4 15.7 %copy-start.3 = (bf16[128,256]{1,0:T(8,128)(2,1)S(1)}, bf16[128,256]{1,0:T(8,128)(2,1)}, u32[]{:S(2)}) copy-start(bf16[128,256]{1,0:T(8,128)(2,1)} %get-tuple-element.16.placing_ref) | copy-start | bytes 196612
  49.4 15.7 %copy-start.5 = (s32[128]{0:T(128)S(1)}, s32[128]{0:T(128)}, u32[]{:S(2)}) copy-start(s32[128]{0:T(128)} %param.12) | copy-start | bytes 1540
  49.5 20.7 %collective-permute-start.1 = (bf16[2,256,256]{2,1,0:T(8,128)(2,1)S(1)}, bf16[2,256,256]{2,1,0:T(8,128)(2,1)S(1)}, u32[]{:S(2)}, u32[]{:S(2)}) collective-permute-start(bf16[2,256,256]{2,1,0:T(8,128)(2,1)S(1)} %shard_map.116.refs_0_.units_ref), channel_id=1, source_target_pairs={{0,2},{1,3},{2,4},{3,5},{4,6},{5,7},{6,8},{7,9},{8,10},{9,11},{10,... | collective-permute-start | bytes 786440 | tf_op jit(solution)/shard_map/ppermute | solution.py:300
  51.9 18.2 %collective-permute-start.2 = (bf16[2,256,256]{2,1,0:T(8,128)(2,1)S(1)}, bf16[2,256,256]{2,1,0:T(8,128)(2,1)S(1)}, u32[]{:S(2)}, u32[]{:S(2)}) collective-permute-start(bf16[2,256,256]{2,1,0:T(8,128)(2,1)S(1)} %shard_map.116.refs_0_.units_ref), channel_id=1, source_target_pairs={{0,14},{1,15},{2,0},{3,1},{4,2},{5,3},{6,4},{7,5},{8,6},{9,7},{10,... | collective-permute-start | bytes 786440 | tf_op jit(solution)/shard_map/ppermute | solution.py:300
  56.2 13.9 %collective-permute-start.3 = (bf16[2,256,256]{2,1,0:T(8,128)(2,1)S(1)}, bf16[2,256,256]{2,1,0:T(8,128)(2,1)S(1)}, u32[]{:S(2)}, u32[]{:S(2)}) collective-permute-start(bf16[2,256,256]{2,1,0:T(8,128)(2,1)S(1)} %shard_map.116.refs_0_.units_ref), channel_id=1, source_target_pairs={{0,4},{1,13},{2,6},{3,15},{4,8},{5,1},{6,10},{7,3},{8,12},{9,5},{1... | collective-permute-start | bytes 786440 | tf_op jit(solution)/shard_map/ppermute | solution.py:300
  66.6 15.4 %all-to-all-start.2 = ((bf16[8,136,256]{2,1,0:T(8,128)(2,1)}), bf16[8,136,256]{2,1,0:T(8,128)(2,1)S(1)}, u32[]{:S(2)}, u32[]{:S(2)}) async-start(bf16[8,136,256]{2,1,0:T(8,128)(2,1)} %shard_map.115), calls=%async_computation.2 | async-start | bytes 1114112 | tf_op jit(solution)/shard_map/all_to_all | solution.py:328
  70.2 26.8 %copy-start.2 = (bf16[256,256]{1,0:T(8,128)(2,1)S(1)}, bf16[256,256]{1,0:T(8,128)(2,1)}, u32[]{:S(2)}) copy-start(bf16[256,256]{1,0:T(8,128)(2,1)} %users_ref.1) | copy-start | bytes 393220
  70.2 26.8 %copy-start.4 = (s32[256]{0:T(256)S(1)}, s32[256]{0:T(256)}, u32[]{:S(2)}) copy-start(s32[256]{0:T(256)} %param.13) | copy-start | bytes 3076
  82.0 10.7 %collective-permute-start.4 = (bf16[8,136,256]{2,1,0:T(8,128)(2,1)S(1)}, bf16[8,136,256]{2,1,0:T(8,128)(2,1)S(1)}, u32[]{:S(2)}, u32[]{:S(2)}) collective-permute-start(bf16[8,136,256]{2,1,0:T(8,128)(2,1)S(1)} %all-to-all-done.2.vecs_ref.mine_ref), channel_id=1, source_target_pairs={{0,1},{1,0},{2,3},{3,2},{4,5},{5,4},{6,7},{7,6},{8,9},{9,8},{10,11... | collective-permute-start | bytes 1671176 | tf_op jit(solution)/shard_map/ppermute | solution.py:340
  94.7 4.6 %collective-permute-start.5 = (f32[128,256]{1,0:T(8,128)S(1)}, f32[128,256]{1,0:T(8,128)S(1)}, u32[]{:S(2)}, u32[]{:S(2)}) collective-permute-start(f32[128,256]{1,0:T(8,128)S(1)} %get-tuple-element.24), channel_id=1, source_target_pairs={{0,1},{1,0},{2,3},{3,2},{4,5},{5,4},{6,7},{7,6},{8,9},{9,8},{10,11... | collective-permute-start | bytes 393224 | tf_op jit(solution)/shard_map/ppermute | solution.py:357

commit v5 on v4

--- a/solution.py
+++ b/solution.py
@@ -12,6 +12,7 @@
 exponent_scale = logit_scale * log2_e
 vmem = pl.BlockSpec(memory_space=pltpu.VMEM)
 far_memory = pl.BlockSpec(memory_space=pltpu.HBM)
+anywhere = pl.BlockSpec(memory_space=pl.ANY)
 f32, bf16 = jnp.float32, jnp.bfloat16
 extra = 8
 
@@ -81,7 +82,11 @@
     payload_ref[...] = (user_f * inverse).astype(bf16)
 
 
-def table_kernel(table_in, table_ref, sem):
+def early_kernel(payload_ref, out_ref):
+    out_ref[...] = jnp.zeros_like(out_ref)
+
+
+def table_kernel(table_in, after_ref, table_ref, sem):
     copy = pltpu.make_async_copy(table_in, table_ref, sem)
     copy.start()
     copy.wait()
@@ -285,14 +290,15 @@
         room=60,
     )(owner.reshape(1, n), id_row.reshape(1, n), users)
     ids = lax.all_to_all(ids_sent.reshape(owners, 1, 128), "shard", 0, 0, tiled=True)
+    early = call(early_kernel, shape((8, 128), f32), long // 20, 1024, in_specs=[anywhere])(payload)
     table = call(
         table_kernel,
         shape(id_table.shape, bf16),
         long // 20,
         4 * id_table.size,
-        in_specs=[far_memory],
+        in_specs=[far_memory, anywhere],
         scratch=[pltpu.SemaphoreType.DMA],
-    )(id_table)
+    )(id_table, early)
 
     def turn(array, step, other_step=None):
         steps = (step, step if other_step is None else other_step)
@@ -334,7 +340,7 @@
         tiled=True,
     )
     ready = call(
-        ready_kernel, shape((8, 128), f32), long, 1024, in_specs=[pl.BlockSpec(memory_space=pl.ANY)] * 3
+        ready_kernel, shape((8, 128), f32), long, 1024, in_specs=[anywhere] * 3
     )(*units[1:])
     mine, ready = lax.optimization_barrier((mine, ready))
     other = lax.ppermute(mine, "blk", swap)

time: 101 us -> 101 us (level)
  no operation moved by 1% of the time
where the time goes in v5:
time: 101 us; the launch traced here: 100 us
  starting transfers between devices  64.5 us (64%)
  waiting for transfers between devices  20.8 us (21%)
  Pallas kernels  12.3 us (12%)
    all_to_all x1, starting transfers between devices, shards(): lax.all_to_all(ids_sent.reshape(owners, 1, 128), 'shard', 0, 0, tiled=True)  24 us
    ppermute x4, starting transfers between devices, turn(): return lax.ppermute(array, 'blk', pairs)  15.9 us
    all_to_all x1, waiting for transfers between devices, shards(): lax.all_to_all(vecs, 'blk', 0, 0, axis_index_groups=[list(range(c, blocks...  11.8 us
    all_to_all x1, starting transfers between devices, shards(): received = lax.all_to_all(table_rows, 'shard', 0, 0, tiled=True)  9.65 us
    ppermute x1, starting transfers between devices, shards(): other = lax.ppermute(mine, 'blk', swap)  9.11 us
    pallas_call x4, Pallas kernels, step(): call(kernel, out_shape, 2 * pairs * width, moved, pairs, specs, scratch, 48)  7.07 us
    all_to_all x1, waiting for transfers between devices, shards(): received = lax.all_to_all(table_rows, 'shard', 0, 0, tiled=True)  6.24 us
    all_to_all x1, starting transfers between devices, shards(): lax.all_to_all(vecs, 'blk', 0, 0, axis_index_groups=[list(range(c, blocks...  3.55 us
  transfers between devices with their start and end apart: 9, of which 4 were waited for; matrix products, arithmetic and copies ran while one was open for 1% of the time, Pallas kernels for 7%

profile of v5, /device:TPU:1, one launch (start us, length us, event | category | flops | bytes accessed | tf_op | source)
XLA Modules:
  0.0 100.2 jit_solution(15461517357960107362)
XLA Ops:
  0.6 0.0 copy-start
  0.6 2.1 %shard_map.112 = (s32[64,128]{1,0:T(8,128)}, bf16[128,256]{1,0:T(8,128)(2,1)}, bf16[256,256]{1,0:T(8,128)(2,1)}) custom-call(s32[1,128]{1,0:T(1,128)} %bitcast.17, s32[1,128]{1,0:T(1,128)} %bitcast.18, bf16[256,256]{1,0:T(8,128)(2,1)} %users_ref.1), custom_call_target="tpu_custom_call" | custom-call | flops 8388608 | bytes 32768 | tf_op jit(solution)/shard_map/pallas_call | solution.py:278
  2.7 24.0 %all-to-all-start = ((s32[64,1,128]{2,1,0:T(1,128)}), s32[64,1,128]{2,1,0:T(1,128)S(1)}, u32[]{:S(2)}, u32[]{:S(2)}) async-start(s32[64,1,128]{2,1,0:T(1,128)} %bitcast.16), calls=%async_computation | async-start | bytes 65536 | tf_op jit(solution)/shard_map/all_to_all | solution.py:292
  26.7 0.0 copy-start.6
  26.7 7.2 %collective-permute-start = (bf16[256,256]{1,0:T(8,128)(2,1)}, bf16[256,256]{1,0:T(8,128)(2,1)S(1)}, u32[]{:S(2)}, u32[]{:S(2)}) collective-permute-start(bf16[256,256]{1,0:T(8,128)(2,1)} %get-tuple-element.15.payload_ref.near_ref), channel_id=1, source_target_pairs={{0,8},{1,9},{2,10},{3,11},{4,12},{5,13},{6,14},{7,15},{8,0},{9,1},... | collective-permute-start | bytes 393224 | tf_op jit(solution)/shard_map/ppermute | solution.py:306
  34.0 0.0 copy-start.7
  34.0 0.9 copy-done.7
  34.9 0.0 copy-done.6
  34.9 0.0 copy-start.8
  34.9 0.2 shard_map.114.table_ref
  35.1 2.5 %all-to-all-done = s32[64,1,128]{2,1,0:T(1,128)S(1)} async-done(((s32[64,1,128]{2,1,0:T(1,128)}), s32[64,1,128]{2,1,0:T(1,128)S(1)}, u32[]{:S(2)}, u32[]{:S(2)}) %all-to-all-start) | async-done | bytes 32800 | tf_op jit(solution)/shard_map/all_to_all | solution.py:292
  37.6 1.6 %shard_map.115 = bf16[64,4,1024]{2,1,0:T(4,128)(2,1)} custom-call(s32[64,128]{1,0:T(8,128)S(1)} %bitcast.12, bf16[1024,1024]{1,0:T(8,128)(2,1)S(1)} %shard_map.114.table_ref), custom_call_target="tpu_custom_call" | custom-call | flops 536870912 | bytes 2097152 | tf_op jit(solution)/shard_map/pallas_call | solution.py:308
  39.2 9.7 %all-to-all-start.1 = ((bf16[64,4,1024]{2,1,0:T(4,128)(2,1)}), bf16[64,4,1024]{2,1,0:T(4,128)(2,1)S(1)}, u32[]{:S(2)}, u32[]{:S(2)}) async-start(bf16[64,4,1024]{2,1,0:T(4,128)(2,1)} %shard_map.115), calls=%async_computation.1 | async-start | bytes 1048576 | tf_op jit(solution)/shard_map/all_to_all | solution.py:322
  48.9 0.0 copy-start.9
  48.9 0.0 collective-permute-done.far_ref
  48.9 0.0 copy-done.8
  48.9 0.0 copy-start.1
  48.9 0.0 copy-start.3
  49.0 0.0 copy-start.5
  49.0 2.5 %collective-permute-start.1 = (bf16[2,256,256]{2,1,0:T(8,128)(2,1)S(1)}, bf16[2,256,256]{2,1,0:T(8,128)(2,1)S(1)}, u32[]{:S(2)}, u32[]{:S(2)}) collective-permute-start(bf16[2,256,256]{2,1,0:T(8,128)(2,1)S(1)} %shard_map.117.refs_0_.units_ref), channel_id=1, source_target_pairs={{0,2},{1,3},{2,4},{3,5},{4,6},{5,7},{6,8},{7,9},{8,10},{9,11},{10,... | collective-permute-start | bytes 786440 | tf_op jit(solution)/shard_map/ppermute | solution.py:306
  51.5 4.3 %collective-permute-start.2 = (bf16[2,256,256]{2,1,0:T(8,128)(2,1)S(1)}, bf16[2,256,256]{2,1,0:T(8,128)(2,1)S(1)}, u32[]{:S(2)}, u32[]{:S(2)}) collective-permute-start(bf16[2,256,256]{2,1,0:T(8,128)(2,1)S(1)} %shard_map.117.refs_0_.units_ref), channel_id=1, source_target_pairs={{0,14},{1,15},{2,0},{3,1},{4,2},{5,3},{6,4},{7,5},{8,6},{9,7},{10,... | collective-permute-start | bytes 786440 | tf_op jit(solution)/shard_map/ppermute | solution.py:306
  55.7 1.9 %collective-permute-start.3 = (bf16[2,256,256]{2,1,0:T(8,128)(2,1)S(1)}, bf16[2,256,256]{2,1,0:T(8,128)(2,1)S(1)}, u32[]{:S(2)}, u32[]{:S(2)}) collective-permute-start(bf16[2,256,256]{2,1,0:T(8,128)(2,1)S(1)} %shard_map.117.refs_0_.units_ref), channel_id=1, source_target_pairs={{0,4},{1,13},{2,6},{3,15},{4,8},{5,1},{6,10},{7,3},{8,12},{9,5},{1... | collective-permute-start | bytes 786440 | tf_op jit(solution)/shard_map/ppermute | solution.py:306
  57.7 0.0 copy-done
  57.7 0.0 copy-done.9
  57.7 0.7 fusion.pre_ref
  58.4 6.2 %all-to-all-done.1.rows_ref = bf16[64,4,1024]{2,1,0:T(4,128)(2,1)S(1)} async-done(((bf16[64,4,1024]{2,1,0:T(4,128)(2,1)}), bf16[64,4,1024]{2,1,0:T(4,128)(2,1)S(1)}, u32[]{:S(2)}, u32[]{:S(2)}) %all-to-all-start.1) | async-done | bytes 524320 | tf_op jit(solution)/shard_map/all_to_all | solution.py:322
  64.7 0.0 copy-done.1
  64.7 0.0 copy-done.3
  64.7 0.0 copy-done.5
  64.7 1.4 %shard_map.116 = bf16[8,136,256]{2,1,0:T(8,128)(2,1)} custom-call(f32[128,1024]{1,0:T(8,128)S(1)} %fusion.pre_ref, bf16[128,256]{1,0:T(8,128)(2,1)S(1)} %copy-done.3, bf16[64,4,1024]{2,1,0:T(4,128)(2,1)S(1)} %all-to-all-done.1.rows_ref, bf16[1024,256]{1,0:T(8,128)(2,1)S(1)} %copy-done.1, s32[1,128]{1,0:T(1,128)S(1)} %bitcast.15), custom_call_target="tpu_custom_call" | custom-call | flops 67108864 | bytes 524288 | tf_op jit(solution)/shard_map/pallas_call | solution.py:325
  66.1 3.5 %all-to-all-start.2 = ((bf16[8,136,256]{2,1,0:T(8,128)(2,1)}), bf16[8,136,256]{2,1,0:T(8,128)(2,1)S(1)}, u32[]{:S(2)}, u32[]{:S(2)}) async-start(bf16[8,136,256]{2,1,0:T(8,128)(2,1)} %shard_map.116), calls=%async_computation.2 | async-start | bytes 1114112 | tf_op jit(solution)/shard_map/all_to_all | solution.py:334
  69.6 0.0 collective-permute-done.1.one_ref.refs_1_
  69.6 0.0 collective-permute-done.2.two_ref.refs_2_
  69.6 0.0 collective-permute-done.3.three_ref.refs_3_
  69.7 0.0 copy-start.2
  69.7 0.0 copy-start.4
  69.7 11.8 %all-to-all-done.2.vecs_ref.mine_ref = bf16[8,136,256]{2,1,0:T(8,128)(2,1)S(1)} async-done(((bf16[8,136,256]{2,1,0:T(8,128)(2,1)}), bf16[8,136,256]{2,1,0:T(8,128)(2,1)S(1)}, u32[]{:S(2)}, u32[]{:S(2)}) %all-to-all-start.2) | async-done | bytes 557088 | tf_op jit(solution)/shard_map/all_to_all | solution.py:334
  81.5 9.1 %collective-permute-start.4 = (bf16[8,136,256]{2,1,0:T(8,128)(2,1)S(1)}, bf16[8,136,256]{2,1,0:T(8,128)(2,1)S(1)}, u32[]{:S(2)}, u32[]{:S(2)}) collective-permute-start(bf16[8,136,256]{2,1,0:T(8,128)(2,1)S(1)} %all-to-all-done.2.vecs_ref.mine_ref), channel_id=1, source_target_pairs={{0,1},{1,0},{2,3},{3,2},{4,5},{5,4},{6,7},{7,6},{8,9},{9,8},{10,11... | collective-permute-start | bytes 1671176 | tf_op jit(solution)/shard_map/ppermute | solution.py:346
  90.7 1.4 %shard_map.119.first_ref = f32[8,256]{1,0:T(8,128)S(1)} custom-call(bf16[8,136,256]{2,1,0:T(8,128)(2,1)S(1)} %all-to-all-done.2.vecs_ref.mine_ref, f32[8,128]{1,0:T(8,128)S(1)} %shard_map.118.ready_ref, bf16[2,256,256]{2,1,0:T(8,128)(2,1)S(1)} %shard_map.117.refs_0_.units_ref, bf16[2,256,256]{2,1,0:T(8,128)(2,1)S(1)} %collective-permute-done.1.one_ref.refs_1_, ...), custom_call_target="tpu_custom_call" | custom-call | flops 1073741824 | bytes 2097152 | tf_op jit(solution)/shard_map/pallas_call | solution.py:352
  92.0 0.2 collective-permute-done.4.vecs_ref.other_ref
  92.2 2.0 %shard_map.120 = (f32[8,256]{1,0:T(8,128)S(1)}, f32[128,256]{1,0:T(8,128)S(1)}) custom-call(s32[1]{0:T(128)} %bitcast.place_ref, bf16[8,136,256]{2,1,0:T(8,128)(2,1)S(1)} %collective-permute-done.4.vecs_ref.other_ref, f32[8,256]{1,0:T(8,128)S(1)} %shard_map.119.first_ref, bf16[2,256,256]{2,1,0:T(8,128)(2,1)S(1)} %shard_map.117.refs_0_.units_ref, ...), custom_call_target="tpu_custom_call" | custom-call | flops 1073741824 | bytes 2097152 | tf_op jit(solution)/shard_map/pallas_call | solution.py:352
  94.2 2.3 %collective-permute-start.5 = (f32[128,256]{1,0:T(8,128)S(1)}, f32[128,256]{1,0:T(8,128)S(1)}, u32[]{:S(2)}, u32[]{:S(2)}) collective-permute-start(f32[128,256]{1,0:T(8,128)S(1)} %get-tuple-element.24), channel_id=1, source_target_pairs={{0,1},{1,0},{2,3},{3,2},{4,5},{5,4},{6,7},{7,6},{8,9},{9,8},{10,11... | collective-permute-start | bytes 393224 | tf_op jit(solution)/shard_map/ppermute | solution.py:363
  96.5 0.0 copy-done.2
  96.5 0.0 copy-done.4
  96.5 2.3 %shard_map.121 = (f32[1,256]{1,0:T(1,128)}, f32[256,256]{1,0:T(8,128)}) custom-call(s32[1]{0:T(128)} %bitcast.place_ref, bf16[8,136,256]{2,1,0:T(8,128)(2,1)S(1)} %all-to-all-done.2.vecs_ref.mine_ref, bf16[8,136,256]{2,1,0:T(8,128)(2,1)S(1)} %collective-permute-done.4.vecs_ref.other_ref, f32[8,256]{1,0:T(8,128)S(1)} %get-tuple-element.21.sums_ref, ...), custom_call_target="tpu_custom_call" | custom-call | flops 1073741824 | bytes 2097152 | tf_op jit(solution)/shard_map/pallas_call | solution.py:352
  98.8 0.0 collective-permute-done.5.taken_ref
  98.8 1.5 %shard_map.122 = f32[128,256]{1,0:T(8,128)} custom-call(s32[1]{0:T(128)} %bitcast.place_ref, bf16[8,136,256]{2,1,0:T(8,128)(2,1)S(1)} %all-to-all-done.2.vecs_ref.mine_ref, f32[8,256]{1,0:T(8,128)S(1)} %get-tuple-element.21.sums_ref, s32[1,256]{1,0:T(1,128)S(1)} %bitcast.14, f32[128,256]{1,0:T(8,128)S(1)} %collective-permute-done.5.taken_ref, ...), custom_call_target="tpu_custom_call" | custom-call | flops 134217728 | bytes 2097152 | tf_op jit(solution)/shard_map/pallas_call | solution.py:352
  (3 shorter events, 0.0 us)
Async XLA Ops:
  0.6 57.0 %copy-start = (bf16[128,2048]{1,0:T(8,128)(2,1)S(1)}, bf16[128,2048]{1,0:T(8,128)(2,1)}, u32[]{:S(2)}) copy-start(bf16[128,2048]{1,0:T(8,128)(2,1)} %param.9) | copy-start | bytes 1572868
  2.7 34.8 %all-to-all-start = ((s32[64,1,128]{2,1,0:T(1,128)}), s32[64,1,128]{2,1,0:T(1,128)S(1)}, u32[]{:S(2)}, u32[]{:S(2)}) async-start(s32[64,1,128]{2,1,0:T(1,128)} %bitcast.16), calls=%async_computation | async-start | bytes 65536 | tf_op jit(solution)/shard_map/all_to_all | solution.py:292
  26.7 8.2 %copy-start.6 = (bf16[1024,1024]{1,0:T(8,128)(2,1)S(1)}, bf16[1024,1024]{1,0:T(8,128)(2,1)}, u32[]{:S(2)}) copy-start(bf16[1024,1024]{1,0:T(8,128)(2,1)} %table_in.1) | copy-start | bytes 6291460
  26.7 22.2 %collective-permute-start = (bf16[256,256]{1,0:T(8,128)(2,1)}, bf16[256,256]{1,0:T(8,128)(2,1)S(1)}, u32[]{:S(2)}, u32[]{:S(2)}) collective-permute-start(bf16[256,256]{1,0:T(8,128)(2,1)} %get-tuple-element.15.payload_ref.near_ref), channel_id=1, source_target_pairs={{0,8},{1,9},{2,10},{3,11},{4,12},{5,13},{6,14},{7,15},{8,0},{9,1},... | collective-permute-start | bytes 393224 | tf_op jit(solution)/shard_map/ppermute | solution.py:306
  34.0 0.9 copy-start.7
  34.9 14.0 %copy-start.8 = (bf16[256,256]{1,0:T(8,128)(2,1)S(1)}, bf16[256,256]{1,0:T(8,128)(2,1)}, u32[]{:S(2)}) copy-start(bf16[256,256]{1,0:T(8,128)(2,1)} %get-tuple-element.15.payload_ref.near_ref) | copy-start | bytes 393220
  39.2 25.5 %all-to-all-start.1 = ((bf16[64,4,1024]{2,1,0:T(4,128)(2,1)}), bf16[64,4,1024]{2,1,0:T(4,128)(2,1)S(1)}, u32[]{:S(2)}, u32[]{:S(2)}) async-start(bf16[64,4,1024]{2,1,0:T(4,128)(2,1)} %shard_map.115), calls=%async_computation.1 | async-start | bytes 1048576 | tf_op jit(solution)/shard_map/all_to_all | solution.py:322
  48.9 8.8 %copy-start.9 = (bf16[2048,1024]{1,0:T(8,128)(2,1)S(1)}, bf16[2048,1024]{1,0:T(8,128)(2,1)}, u32[]{:S(2)}) copy-start(bf16[2048,1024]{1,0:T(8,128)(2,1)} %param.15) | copy-start | bytes 12582916
  48.9 15.8 %copy-start.1 = (bf16[1024,256]{1,0:T(8,128)(2,1)S(1)}, bf16[1024,256]{1,0:T(8,128)(2,1)}, u32[]{:S(2)}) copy-start(bf16[1024,256]{1,0:T(8,128)(2,1)} %second_ref.1) | copy-start | bytes 1572868
  48.9 15.7 %copy-start.3 = (bf16[128,256]{1,0:T(8,128)(2,1)S(1)}, bf16[128,256]{1,0:T(8,128)(2,1)}, u32[]{:S(2)}) copy-start(bf16[128,256]{1,0:T(8,128)(2,1)} %get-tuple-element.17.placing_ref) | copy-start | bytes 196612
  49.0 15.7 %copy-start.5 = (s32[128]{0:T(128)S(1)}, s32[128]{0:T(128)}, u32[]{:S(2)}) copy-start(s32[128]{0:T(128)} %param.12) | copy-start | bytes 1540
  49.0 20.7 %collective-permute-start.1 = (bf16[2,256,256]{2,1,0:T(8,128)(2,1)S(1)}, bf16[2,256,256]{2,1,0:T(8,128)(2,1)S(1)}, u32[]{:S(2)}, u32[]{:S(2)}) collective-permute-start(bf16[2,256,256]{2,1,0:T(8,128)(2,1)S(1)} %shard_map.117.refs_0_.units_ref), channel_id=1, source_target_pairs={{0,2},{1,3},{2,4},{3,5},{4,6},{5,7},{6,8},{7,9},{8,10},{9,11},{10,... | collective-permute-start | bytes 786440 | tf_op jit(solution)/shard_map/ppermute | solution.py:306
  51.5 18.2 %collective-permute-start.2 = (bf16[2,256,256]{2,1,0:T(8,128)(2,1)S(1)}, bf16[2,256,256]{2,1,0:T(8,128)(2,1)S(1)}, u32[]{:S(2)}, u32[]{:S(2)}) collective-permute-start(bf16[2,256,256]{2,1,0:T(8,128)(2,1)S(1)} %shard_map.117.refs_0_.units_ref), channel_id=1, source_target_pairs={{0,14},{1,15},{2,0},{3,1},{4,2},{5,3},{6,4},{7,5},{8,6},{9,7},{10,... | collective-permute-start | bytes 786440 | tf_op jit(solution)/shard_map/ppermute | solution.py:306
  55.7 13.9 %collective-permute-start.3 = (bf16[2,256,256]{2,1,0:T(8,128)(2,1)S(1)}, bf16[2,256,256]{2,1,0:T(8,128)(2,1)S(1)}, u32[]{:S(2)}, u32[]{:S(2)}) collective-permute-start(bf16[2,256,256]{2,1,0:T(8,128)(2,1)S(1)} %shard_map.117.refs_0_.units_ref), channel_id=1, source_target_pairs={{0,4},{1,13},{2,6},{3,15},{4,8},{5,1},{6,10},{7,3},{8,12},{9,5},{1... | collective-permute-start | bytes 786440 | tf_op jit(solution)/shard_map/ppermute | solution.py:306
  66.1 15.4 %all-to-all-start.2 = ((bf16[8,136,256]{2,1,0:T(8,128)(2,1)}), bf16[8,136,256]{2,1,0:T(8,128)(2,1)S(1)}, u32[]{:S(2)}, u32[]{:S(2)}) async-start(bf16[8,136,256]{2,1,0:T(8,128)(2,1)} %shard_map.116), calls=%async_computation.2 | async-start | bytes 1114112 | tf_op jit(solution)/shard_map/all_to_all | solution.py:334
  69.7 26.8 %copy-start.2 = (bf16[256,256]{1,0:T(8,128)(2,1)S(1)}, bf16[256,256]{1,0:T(8,128)(2,1)}, u32[]{:S(2)}) copy-start(bf16[256,256]{1,0:T(8,128)(2,1)} %users_ref.1) | copy-start | bytes 393220
  69.7 26.8 %copy-start.4 = (s32[256]{0:T(256)S(1)}, s32[256]{0:T(256)}, u32[]{:S(2)}) copy-start(s32[256]{0:T(256)} %param.13) | copy-start | bytes 3076
  81.5 10.7 %collective-permute-start.4 = (bf16[8,136,256]{2,1,0:T(8,128)(2,1)S(1)}, bf16[8,136,256]{2,1,0:T(8,128)(2,1)S(1)}, u32[]{:S(2)}, u32[]{:S(2)}) collective-permute-start(bf16[8,136,256]{2,1,0:T(8,128)(2,1)S(1)} %all-to-all-done.2.vecs_ref.mine_ref), channel_id=1, source_target_pairs={{0,1},{1,0},{2,3},{3,2},{4,5},{5,4},{6,7},{7,6},{8,9},{9,8},{10,11... | collective-permute-start | bytes 1671176 | tf_op jit(solution)/shard_map/ppermute | solution.py:346
  94.2 4.6 %collective-permute-start.5 = (f32[128,256]{1,0:T(8,128)S(1)}, f32[128,256]{1,0:T(8,128)S(1)}, u32[]{:S(2)}, u32[]{:S(2)}) collective-permute-start(f32[128,256]{1,0:T(8,128)S(1)} %get-tuple-element.24), channel_id=1, source_target_pairs={{0,1},{1,0},{2,3},{3,2},{4,5},{5,4},{6,7},{7,6},{8,9},{9,8},{10,11... | collective-permute-start | bytes 393224 | tf_op jit(solution)/shard_map/ppermute | solution.py:363

commit v6 on v5

--- a/solution.py
+++ b/solution.py
@@ -14,7 +14,7 @@
 far_memory = pl.BlockSpec(memory_space=pltpu.HBM)
 anywhere = pl.BlockSpec(memory_space=pl.ANY)
 f32, bf16 = jnp.float32, jnp.bfloat16
-extra = 8
+extra = 16
 
 
 def call(kernel, out_shape, flops, moved, exps=0, in_specs=None, scratch=(), room=16, out_specs=None):

time: 101 us -> 101 us (level)
  no operation moved by 1% of the time
where the time goes in v6:
time: 101 us
  starting transfers between devices  64.7 us (64%)
  waiting for transfers between devices  21.3 us (21%)
  Pallas kernels  12.4 us (12%)
    all_to_all x1, starting transfers between devices, shards(): lax.all_to_all(ids_sent.reshape(owners, 1, 128), 'shard', 0, 0, tiled=True)  24 us
    ppermute x4, starting transfers between devices, turn(): return lax.ppermute(array, 'blk', pairs)  15.9 us
    all_to_all x1, waiting for transfers between devices, shards(): lax.all_to_all(vecs, 'blk', 0, 0, axis_index_groups=[list(range(c, blocks...  12.3 us
    all_to_all x1, starting transfers between devices, shards(): received = lax.all_to_all(table_rows, 'shard', 0, 0, tiled=True)  9.65 us
    ppermute x1, starting transfers between devices, shards(): other = lax.ppermute(mine, 'blk', swap)  9.34 us
    pallas_call x4, Pallas kernels, step(): call(kernel, out_shape, 2 * pairs * width, moved, pairs, specs, scratch, 48)  7.08 us
    all_to_all x1, waiting for transfers between devices, shards(): received = lax.all_to_all(table_rows, 'shard', 0, 0, tiled=True)  6.24 us
    all_to_all x1, starting transfers between devices, shards(): lax.all_to_all(vecs, 'blk', 0, 0, axis_index_groups=[list(range(c, blocks...  3.55 us
  transfers between devices with their start and end apart: 9, of which 4 were waited for; matrix products, arithmetic and copies ran while one was open for 1% of the time, Pallas kernels for 7%

profile of v6, /device:TPU:1, one launch (start us, length us, event | category | flops | bytes accessed | tf_op | source)
XLA Modules:
  0.0 101.0 jit_solution(15198899747302523447)
XLA Ops:
  0.6 0.0 copy-start
  0.6 2.1 %shard_map.112 = (s32[64,128]{1,0:T(8,128)}, bf16[128,256]{1,0:T(8,128)(2,1)}, bf16[256,256]{1,0:T(8,128)(2,1)}) custom-call(s32[1,128]{1,0:T(1,128)} %bitcast.17, s32[1,128]{1,0:T(1,128)} %bitcast.18, bf16[256,256]{1,0:T(8,128)(2,1)} %users_ref.1), custom_call_target="tpu_custom_call" | custom-call | flops 8388608 | bytes 32768 | tf_op jit(solution)/shard_map/pallas_call | solution.py:278
  2.7 24.0 %all-to-all-start = ((s32[64,1,128]{2,1,0:T(1,128)}), s32[64,1,128]{2,1,0:T(1,128)S(1)}, u32[]{:S(2)}, u32[]{:S(2)}) async-start(s32[64,1,128]{2,1,0:T(1,128)} %bitcast.16), calls=%async_computation | async-start | bytes 65536 | tf_op jit(solution)/shard_map/all_to_all | solution.py:292
  26.7 0.0 copy-start.6
  26.7 7.2 %collective-permute-start = (bf16[256,256]{1,0:T(8,128)(2,1)}, bf16[256,256]{1,0:T(8,128)(2,1)S(1)}, u32[]{:S(2)}, u32[]{:S(2)}) collective-permute-start(bf16[256,256]{1,0:T(8,128)(2,1)} %get-tuple-element.15.payload_ref.near_ref), channel_id=1, source_target_pairs={{0,8},{1,9},{2,10},{3,11},{4,12},{5,13},{6,14},{7,15},{8,0},{9,1},... | collective-permute-start | bytes 393224 | tf_op jit(solution)/shard_map/ppermute | solution.py:306
  34.0 0.0 copy-start.7
  34.0 0.9 copy-done.7
  34.9 0.0 copy-done.6
  34.9 0.0 copy-start.8
  34.9 0.2 shard_map.114.table_ref
  35.1 2.5 %all-to-all-done = s32[64,1,128]{2,1,0:T(1,128)S(1)} async-done(((s32[64,1,128]{2,1,0:T(1,128)}), s32[64,1,128]{2,1,0:T(1,128)S(1)}, u32[]{:S(2)}, u32[]{:S(2)}) %all-to-all-start) | async-done | bytes 32800 | tf_op jit(solution)/shard_map/all_to_all | solution.py:292
  37.6 1.6 %shard_map.115 = bf16[64,4,1024]{2,1,0:T(4,128)(2,1)} custom-call(s32[64,128]{1,0:T(8,128)S(1)} %bitcast.12, bf16[1024,1024]{1,0:T(8,128)(2,1)S(1)} %shard_map.114.table_ref), custom_call_target="tpu_custom_call" | custom-call | flops 536870912 | bytes 2097152 | tf_op jit(solution)/shard_map/pallas_call | solution.py:308
  39.2 9.7 %all-to-all-start.1 = ((bf16[64,4,1024]{2,1,0:T(4,128)(2,1)}), bf16[64,4,1024]{2,1,0:T(4,128)(2,1)S(1)}, u32[]{:S(2)}, u32[]{:S(2)}) async-start(bf16[64,4,1024]{2,1,0:T(4,128)(2,1)} %shard_map.115), calls=%async_computation.1 | async-start | bytes 1048576 | tf_op jit(solution)/shard_map/all_to_all | solution.py:322
  48.9 0.0 copy-start.9
  48.9 0.0 collective-permute-done.far_ref
  48.9 0.0 copy-done.8
  48.9 0.0 copy-start.1
  48.9 0.0 copy-start.3
  49.0 0.0 copy-start.5
  49.0 2.5 %collective-permute-start.1 = (bf16[2,256,256]{2,1,0:T(8,128)(2,1)S(1)}, bf16[2,256,256]{2,1,0:T(8,128)(2,1)S(1)}, u32[]{:S(2)}, u32[]{:S(2)}) collective-permute-start(bf16[2,256,256]{2,1,0:T(8,128)(2,1)S(1)} %shard_map.117.refs_0_.units_ref), channel_id=1, source_target_pairs={{0,2},{1,3},{2,4},{3,5},{4,6},{5,7},{6,8},{7,9},{8,10},{9,11},{10,... | collective-permute-start | bytes 786440 | tf_op jit(solution)/shard_map/ppermute | solution.py:306
  51.5 4.3 %collective-permute-start.2 = (bf16[2,256,256]{2,1,0:T(8,128)(2,1)S(1)}, bf16[2,256,256]{2,1,0:T(8,128)(2,1)S(1)}, u32[]{:S(2)}, u32[]{:S(2)}) collective-permute-start(bf16[2,256,256]{2,1,0:T(8,128)(2,1)S(1)} %shard_map.117.refs_0_.units_ref), channel_id=1, source_target_pairs={{0,14},{1,15},{2,0},{3,1},{4,2},{5,3},{6,4},{7,5},{8,6},{9,7},{10,... | collective-permute-start | bytes 786440 | tf_op jit(solution)/shard_map/ppermute | solution.py:306
  55.7 1.9 %collective-permute-start.3 = (bf16[2,256,256]{2,1,0:T(8,128)(2,1)S(1)}, bf16[2,256,256]{2,1,0:T(8,128)(2,1)S(1)}, u32[]{:S(2)}, u32[]{:S(2)}) collective-permute-start(bf16[2,256,256]{2,1,0:T(8,128)(2,1)S(1)} %shard_map.117.refs_0_.units_ref), channel_id=1, source_target_pairs={{0,4},{1,13},{2,6},{3,15},{4,8},{5,1},{6,10},{7,3},{8,12},{9,5},{1... | collective-permute-start | bytes 786440 | tf_op jit(solution)/shard_map/ppermute | solution.py:306
  57.7 0.0 copy-done
  57.7 0.0 copy-done.9
  57.7 0.7 fusion.pre_ref
  58.4 6.2 %all-to-all-done.1.rows_ref = bf16[64,4,1024]{2,1,0:T(4,128)(2,1)S(1)} async-done(((bf16[64,4,1024]{2,1,0:T(4,128)(2,1)}), bf16[64,4,1024]{2,1,0:T(4,128)(2,1)S(1)}, u32[]{:S(2)}, u32[]{:S(2)}) %all-to-all-start.1) | async-done | bytes 524320 | tf_op jit(solution)/shard_map/all_to_all | solution.py:322
  64.7 0.0 copy-done.1
  64.7 0.0 copy-done.3
  64.7 0.0 copy-done.5
  64.7 1.4 %shard_map.116 = bf16[8,144,256]{2,1,0:T(8,128)(2,1)} custom-call(f32[128,1024]{1,0:T(8,128)S(1)} %fusion.pre_ref, bf16[128,256]{1,0:T(8,128)(2,1)S(1)} %copy-done.3, bf16[64,4,1024]{2,1,0:T(4,128)(2,1)S(1)} %all-to-all-done.1.rows_ref, bf16[1024,256]{1,0:T(8,128)(2,1)S(1)} %copy-done.1, s32[1,128]{1,0:T(1,128)S(1)} %bitcast.15), custom_call_target="tpu_custom_call" | custom-call | flops 67108864 | bytes 524288 | tf_op jit(solution)/shard_map/pallas_call | solution.py:325
  66.1 3.5 %all-to-all-start.2 = ((bf16[8,144,256]{2,1,0:T(8,128)(2,1)}), bf16[8,144,256]{2,1,0:T(8,128)(2,1)S(1)}, u32[]{:S(2)}, u32[]{:S(2)}) async-start(bf16[8,144,256]{2,1,0:T(8,128)(2,1)} %shard_map.116), calls=%async_computation.2 | async-start | bytes 1179648 | tf_op jit(solution)/shard_map/all_to_all | solution.py:334
  69.6 0.0 collective-permute-done.1.one_ref.refs_1_
  69.7 0.0 collective-permute-done.2.two_ref.refs_2_
  69.7 0.0 collective-permute-done.3.three_ref.refs_3_
  69.7 0.0 copy-start.2
  69.7 0.0 copy-start.4
  69.7 12.3 %all-to-all-done.2.vecs_ref.mine_ref = bf16[8,144,256]{2,1,0:T(8,128)(2,1)S(1)} async-done(((bf16[8,144,256]{2,1,0:T(8,128)(2,1)}), bf16[8,144,256]{2,1,0:T(8,128)(2,1)S(1)}, u32[]{:S(2)}, u32[]{:S(2)}) %all-to-all-start.2) | async-done | bytes 589856 | tf_op jit(solution)/shard_map/all_to_all | solution.py:334
  82.0 9.3 %collective-permute-start.4 = (bf16[8,144,256]{2,1,0:T(8,128)(2,1)S(1)}, bf16[8,144,256]{2,1,0:T(8,128)(2,1)S(1)}, u32[]{:S(2)}, u32[]{:S(2)}) collective-permute-start(bf16[8,144,256]{2,1,0:T(8,128)(2,1)S(1)} %all-to-all-done.2.vecs_ref.mine_ref), channel_id=1, source_target_pairs={{0,1},{1,0},{2,3},{3,2},{4,5},{5,4},{6,7},{7,6},{8,9},{9,8},{10,11... | collective-permute-start | bytes 1769480 | tf_op jit(solution)/shard_map/ppermute | solution.py:346
  91.3 1.4 %shard_map.119.first_ref = f32[8,256]{1,0:T(8,128)S(1)} custom-call(bf16[8,144,256]{2,1,0:T(8,128)(2,1)S(1)} %all-to-all-done.2.vecs_ref.mine_ref, f32[8,128]{1,0:T(8,128)S(1)} %shard_map.118.ready_ref, bf16[2,256,256]{2,1,0:T(8,128)(2,1)S(1)} %shard_map.117.refs_0_.units_ref, bf16[2,256,256]{2,1,0:T(8,128)(2,1)S(1)} %collective-permute-done.1.one_ref.refs_1_, ...), custom_call_target="tpu_custom_call" | custom-call | flops 1073741824 | bytes 2097152 | tf_op jit(solution)/shard_map/pallas_call | solution.py:352
  92.7 0.2 collective-permute-done.4.vecs_ref.other_ref
  92.9 2.0 %shard_map.120 = (f32[8,256]{1,0:T(8,128)S(1)}, f32[128,256]{1,0:T(8,128)S(1)}) custom-call(s32[1]{0:T(128)} %bitcast.place_ref, bf16[8,144,256]{2,1,0:T(8,128)(2,1)S(1)} %collective-permute-done.4.vecs_ref.other_ref, f32[8,256]{1,0:T(8,128)S(1)} %shard_map.119.first_ref, bf16[2,256,256]{2,1,0:T(8,128)(2,1)S(1)} %shard_map.117.refs_0_.units_ref, ...), custom_call_target="tpu_custom_call" | custom-call | flops 1073741824 | bytes 2097152 | tf_op jit(solution)/shard_map/pallas_call | solution.py:352
  94.9 2.3 %collective-permute-start.5 = (f32[128,256]{1,0:T(8,128)S(1)}, f32[128,256]{1,0:T(8,128)S(1)}, u32[]{:S(2)}, u32[]{:S(2)}) collective-permute-start(f32[128,256]{1,0:T(8,128)S(1)} %get-tuple-element.24), channel_id=1, source_target_pairs={{0,1},{1,0},{2,3},{3,2},{4,5},{5,4},{6,7},{7,6},{8,9},{9,8},{10,11... | collective-permute-start | bytes 393224 | tf_op jit(solution)/shard_map/ppermute | solution.py:363
  97.2 0.0 copy-done.2
  97.2 0.0 copy-done.4
  97.2 2.3 %shard_map.121 = (f32[1,256]{1,0:T(1,128)}, f32[256,256]{1,0:T(8,128)}) custom-call(s32[1]{0:T(128)} %bitcast.place_ref, bf16[8,144,256]{2,1,0:T(8,128)(2,1)S(1)} %all-to-all-done.2.vecs_ref.mine_ref, bf16[8,144,256]{2,1,0:T(8,128)(2,1)S(1)} %collective-permute-done.4.vecs_ref.other_ref, f32[8,256]{1,0:T(8,128)S(1)} %get-tuple-element.21.sums_ref, ...), custom_call_target="tpu_custom_call" | custom-call | flops 1073741824 | bytes 2097152 | tf_op jit(solution)/shard_map/pallas_call | solution.py:352
  99.5 0.0 collective-permute-done.5.taken_ref
  99.5 1.5 %shard_map.122 = f32[128,256]{1,0:T(8,128)} custom-call(s32[1]{0:T(128)} %bitcast.place_ref, bf16[8,144,256]{2,1,0:T(8,128)(2,1)S(1)} %all-to-all-done.2.vecs_ref.mine_ref, f32[8,256]{1,0:T(8,128)S(1)} %get-tuple-element.21.sums_ref, s32[1,256]{1,0:T(1,128)S(1)} %bitcast.14, f32[128,256]{1,0:T(8,128)S(1)} %collective-permute-done.5.taken_ref, ...), custom_call_target="tpu_custom_call" | custom-call | flops 134217728 | bytes 2097152 | tf_op jit(solution)/shard_map/pallas_call | solution.py:352
  (3 shorter events, 0.0 us)
Async XLA Ops:
  0.6 57.0 %copy-start = (bf16[128,2048]{1,0:T(8,128)(2,1)S(1)}, bf16[128,2048]{1,0:T(8,128)(2,1)}, u32[]{:S(2)}) copy-start(bf16[128,2048]{1,0:T(8,128)(2,1)} %param.9) | copy-start | bytes 1572868
  2.7 34.8 %all-to-all-start = ((s32[64,1,128]{2,1,0:T(1,128)}), s32[64,1,128]{2,1,0:T(1,128)S(1)}, u32[]{:S(2)}, u32[]{:S(2)}) async-start(s32[64,1,128]{2,1,0:T(1,128)} %bitcast.16), calls=%async_computation | async-start | bytes 65536 | tf_op jit(solution)/shard_map/all_to_all | solution.py:292
  26.7 8.2 %copy-start.6 = (bf16[1024,1024]{1,0:T(8,128)(2,1)S(1)}, bf16[1024,1024]{1,0:T(8,128)(2,1)}, u32[]{:S(2)}) copy-start(bf16[1024,1024]{1,0:T(8,128)(2,1)} %table_in.1) | copy-start | bytes 6291460
  26.7 22.2 %collective-permute-start = (bf16[256,256]{1,0:T(8,128)(2,1)}, bf16[256,256]{1,0:T(8,128)(2,1)S(1)}, u32[]{:S(2)}, u32[]{:S(2)}) collective-permute-start(bf16[256,256]{1,0:T(8,128)(2,1)} %get-tuple-element.15.payload_ref.near_ref), channel_id=1, source_target_pairs={{0,8},{1,9},{2,10},{3,11},{4,12},{5,13},{6,14},{7,15},{8,0},{9,1},... | collective-permute-start | bytes 393224 | tf_op jit(solution)/shard_map/ppermute | solution.py:306
  34.0 0.9 copy-start.7
  34.9 14.0 %copy-start.8 = (bf16[256,256]{1,0:T(8,128)(2,1)S(1)}, bf16[256,256]{1,0:T(8,128)(2,1)}, u32[]{:S(2)}) copy-start(bf16[256,256]{1,0:T(8,128)(2,1)} %get-tuple-element.15.payload_ref.near_ref) | copy-start | bytes 393220
  39.2 25.5 %all-to-all-start.1 = ((bf16[64,4,1024]{2,1,0:T(4,128)(2,1)}), bf16[64,4,1024]{2,1,0:T(4,128)(2,1)S(1)}, u32[]{:S(2)}, u32[]{:S(2)}) async-start(bf16[64,4,1024]{2,1,0:T(4,128)(2,1)} %shard_map.115), calls=%async_computation.1 | async-start | bytes 1048576 | tf_op jit(solution)/shard_map/all_to_all | solution.py:322
  48.9 8.8 %copy-start.9 = (bf16[2048,1024]{1,0:T(8,128)(2,1)S(1)}, bf16[2048,1024]{1,0:T(8,128)(2,1)}, u32[]{:S(2)}) copy-start(bf16[2048,1024]{1,0:T(8,128)(2,1)} %param.15) | copy-start | bytes 12582916
  48.9 15.8 %copy-start.1 = (bf16[1024,256]{1,0:T(8,128)(2,1)S(1)}, bf16[1024,256]{1,0:T(8,128)(2,1)}, u32[]{:S(2)}) copy-start(bf16[1024,256]{1,0:T(8,128)(2,1)} %second_ref.1) | copy-start | bytes 1572868
  48.9 15.7 %copy-start.3 = (bf16[128,256]{1,0:T(8,128)(2,1)S(1)}, bf16[128,256]{1,0:T(8,128)(2,1)}, u32[]{:S(2)}) copy-start(bf16[128,256]{1,0:T(8,128)(2,1)} %get-tuple-element.17.placing_ref) | copy-start | bytes 196612
  49.0 15.7 %copy-start.5 = (s32[128]{0:T(128)S(1)}, s32[128]{0:T(128)}, u32[]{:S(2)}) copy-start(s32[128]{0:T(128)} %param.12) | copy-start | bytes 1540
  49.0 20.7 %collective-permute-start.1 = (bf16[2,256,256]{2,1,0:T(8,128)(2,1)S(1)}, bf16[2,256,256]{2,1,0:T(8,128)(2,1)S(1)}, u32[]{:S(2)}, u32[]{:S(2)}) collective-permute-start(bf16[2,256,256]{2,1,0:T(8,128)(2,1)S(1)} %shard_map.117.refs_0_.units_ref), channel_id=1, source_target_pairs={{0,2},{1,3},{2,4},{3,5},{4,6},{5,7},{6,8},{7,9},{8,10},{9,11},{10,... | collective-permute-start | bytes 786440 | tf_op jit(solution)/shard_map/ppermute | solution.py:306
  51.5 18.2 %collective-permute-start.2 = (bf16[2,256,256]{2,1,0:T(8,128)(2,1)S(1)}, bf16[2,256,256]{2,1,0:T(8,128)(2,1)S(1)}, u32[]{:S(2)}, u32[]{:S(2)}) collective-permute-start(bf16[2,256,256]{2,1,0:T(8,128)(2,1)S(1)} %shard_map.117.refs_0_.units_ref), channel_id=1, source_target_pairs={{0,14},{1,15},{2,0},{3,1},{4,2},{5,3},{6,4},{7,5},{8,6},{9,7},{10,... | collective-permute-start | bytes 786440 | tf_op jit(solution)/shard_map/ppermute | solution.py:306
  55.7 13.9 %collective-permute-start.3 = (bf16[2,256,256]{2,1,0:T(8,128)(2,1)S(1)}, bf16[2,256,256]{2,1,0:T(8,128)(2,1)S(1)}, u32[]{:S(2)}, u32[]{:S(2)}) collective-permute-start(bf16[2,256,256]{2,1,0:T(8,128)(2,1)S(1)} %shard_map.117.refs_0_.units_ref), channel_id=1, source_target_pairs={{0,4},{1,13},{2,6},{3,15},{4,8},{5,1},{6,10},{7,3},{8,12},{9,5},{1... | collective-permute-start | bytes 786440 | tf_op jit(solution)/shard_map/ppermute | solution.py:306
  66.1 15.9 %all-to-all-start.2 = ((bf16[8,144,256]{2,1,0:T(8,128)(2,1)}), bf16[8,144,256]{2,1,0:T(8,128)(2,1)S(1)}, u32[]{:S(2)}, u32[]{:S(2)}) async-start(bf16[8,144,256]{2,1,0:T(8,128)(2,1)} %shard_map.116), calls=%async_computation.2 | async-start | bytes 1179648 | tf_op jit(solution)/shard_map/all_to_all | solution.py:334
  69.7 27.5 %copy-start.2 = (bf16[256,256]{1,0:T(8,128)(2,1)S(1)}, bf16[256,256]{1,0:T(8,128)(2,1)}, u32[]{:S(2)}) copy-start(bf16[256,256]{1,0:T(8,128)(2,1)} %users_ref.1) | copy-start | bytes 393220
  69.7 27.5 %copy-start.4 = (s32[256]{0:T(256)S(1)}, s32[256]{0:T(256)}, u32[]{:S(2)}) copy-start(s32[256]{0:T(256)} %param.13) | copy-start | bytes 3076
  82.0 11.0 %collective-permute-start.4 = (bf16[8,144,256]{2,1,0:T(8,128)(2,1)S(1)}, bf16[8,144,256]{2,1,0:T(8,128)(2,1)S(1)}, u32[]{:S(2)}, u32[]{:S(2)}) collective-permute-start(bf16[8,144,256]{2,1,0:T(8,128)(2,1)S(1)} %all-to-all-done.2.vecs_ref.mine_ref), channel_id=1, source_target_pairs={{0,1},{1,0},{2,3},{3,2},{4,5},{5,4},{6,7},{7,6},{8,9},{9,8},{10,11... | collective-permute-start | bytes 1769480 | tf_op jit(solution)/shard_map/ppermute | solution.py:346
  94.9 4.6 %collective-permute-start.5 = (f32[128,256]{1,0:T(8,128)S(1)}, f32[128,256]{1,0:T(8,128)S(1)}, u32[]{:S(2)}, u32[]{:S(2)}) collective-permute-start(f32[128,256]{1,0:T(8,128)S(1)} %get-tuple-element.24), channel_id=1, source_target_pairs={{0,1},{1,0},{2,3},{3,2},{4,5},{5,4},{6,7},{7,6},{8,9},{9,8},{10,11... | collective-permute-start | bytes 393224 | tf_op jit(solution)/shard_map/ppermute | solution.py:363
